TPU v7x, 32 devices: a whole 2x2x4 slice. The times are simulated.
32 devices in a mesh: param: 4 (over y, x), space: 2 (over core), term: 4 (over z).
Axes of the slice: x: 2, y: 2, z: 4, core: 2. Of those that a mesh axis runs over, the one named last changes fastest.
Arguments:
- fields: float32 [16, 2, 8, 128, 128], P('param', None, None, 'space'), may hold values from -4 to 4
- library: int32 [168, 4], P('term'), may hold values from 0 to 6, as said below
- centers_x: int32 [16], replicated, may hold values from 0 to 127
- centers_y: int32 [16], replicated, may hold values from 0 to 127
- centers_t: int32 [4], replicated, may hold values from 0 to 7
- groups: int32 [168], replicated, may hold values from 0 to 23
Outputs:
- coefficients: float32 [16, 2, 168], P(('param', 'term'))
- misfit: float32 [16, 2, 168], P(('param', 'term'))
Inputs may be any that keep to these rules, and one draw needn't show every extreme that they name: `library`: each row (a, b, dx, dy) gives powers a and b of 0 to 6 and derivative orders dx and dy of 0 to 2; rows are distinct, and a = b = 0 only with dx = dy = 0.
All inputs are finite; a program needn't handle non-finite values.
Results may differ from a plain program's by a relative error of at most 0.00011.
Values sent between devices are 32-bit elements; how exact they have to be, the bound alone decides.
No kernel may reach another device: no remote copies, remote signals or barrier semaphores. Data moves between devices by JAX's collectives and lax.ppermute only.
A program may use at most 64 MiB of HBM per device.

v0:
```python
import jax
import jax.numpy as jnp
from jax import lax
from jax.sharding import PartitionSpec as P

NX = 128
NY = 128
NT = 8
POWERS = 7
TERMS = 168
TESTS = 1024
RX = 16
RT = 4
GROUPS = 24


highest = lax.Precision.HIGHEST


def space_table(centers, first_row, row_count, extent):
    cell_index = first_row + jnp.arange(row_count, dtype=jnp.int32)
    offset = (cell_index[None, :] - centers[:, None] + extent // 2) % extent - extent // 2
    scaled = offset.astype(jnp.float32) / RX
    bump_base = 1.0 - scaled * scaled
    inside = jnp.abs(scaled) < 1.0
    cube = bump_base * bump_base * bump_base
    bump_value = jnp.where(inside, cube * bump_base, 0.0)
    bump_first = jnp.where(inside, 8.0 * scaled * cube / RX, 0.0)
    bump_second = jnp.where(
        inside, -8.0 * (cube - 6.0 * scaled * scaled * bump_base * bump_base) / (RX * RX), 0.0
    )
    return jnp.stack([bump_value, bump_first, bump_second])


def time_table(centers):
    step_index = jnp.arange(NT, dtype=jnp.int32)
    scaled = (step_index[None, :] - centers[:, None]).astype(jnp.float32) / RT
    bump_base = 1.0 - scaled * scaled
    inside = jnp.abs(scaled) < 1.0
    time_bump = jnp.where(inside, bump_base * bump_base, 0.0)
    time_slope = jnp.where(inside, 4.0 * scaled * bump_base / RT, 0.0)
    return (time_bump, time_slope)


def normalize(gram_matrix):
    diagonal = jnp.diagonal(gram_matrix, axis1=1, axis2=2)
    row_scale = jnp.sqrt(diagonal / TESTS + 1e-06)
    term_scale = row_scale[:, :TERMS]
    correlation = gram_matrix[:, :TERMS, :TERMS] / (
        TESTS * term_scale[:, :, None] * term_scale[:, None, :]
    )
    right_side = gram_matrix[:, TERMS:, :TERMS] / (
        TESTS * term_scale[:, None, :] * row_scale[:, TERMS:, None]
    )
    frobenius = jnp.sqrt(jnp.sum(correlation * correlation, axis=(1, 2)))
    return (correlation, right_side, frobenius)


def group_squares(values, onehot):
    return jnp.dot(jnp.sum(values * values, axis=(0, 1)), onehot, precision=highest)


def shrink(values, totals, onehot):
    threshold = 0.7 * jnp.sqrt(jnp.mean(totals))
    per_term = jnp.dot(onehot, totals, precision=highest)
    factor = jnp.maximum(0.0, 1.0 - threshold / jnp.sqrt(per_term + 1e-12))
    return values * factor


def correlate(correlation, values):
    return jnp.einsum("pij,psj->psi", correlation, values, precision=highest)


def body(fields, library, centers_x, centers_y, centers_t, groups):
    pgroup = fields.shape[0]
    tile_rows = fields.shape[3]
    space_count = lax.axis_size("space")
    term_count = lax.axis_size("term")
    local_terms = library.shape[0]
    row_count = local_terms + 2
    half_tests = TESTS // space_count
    y_table = space_table(centers_y, 0, NY, NY)
    time_bump, time_slope = time_table(centers_t)
    x_table = space_table(centers_x, lax.axis_index("space") * tile_rows, tile_rows, NX)
    share_rows = tile_rows // term_count
    share_start = lax.axis_index("term") * share_rows
    x_share = lax.dynamic_slice_in_dim(x_table[0], share_start, share_rows, 1)
    power_a = library[:, 0]
    power_b = library[:, 1]
    orders = jnp.arange(3, dtype=jnp.int32)
    pick_x = (library[:, 2][:, None] == orders[None, :]).astype(jnp.float32)
    pick_y = (library[:, 3][:, None] == orders[None, :]).astype(jnp.float32)
    x_pick = jnp.einsum("jd,dlx->jlx", pick_x, x_table, precision=highest)
    y_pick = jnp.einsum("jd,dky->jky", pick_y, y_table, precision=highest)

    def tile_integrals(field_pair):
        species_u = field_pair[0]
        species_v = field_pair[1]
        power_u = jnp.ones((local_terms,) + species_u.shape, jnp.float32)
        power_v = jnp.ones((local_terms,) + species_v.shape, jnp.float32)
        for degree in range(1, POWERS):
            power_u = power_u * jnp.where(
                power_a[:, None, None, None] >= degree, species_u[None], 1.0
            )
            power_v = power_v * jnp.where(
                power_b[:, None, None, None] >= degree, species_v[None], 1.0
            )
        monomial = power_u * power_v
        across_y = jnp.einsum("jtxy,jky->jtxk", monomial, y_pick, precision=highest)
        across_t = jnp.einsum("jtxk,rt->jrxk", across_y, time_bump, precision=highest)
        features = jnp.einsum("jrxk,jlx->jrkl", across_t, x_pick, precision=highest).reshape(
            local_terms, TESTS
        )
        share = lax.dynamic_slice_in_dim(field_pair, share_start, share_rows, 2)
        target_y = jnp.einsum("stxy,ky->stxk", share, y_table[0], precision=highest)
        targets = jnp.einsum(
            "stxk,rt,lx->srkl", target_y, time_slope, x_share, precision=highest
        ).reshape(2, TESTS)
        joined = jnp.concatenate([features, targets], axis=0).reshape(
            row_count, space_count, half_tests
        )
        return jnp.swapaxes(joined, 0, 1)

    def fill_param(index, buffer):
        field_pair = lax.dynamic_index_in_dim(fields, index, 0, keepdims=False)
        return lax.dynamic_update_slice_in_dim(
            buffer, tile_integrals(field_pair)[:, None], index, 1
        )

    buffer = jnp.zeros((space_count, pgroup, row_count, half_tests), jnp.float32)
    buffer = lax.fori_loop(0, pgroup, fill_param, buffer)
    received = lax.all_to_all(
        buffer.reshape(space_count * pgroup, row_count, half_tests),
        ("space", "term"),
        split_axis=0,
        concat_axis=1,
        tiled=True,
    )
    blocks = jnp.sum(received.reshape(space_count, term_count, row_count, half_tests), axis=0)
    features_half = blocks[:, :local_terms].reshape(term_count * local_terms, half_tests)
    targets_half = jnp.sum(blocks[:, local_terms:], axis=0)
    half_rows = jnp.concatenate([features_half, targets_half], axis=0)
    whole_rows = lax.all_gather(half_rows, "space", axis=1, tiled=True)
    gram_matrix = jnp.dot(whole_rows, whole_rows.T, precision=highest)[None]
    correlation, right_side, frobenius = normalize(gram_matrix)
    onehot = (groups[:, None] == jnp.arange(GROUPS, dtype=jnp.int32)[None, :]).astype(jnp.float32)
    largest = lax.pmax(jnp.max(frobenius), ("param", "term"))
    step_size = 1.0 / largest
    first_guess = step_size * right_side
    first_sq = lax.psum(group_squares(first_guess, onehot), ("param", "term"))
    first = shrink(first_guess, first_sq, onehot)
    second_guess = first - step_size * (correlate(correlation, first) - right_side)
    second_sq = lax.psum(group_squares(second_guess, onehot), ("param", "term"))
    second = shrink(second_guess, second_sq, onehot)
    coefficients = second / step_size
    misfit = right_side - correlate(correlation, second)
    return (coefficients, misfit)


def solution(mesh):
    return jax.shard_map(
        body,
        mesh=mesh,
        in_specs=(P("param", None, None, "space", None), P("term", None), P(), P(), P(), P()),
        out_specs=(P(("param", "term"), None, None), P(("param", "term"), None, None)),
        check_vma=False,
    )
```

profile of v0, /device:TPU:0, one launch (start us, length us, event | category | flops | bytes accessed | tf_op | source)
XLA Modules:
  0.0 323.1 jit_solution(14601144981457283603)
XLA Ops:
  0.6 0.8 multiply_select_fusion.2
  1.5 0.7 fusion.141
  2.2 0.8 slice_bitcast_fusion.1
  3.0 0.4 fusion.130
  3.6 0.8 multiply_select_fusion.5
  4.4 0.4 fusion.124
  4.9 164.0 %while.18 = (s32[]{:T(128)}, f32[2,4,44,512]{3,0,2,1:T(2,128)S(1)}, s32[42,1]{0,1:T(1,128)S(1)}, f32[4,2,8,64,128]{4,3,2,1,0:T(8,128)}, s32[42,1]{0,1:T(1,128)S(...) while((s32[]{:T(128)}, f32[2,4,44,512]{3,0,2,1:T(2,128)S(1)}, ...), condition=%wide.region_1.2_spmd.clone.clone, body=%wide.region_0.1_spmd.clone.clone.sunk | while | flops 648311936 | bytes 7924693 | solution.py:131
  5.0 1.1 dynamic-slice_bitcast_fusion.6
  6.1 32.0 %fusion.203 = f32[42,8,64,16]{2,3,1,0:T(8,128)S(1)} fusion(f32[8,64,128]{2,1,0:T(8,128)S(1)} %get-tuple-element.566, f32[8,64,128]{2,1,0:T(8,128)S(1)} %get-tuple-element.567, pred[42]{0:T(512)(128)(4,1)S(1)} %get-tuple-element.568, pred[42]{0:T(512)(128)(4,1)S(1)} %get-tuple-element.569, pred[42]{0:T(512)(128)(4,1)S(1)} %get-tuple-element.570, ...), kind=kOutput, calls=%fused_computation.4.clone.1 | convolution fusion | flops 591790080 | bytes 2245112 | tf_op jit(solution)/shard_map/while/body/eval_jaxpr/jtxy,jky->jtxk/dot_general | solution.py:109
  38.1 3.1 fusion.204
  41.3 1.3 fusion.205
  42.6 0.9 copy.65
  43.8 1.0 dynamic-slice_bitcast_fusion.5
  44.7 0.3 fusion.202
  45.9 1.1 dynamic-slice_bitcast_fusion.6
  47.0 32.0 %fusion.203 = f32[42,8,64,16]{2,3,1,0:T(8,128)S(1)} fusion(f32[8,64,128]{2,1,0:T(8,128)S(1)} %get-tuple-element.566, f32[8,64,128]{2,1,0:T(8,128)S(1)} %get-tuple-element.567, pred[42]{0:T(512)(128)(4,1)S(1)} %get-tuple-element.568, pred[42]{0:T(512)(128)(4,1)S(1)} %get-tuple-element.569, pred[42]{0:T(512)(128)(4,1)S(1)} %get-tuple-element.570, ...), kind=kOutput, calls=%fused_computation.4.clone.1 | convolution fusion | flops 591790080 | bytes 2245112 | tf_op jit(solution)/shard_map/while/body/eval_jaxpr/jtxy,jky->jtxk/dot_general | solution.py:109
  79.1 3.1 fusion.204
  82.2 1.3 fusion.205
  83.6 0.9 copy.65
  84.7 1.0 dynamic-slice_bitcast_fusion.5
  85.7 0.3 fusion.202
  86.9 1.1 dynamic-slice_bitcast_fusion.6
  88.0 32.0 %fusion.203 = f32[42,8,64,16]{2,3,1,0:T(8,128)S(1)} fusion(f32[8,64,128]{2,1,0:T(8,128)S(1)} %get-tuple-element.566, f32[8,64,128]{2,1,0:T(8,128)S(1)} %get-tuple-element.567, pred[42]{0:T(512)(128)(4,1)S(1)} %get-tuple-element.568, pred[42]{0:T(512)(128)(4,1)S(1)} %get-tuple-element.569, pred[42]{0:T(512)(128)(4,1)S(1)} %get-tuple-element.570, ...), kind=kOutput, calls=%fused_computation.4.clone.1 | convolution fusion | flops 591790080 | bytes 2245112 | tf_op jit(solution)/shard_map/while/body/eval_jaxpr/jtxy,jky->jtxk/dot_general | solution.py:109
  120.0 3.1 fusion.204
  123.2 1.3 fusion.205
  124.5 0.9 copy.65
  125.7 1.0 dynamic-slice_bitcast_fusion.5
  126.7 0.3 fusion.202
  127.9 1.1 dynamic-slice_bitcast_fusion.6
  129.0 32.0 %fusion.203 = f32[42,8,64,16]{2,3,1,0:T(8,128)S(1)} fusion(f32[8,64,128]{2,1,0:T(8,128)S(1)} %get-tuple-element.566, f32[8,64,128]{2,1,0:T(8,128)S(1)} %get-tuple-element.567, pred[42]{0:T(512)(128)(4,1)S(1)} %get-tuple-element.568, pred[42]{0:T(512)(128)(4,1)S(1)} %get-tuple-element.569, pred[42]{0:T(512)(128)(4,1)S(1)} %get-tuple-element.570, ...), kind=kOutput, calls=%fused_computation.4.clone.1 | convolution fusion | flops 591790080 | bytes 2245112 | tf_op jit(solution)/shard_map/while/body/eval_jaxpr/jtxy,jky->jtxk/dot_general | solution.py:109
  161.0 3.1 fusion.204
  164.2 1.3 fusion.205
  165.5 0.9 copy.65
  166.6 1.0 dynamic-slice_bitcast_fusion.5
  169.0 1.0 copy.37
  170.0 6.2 %all-to-all-start = ((f32[8,44,512]{2,1,0:T(8,128)}), f32[8,44,512]{2,1,0:T(8,128)S(1)}, u32[]{:S(2)}, u32[]{:S(2)}) async-start(f32[8,44,512]{2,1,0:T(8,128)} %bitcast.4), calls=%async_computation | async-start | bytes 1572864 | tf_op jit(solution)/shard_map/all_to_all | solution.py:132
  176.2 20.5 %all-to-all-done = f32[8,44,512]{2,1,0:T(8,128)S(1)} async-done(((f32[8,44,512]{2,1,0:T(8,128)}), f32[8,44,512]{2,1,0:T(8,128)S(1)}, u32[]{:S(2)}, u32[]{:S(2)}) %all-to-all-start) | async-done | bytes 720928 | tf_op jit(solution)/shard_map/all_to_all | solution.py:132
  196.9 2.3 all_gather.3
  199.3 0.7 fusion.167
  200.0 2.8 gather_fusion
  202.9 0.7 multiply_reduce_fusion
  204.3 37.2 %pmax.7 = f32[]{:T(128)} all-reduce(f32[]{:T(128)S(6)} %sqrt.28), channel_id=1, replica_groups=mesh['param'=4,'space'=2,'term'=4] {'param','term'}, use_global_device_ids=true, to_apply=%region_5.6 | all-reduce | flops 1 | bytes 8 | tf_op jit(solution)/shard_map/pmax | solution.py:147
  242.6 38.8 %psum.14 = f32[24]{0:T(128)S(1)} all-reduce(f32[24]{0:T(128)S(1)} %convolution_bitcast_fusion.5), channel_id=1, replica_groups=mesh['param'=4,'space'=2,'term'=4] {'param','term'}, use_global_device_ids=true, to_apply=%region_7.8 | all-reduce | flops 24 | bytes 192 | tf_op jit(solution)/shard_map/psum | solution.py:150
  281.3 0.6 reduce_sum.67
  283.4 36.7 %psum.15 = f32[24]{0:T(128)S(1)} all-reduce(f32[24]{0:T(128)S(1)} %convolution_bitcast_fusion.4), channel_id=1, replica_groups=mesh['param'=4,'space'=2,'term'=4] {'param','term'}, use_global_device_ids=true, to_apply=%region_10.11 | all-reduce | flops 24 | bytes 192 | tf_op jit(solution)/shard_map/psum | solution.py:153
  320.1 0.6 reduce_sum.69
  321.7 0.8 fusion.112
  322.6 0.6 multiply_divide_fusion
  (68 shorter events, 6.2 us)
Async XLA Ops:
  6.0 32.0 %copy-start = (s32[4]{0:T(128)S(1)}, s32[4]{0:T(128)}, u32[]{:S(2)}) copy-start(s32[4]{0:T(128)} %get-tuple-element.619) | copy-start | bytes 52 | tf_op jit(solution)/shard_map/while
  41.2 3.5 %copy-start.1 = (s32[16]{0:T(128)S(1)}, s32[16]{0:T(128)}, u32[]{:S(2)}) copy-start(s32[16]{0:T(128)} %get-tuple-element.620) | copy-start | bytes 196 | tf_op jit(solution)/shard_map/while
  47.0 32.0 %copy-start = (s32[4]{0:T(128)S(1)}, s32[4]{0:T(128)}, u32[]{:S(2)}) copy-start(s32[4]{0:T(128)} %get-tuple-element.619) | copy-start | bytes 52 | tf_op jit(solution)/shard_map/while
  82.2 3.5 %copy-start.1 = (s32[16]{0:T(128)S(1)}, s32[16]{0:T(128)}, u32[]{:S(2)}) copy-start(s32[16]{0:T(128)} %get-tuple-element.620) | copy-start | bytes 196 | tf_op jit(solution)/shard_map/while
  88.0 32.0 %copy-start = (s32[4]{0:T(128)S(1)}, s32[4]{0:T(128)}, u32[]{:S(2)}) copy-start(s32[4]{0:T(128)} %get-tuple-element.619) | copy-start | bytes 52 | tf_op jit(solution)/shard_map/while
  123.2 3.5 %copy-start.1 = (s32[16]{0:T(128)S(1)}, s32[16]{0:T(128)}, u32[]{:S(2)}) copy-start(s32[16]{0:T(128)} %get-tuple-element.620) | copy-start | bytes 196 | tf_op jit(solution)/shard_map/while
  128.9 32.0 %copy-start = (s32[4]{0:T(128)S(1)}, s32[4]{0:T(128)}, u32[]{:S(2)}) copy-start(s32[4]{0:T(128)} %get-tuple-element.619) | copy-start | bytes 52 | tf_op jit(solution)/shard_map/while
  164.1 3.5 %copy-start.1 = (s32[16]{0:T(128)S(1)}, s32[16]{0:T(128)}, u32[]{:S(2)}) copy-start(s32[16]{0:T(128)} %get-tuple-element.620) | copy-start | bytes 196 | tf_op jit(solution)/shard_map/while
  170.0 26.7 %all-to-all-start = ((f32[8,44,512]{2,1,0:T(8,128)}), f32[8,44,512]{2,1,0:T(8,128)S(1)}, u32[]{:S(2)}, u32[]{:S(2)}) async-start(f32[8,44,512]{2,1,0:T(8,128)} %bitcast.4), calls=%async_computation | async-start | bytes 1572864 | tf_op jit(solution)/shard_map/all_to_all | solution.py:132
  196.8 45.5 %copy-start.2 = (s32[168]{0:T(256)S(1)}, s32[168]{0:T(256)}, u32[]{:S(2)}) copy-start(s32[168]{0:T(256)} %param.13) | copy-start | bytes 2020
where the time goes:
time: 324 us; the launch traced here: 323 us
  matrix products  153 us (47%)
  blocking collectives  115 us (35%)
  waiting for transfers between devices  20.5 us (6%)
  local copies, waits for them, and re-layouts  18.2 us (6%)
  starting transfers between devices  6.23 us (2%)
  other arithmetic  5.62 us (2%)
  between operations  3.73 us (1%)
    dot_general x4, matrix products, tile_integrals(): across_y = jnp.einsum('jtxy,jky->jtxk', monomial, y_pick, precision=highest)  128 us
    psum x1, blocking collectives, body(): first_sq = lax.psum(group_squares(first_guess, onehot), ('param', 'term'))  38.8 us
    pmax x1, blocking collectives, body(): largest = lax.pmax(jnp.max(frobenius), ('param', 'term'))  37.2 us
    psum x1, blocking collectives, body(): second_sq = lax.psum(group_squares(second_guess, onehot), ('param', 'term'))  36.7 us
    all_to_all x1, waiting for transfers between devices, body(): lax.all_to_all(buffer.reshape(space_count * pgroup, row_count, half_tests...  20.5 us
    dot_general x4, matrix products, tile_integrals(): jnp.einsum('jtxk,rt->jrxk', across_y, time_bump, precision=highest)  12.6 us
  transfers between devices with their start and end apart: 1, of which 1 were waited for; matrix products, arithmetic and copies ran while one was open for 0% of the time, Pallas kernels for 0%

commit v1 on v0

v1 whole, which is shorter than its diff:
```python
import functools

import jax
import jax.numpy as jnp
from jax import lax
from jax.experimental import pallas as pl
from jax.experimental.pallas import tpu as pltpu
from jax.sharding import PartitionSpec as P

NX = 128
NY = 128
NT = 8
POWERS = 7
TERMS = 168
TESTS = 1024
KX = 16
KY = 16
KT = 4
RX = 16
RT = 4
GROUPS = 24
ROWS = 3 * KY
LANES = 4 * KT * KX
VMEM_LIMIT = 40 * 2**20

f32, bf16 = jnp.float32, jnp.bfloat16
NT_DIMS = ((1,), (1,))
NN_DIMS = ((1,), (0,))


def split(x):
    high = x.astype(bf16)
    return high, (x - high.astype(f32)).astype(bf16)


def dot(a, b, dims):
    return lax.dot_general(a, b, (dims, ((), ())), preferred_element_type=f32)


def dot3(a, b, dims):
    ah, al = split(a)
    bh, bl = split(b)
    return dot(ah, bh, dims) + (dot(ah, bl, dims) + dot(al, bh, dims))


def space_rows(offset):
    scaled = offset.astype(f32) * (1.0 / RX)
    base = 1.0 - scaled * scaled
    inside = jnp.abs(scaled) < 1.0
    cube = base * base * base
    value = jnp.where(inside, cube * base, 0.0)
    first = jnp.where(inside, 8.0 * scaled * cube * (1.0 / RX), 0.0)
    second = jnp.where(
        inside, -8.0 * (cube - 6.0 * scaled * scaled * base * base) * (1.0 / (RX * RX)), 0.0
    )
    return value, first, second


def integrals_kernel(
    rows, where, cx, cy, ct, fields, out, pair, power_u, powers_v, y_split, tx_split, high, low, sem
):
    cells = NT * rows
    copy = pltpu.make_async_copy(fields.at[where[0]], pair, sem)
    copy.start()
    row = lax.broadcasted_iota(jnp.int32, (KY, NY), 0)
    lane = lax.broadcasted_iota(jnp.int32, (KY, NY), 1)
    center = jnp.zeros((KY, NY), jnp.int32)
    for k in range(KY):
        center = jnp.where(row == k, cy[k], center)
    offset = ((lane - center + NY // 2) & (NY - 1)) - NY // 2
    for i, part in enumerate(split(jnp.concatenate(space_rows(offset), axis=0))):
        y_split[pl.ds(i * ROWS, ROWS), :] = jnp.concatenate([part, part], axis=1)
    lane = lax.broadcasted_iota(jnp.int32, (1, LANES), 1)
    slot, kt, kx = lane >> 6, (lane >> 4) & 3, lane & 15
    center_x = jnp.zeros((1, LANES), jnp.int32)
    center_t = jnp.zeros((1, LANES), jnp.int32)
    for k in range(KX):
        center_x = jnp.where(kx == k, cx[k], center_x)
    for k in range(KT):
        center_t = jnp.where(kt == k, ct[k], center_t)
    row = lax.broadcasted_iota(jnp.int32, (rows, LANES), 0) + where[1]
    offset = ((row - center_x + NX // 2) & (NX - 1)) - NX // 2
    value, first, second = space_rows(offset)
    x_table = jnp.where(slot == 1, first, jnp.where(slot == 2, second, value))
    for t in range(NT):
        scaled = (t - center_t).astype(f32) * (1.0 / RT)
        base = 1.0 - scaled * scaled
        weight = jnp.where(slot == 3, 4.0 * scaled * base * (1.0 / RT), base * base)
        weight = jnp.where(jnp.abs(scaled) < 1.0, weight, 0.0)
        for i, part in enumerate(split(x_table * weight)):
            tx_split[i, pl.ds(t * rows, rows), :] = part
    copy.wait()
    power_u[...] = jnp.ones((cells, NY), f32)
    v = pair[1].reshape(cells, NY)
    power = v
    powers_v[0] = v
    for b in range(1, POWERS - 1):
        power = power * v
        powers_v[b] = power
    tile = 256

    def one_power(a, _):
        for b in range(POWERS):
            for h in range(cells // tile):
                part = pl.ds(h * tile, tile)
                monomial = power_u[part, :]
                if b:
                    monomial = monomial * powers_v[b - 1, part, :]
                both = jnp.concatenate(split(monomial), axis=1)
                across = dot(y_split[...], both, NT_DIMS)
                across_high, across_low = split(across[:ROWS] + across[ROWS:])
                high[pl.ds(b * ROWS, ROWS), part] = across_high
                low[pl.ds(b * ROWS, ROWS), part] = across_low
        result = (
            dot(high[...], tx_split[0], NN_DIMS)
            + dot(low[...], tx_split[0], NN_DIMS)
            + dot(high[...], tx_split[1], NN_DIMS)
        )
        span = POWERS * ROWS
        place = pl.ds(pl.multiple_of(a * span, 8), span)
        out[0, place, :] = result[:, :128]
        out[1, place, :] = result[:, 128:]
        power_u[...] = power_u[...] * pair[0].reshape(cells, NY)
        return 0

    lax.fori_loop(0, POWERS, one_power, 0)


def integrals(where, cx, cy, ct, fields):
    rows = fields.shape[3]
    cells = NT * rows
    smem = pl.BlockSpec(memory_space=pltpu.SMEM)
    return pl.pallas_call(
        functools.partial(integrals_kernel, rows),
        out_shape=jax.ShapeDtypeStruct((2, POWERS * POWERS * ROWS, 128), f32),
        in_specs=[smem] * 4 + [pl.BlockSpec(memory_space=pl.ANY)],
        out_specs=pl.BlockSpec(memory_space=pltpu.VMEM),
        scratch_shapes=[
            pltpu.VMEM((2, NT, rows, NY), f32),
            pltpu.VMEM((cells, NY), f32),
            pltpu.VMEM((POWERS - 1, cells, NY), f32),
            pltpu.VMEM((2 * ROWS, 2 * NY), bf16),
            pltpu.VMEM((2, cells, LANES), bf16),
            pltpu.VMEM((POWERS * ROWS, cells), bf16),
            pltpu.VMEM((POWERS * ROWS, cells), bf16),
            pltpu.SemaphoreType.DMA,
        ],
        compiler_params=pltpu.CompilerParams(vmem_limit_bytes=VMEM_LIMIT),
        cost_estimate=pl.CostEstimate(flops=10**10, bytes_accessed=3 * 10**6, transcendentals=0),
        name="integrals",
    )(where, cx, cy, ct, fields)


def pick_kernel(local, shares, me, *refs):
    libs = refs[:shares]
    flat, out = refs[shares:]
    lane = lax.broadcasted_iota(jnp.int32, (8, 128), 1)
    left = lane < 64

    def place(j, a, b, dx, dy):
        row = pl.multiple_of((a * POWERS + b) * ROWS + dy * KY, 8)
        chunk = dx >> 1
        odd = (dx & 1) == 1
        top = flat[chunk, pl.ds(row, 8), :]
        low = flat[chunk, pl.ds(row + 8, 8), :]
        even_value = jnp.where(left, top, pltpu.roll(low, 64, 1))
        odd_value = jnp.where(left, pltpu.roll(top, 64, 1), low)
        out[pl.ds(pl.multiple_of(j * 8, 8), 8), :] = jnp.where(odd, odd_value, even_value)

    for k in range(shares):
        owner = lax.rem(me[0] + k, shares)
        lib = libs[k]

        def term(i, _):
            place(owner * local + i, lib[i, 0], lib[i, 1], lib[i, 2], lib[i, 3])
            return 0

        lax.fori_loop(0, local, term, 0)
    place(TERMS, 1, 0, 3, 0)
    place(TERMS + 1, 0, 1, 3, 0)
    out[pl.ds((TERMS + 2) * 8, 48), :] = jnp.zeros((48, 128), f32)


def pick(where, libs, flat):
    shares = len(libs)
    smem = pl.BlockSpec(memory_space=pltpu.SMEM)
    vmem = pl.BlockSpec(memory_space=pltpu.VMEM)
    return pl.pallas_call(
        functools.partial(pick_kernel, libs[0].shape[0], shares),
        out_shape=jax.ShapeDtypeStruct(((TERMS + 8) * 8, 128), f32),
        in_specs=[smem] * (1 + shares) + [vmem],
        out_specs=vmem,
        compiler_params=pltpu.CompilerParams(vmem_limit_bytes=VMEM_LIMIT),
        name="pick",
    )(where, *libs, flat)


def fit_kernel(own, other, grp, payload, normal, dmat):
    pad = TERMS + 8
    gram = jnp.zeros((pad, pad), f32)
    for q in range(4):
        parts = []
        for s in (2 * q, 2 * q + 1):
            rows = pl.ds(s, pad, stride=8)
            parts.append(own[rows, :] + other[rows, :])
        x = jnp.concatenate(parts, axis=1)
        gram = gram + dot3(x, x, NT_DIMS)
    ri = lax.broadcasted_iota(jnp.int32, (pad, pad), 0)
    ci = lax.broadcasted_iota(jnp.int32, (pad, pad), 1)
    diagonal = jnp.where(ri == ci, gram, 0.0)
    dcol = jnp.sum(diagonal, axis=1, keepdims=True)
    drow = jnp.sum(diagonal, axis=0, keepdims=True)
    icol = 1.0 / jnp.sqrt(dcol * (1.0 / TESTS) + 1e-06)
    irow = 1.0 / jnp.sqrt(drow * (1.0 / TESTS) + 1e-06)
    norm = (gram * (icol * (1.0 / TESTS))) * irow
    norm = jnp.where(ci < TERMS, norm, 0.0)
    corr = norm[:TERMS, :TERMS]
    squares = jnp.sum(jnp.sum(corr * corr, axis=0, keepdims=True), axis=1, keepdims=True)
    normal[...] = norm[:, :TERMS]
    gi = lax.broadcasted_iota(jnp.int32, (GROUPS, TERMS), 0)
    onehot = gi == grp[...]
    quad = jnp.zeros((32, GROUPS * GROUPS + GROUPS), f32)
    for s in range(2):
        right = norm[TERMS + s : TERMS + s + 1, :TERMS]
        spread = jnp.where(onehot, right, 0.0)
        d = dot3(spread, corr, NN_DIMS)
        dmat[pl.ds(s * GROUPS, GROUPS), :] = d
        masked = [jnp.where(grp[...] == h, d, 0.0) for h in range(GROUPS)]
        masked = jnp.concatenate(masked + [spread], axis=0)
        left = jnp.concatenate([d, right, jnp.zeros((7, TERMS), f32)], axis=0)
        quad = quad + dot3(left, masked, NT_DIMS)
    width = payload.shape[1]
    payload[...] = jnp.zeros((32, width), f32)
    payload[:, : quad.shape[1]] = quad
    payload[pl.ds(31, 1), :] = jnp.broadcast_to(squares, (1, width))


def fit(own, other, grp):
    vmem = pl.BlockSpec(memory_space=pltpu.VMEM)
    return pl.pallas_call(
        fit_kernel,
        out_shape=(
            jax.ShapeDtypeStruct((32, 640), f32),
            jax.ShapeDtypeStruct((TERMS + 8, TERMS), f32),
            jax.ShapeDtypeStruct((2 * GROUPS, TERMS), f32),
        ),
        in_specs=[vmem] * 3,
        out_specs=(vmem,) * 3,
        compiler_params=pltpu.CompilerParams(vmem_limit_bytes=VMEM_LIMIT),
        name="fit",
    )(own, other, grp)


def column(row, n):
    ri = lax.broadcasted_iota(jnp.int32, (n, n), 0)
    ci = lax.broadcasted_iota(jnp.int32, (n, n), 1)
    return jnp.sum(jnp.where(ri == ci, row, 0.0), axis=1, keepdims=True)


def end_kernel(shares, grp, normal, dmat, *refs):
    pieces = refs[:shares]
    coef, misfit = refs[shares:]
    total = pieces[0][...]
    largest = total[31:32, :1]
    for piece in pieces[1:]:
        value = piece[...]
        total = total + value
        largest = jnp.maximum(largest, value[31:32, :1])
    step = 1.0 / jnp.sqrt(largest)
    wide = GROUPS * GROUPS
    quad = total[:GROUPS, :wide]
    cross = total[GROUPS : GROUPS + 1, :wide]
    rr = total[GROUPS : GROUPS + 1, wide : wide + GROUPS]

    def factor(totals):
        threshold = 0.7 * jnp.sqrt(jnp.sum(totals, axis=1, keepdims=True) * (1.0 / GROUPS))
        return jnp.maximum(0.0, 1.0 - threshold / jnp.sqrt(totals + 1e-12))

    f_row = factor(step * step * rr)
    f_col = column(f_row, GROUPS)
    ci = lax.broadcasted_iota(jnp.int32, (GROUPS, wide), 1)
    gi = lax.broadcasted_iota(jnp.int32, (GROUPS, wide), 0)
    block = (ci >= gi * GROUPS) & (ci < gi * GROUPS + GROUPS)
    first_col = jnp.sum(jnp.where(block, gi * GROUPS, 0), axis=0, keepdims=True)
    tiled = jnp.sum(jnp.where(ci - first_col == gi, f_col, 0.0), axis=0, keepdims=True)
    dd = jnp.sum(quad * f_col, axis=0, keepdims=True) * tiled
    rd = cross * tiled
    dd_col = jnp.sum(jnp.where(block, dd, 0.0), axis=1, keepdims=True)
    rd_col = jnp.sum(jnp.where(block, rd, 0.0), axis=1, keepdims=True)
    grow = 1.0 + f_col
    rr_col = column(rr, GROUPS)
    two_col = (step * step) * (grow * grow * rr_col - 2.0 * step * grow * rd_col + step * step * dd_col)
    two_col = jnp.maximum(two_col, 0.0)
    threshold = 0.7 * jnp.sqrt(jnp.sum(two_col, axis=0, keepdims=True) * (1.0 / GROUPS))
    f2_col = jnp.maximum(0.0, 1.0 - threshold / jnp.sqrt(two_col + 1e-12))
    g2 = lax.broadcasted_iota(jnp.int32, (GROUPS, TERMS), 0)
    onehot = g2 == grp[...]
    f_term = jnp.sum(jnp.where(onehot, f_col, 0.0), axis=0, keepdims=True)
    f2_term = jnp.sum(jnp.where(onehot, f2_col, 0.0), axis=0, keepdims=True)
    seconds = []
    for s in range(2):
        right = normal[pl.ds(TERMS + s, 1), :]
        pulled = jnp.sum(dmat[pl.ds(s * GROUPS, GROUPS), :] * f_col, axis=0, keepdims=True)
        seconds.append(step * ((1.0 + f_term) * right - step * pulled) * f2_term)
    second = jnp.concatenate(seconds + [jnp.zeros((6, TERMS), f32)], axis=0)
    coef[0] = (second / step)[:2]
    moved = dot3(second, normal[pl.ds(0, TERMS), :], NN_DIMS)
    misfit[0] = normal[pl.ds(TERMS, 2), :] - moved[:2]


def end(grp, normal, dmat, pieces):
    vmem = pl.BlockSpec(memory_space=pltpu.VMEM)
    shape = jax.ShapeDtypeStruct((1, 2, TERMS), f32)
    return pl.pallas_call(
        functools.partial(end_kernel, len(pieces)),
        out_shape=(shape, shape),
        in_specs=[vmem] * (3 + len(pieces)),
        out_specs=(vmem, vmem),
        compiler_params=pltpu.CompilerParams(vmem_limit_bytes=VMEM_LIMIT),
        name="finish",
    )(grp, normal, dmat, *pieces)


def body(fields, library, centers_x, centers_y, centers_t, groups):
    pgroup, rows = fields.shape[0], fields.shape[3]
    shares = lax.axis_size("term")
    local = library.shape[0]
    if pgroup != shares or local * shares != TERMS:
        raise ValueError("unexpected split")
    me = lax.axis_index("term")
    libs = [library]
    for k in range(1, shares):
        libs.append(lax.ppermute(library, "term", [((i + k) % shares, i) for i in range(shares)]))
    where = jnp.stack([me, lax.axis_index("space") * rows]).astype(jnp.int32)
    flat = integrals(where, centers_x, centers_y, centers_t, fields)
    own = pick(where, libs, flat)
    spaces = lax.axis_size("space")
    others = [
        lax.ppermute(own, "space", [((i + k) % spaces, i) for i in range(spaces)])
        for k in range(1, spaces)
    ]
    grp = groups.reshape(1, TERMS)
    payload, normal, dmat = fit(own, sum(others[1:], others[0]), grp)
    row = lax.broadcasted_iota(jnp.int32, payload.shape, 0)
    params = lax.axis_size("param")
    pieces = [payload]
    for k in range(1, shares):
        pieces.append(lax.ppermute(payload, "term", [((i + k) % shares, i) for i in range(shares)]))
    total = sum(pieces[1:], pieces[0])
    largest = functools.reduce(jnp.maximum, pieces)
    payload = jnp.where(row == 31, largest, total)
    pieces = [payload]
    for k in range(1, params):
        pieces.append(lax.ppermute(payload, "param", [((i + k) % params, i) for i in range(params)]))
    return end(grp, normal, dmat, pieces)


def solution(mesh):
    return jax.shard_map(
        body,
        mesh=mesh,
        in_specs=(P("param", None, None, "space", None), P("term", None), P(), P(), P(), P()),
        out_specs=(P(("param", "term"), None, None), P(("param", "term"), None, None)),
        check_vma=False,
    )
```

time: 324 us -> 59.2 us (0.18)
  matrix products: 153 us -> 0 us
  blocking collectives: 115 us -> 0 us
  Pallas kernels: 0 us -> 25.5 us
  local copies, waits for them, and re-layouts: 18.2 us -> 4.34 us
  starting transfers between devices: 6.23 us -> 13.7 us
  waiting for transfers between devices: 20.5 us -> 14.6 us
  other arithmetic: 5.62 us -> 0.16 us
    dot_general x33 -> x0, matrix products: 153 us -> none  [the longest x4 128 us: tile_integrals(): across_y = jnp.einsum('jtxy,jky->jtxk', monomial, y_pick, precision=highest)]
    psum x2 -> x0, blocking collectives: 75.5 us -> none  [the longest x1 38.8 us: body(): first_sq = lax.psum(group_squares(first_guess, onehot), ('param', 'term'))]
    pmax x1 -> x0, blocking collectives: 37.2 us -> none  [body(): largest = lax.pmax(jnp.max(frobenius), ('param', 'term'))]
    pallas_call x0 -> x4, Pallas kernels: none -> 25.5 us  [the longest x1 14.3 us: pick(): pl.pallas_call(functools.partial(pick_kernel, libs[0].shape[0], shares),...]
    all_to_all x1 -> x0, waiting for transfers between devices: 20.5 us -> none  [body(): lax.all_to_all(buffer.reshape(space_count * pgroup, row_count, half_tests...]
    ppermute x0 -> x10, waiting for transfers between devices: none -> 14.6 us  [the longest x3 7.71 us: body(): lax.ppermute(payload, 'term', [((i + k) % shares, i) for i in range(share...]
    ppermute x0 -> x10, starting transfers between devices: none -> 13.7 us  [the longest x3 6.08 us: body(): lax.ppermute(library, 'term', [((i + k) % shares, i) for i in range(share...]
    all_to_all x1 -> x0, starting transfers between devices: 6.23 us -> none  [body(): lax.all_to_all(buffer.reshape(space_count * pgroup, row_count, half_tests...]
  transfers between devices with their start and end apart: 1 -> 10, of which waited for: 1 -> 6; matrix products, arithmetic and copies ran while one was open for 0% -> 0% of each run, Pallas kernels for 0% -> 14%
where the time goes in v1:
time: 59.2 us; the launch traced here: 59 us
  Pallas kernels  25.5 us (43%)
  waiting for transfers between devices  14.6 us (25%)
  starting transfers between devices  13.7 us (23%)
  local copies, waits for them, and re-layouts  4.34 us (7%)
  between operations  0.71 us (1%)
    pallas_call x1, Pallas kernels, pick(): pl.pallas_call(functools.partial(pick_kernel, libs[0].shape[0], shares),...  14.3 us
    pallas_call x1, Pallas kernels, integrals(): pl.pallas_call(functools.partial(integrals_kernel, rows), out_shape=jax.S...  7.99 us
    ppermute x3, waiting for transfers between devices, body(): lax.ppermute(payload, 'term', [((i + k) % shares, i) for i in range(share...  7.71 us
    ppermute x3, starting transfers between devices, body(): lax.ppermute(library, 'term', [((i + k) % shares, i) for i in range(share...  6.08 us
    ppermute x3, waiting for transfers between devices, body(): lax.ppermute(payload, 'param', [((i + k) % params, i) for i in range(para...  4.75 us
    unnamed x11, local copies, waits for them, and re-layouts  4.34 us
    ppermute x3, starting transfers between devices, body(): lax.ppermute(payload, 'term', [((i + k) % shares, i) for i in range(share...  4 us
    ppermute x3, starting transfers between devices, body(): lax.ppermute(payload, 'param', [((i + k) % params, i) for i in range(para...  3.56 us
  transfers between devices with their start and end apart: 10, of which 6 were waited for; matrix products, arithmetic and copies ran while one was open for 0% of the time, Pallas kernels for 14%

profile of v1, /device:TPU:0, one launch (start us, length us, event | category | flops | bytes accessed | tf_op | source)
XLA Modules:
  0.0 59.0 jit_solution(12085490662010063460)
XLA Ops:
  0.6 0.8 %copy.11.refs_0_ = s32[42,4]{1,0:T(8,128)S(1)} copy(s32[42,4]{0,1:T(4,128)} %param.7) | data formatting | bytes 1344 | tf_op args[1]
  1.4 5.1 %collective-permute-start = (s32[42,4]{1,0:T(8,128)S(1)}, s32[42,4]{1,0:T(8,128)S(1)}, u32[]{:S(2)}, u32[]{:S(2)}) collective-permute-start(s32[42,4]{1,0:T(8,128)S(1)} %copy.11.refs_0_), channel_id=1, source_target_pairs={{1,0},{2,1},{3,2},{0,3},{5,4},{6,5},{7,6},{4,7},{9,8},{10,9},{11,1... | collective-permute-start | bytes 2024 | tf_op jit(solution)/shard_map/ppermute | solution.py:333
  6.5 0.0 collective-permute-start.1
  6.5 1.0 %collective-permute-start.2 = (s32[42,4]{1,0:T(8,128)S(1)}, s32[42,4]{1,0:T(8,128)S(1)}, u32[]{:S(2)}, u32[]{:S(2)}) collective-permute-start(s32[42,4]{1,0:T(8,128)S(1)} %copy.11.refs_0_), channel_id=1, source_target_pairs={{3,0},{0,1},{1,2},{2,3},{7,4},{4,5},{5,6},{6,7},{11,8},{8,9},{9,10... | collective-permute-start | bytes 2024 | tf_op jit(solution)/shard_map/ppermute | solution.py:333
  7.5 0.1 pad_add_fusion.where.me
  7.6 0.0 copy-start.1
  7.6 1.6 %copy-done.1 = f32[4,2,8,64,128]{4,3,2,1,0:T(8,128)S(1)} copy-done((f32[4,2,8,64,128]{4,3,2,1,0:T(8,128)S(1)}, f32[4,2,8,64,128]{4,3,2,1,0:T(8,128)}, u32[]{:S(2)}) %copy-start.1) | copy-done | bytes 2097176
  9.2 0.0 copy-start.2
  9.2 0.7 %copy-done.2 = s32[16]{0:T(128)S(1)} copy-done((s32[16]{0:T(128)S(1)}, s32[16]{0:T(128)}, u32[]{:S(2)}) %copy-start.2) | copy-done | bytes 88
  9.8 0.0 copy-start.3
  9.8 0.7 %copy-done.3 = s32[16]{0:T(128)S(1)} copy-done((s32[16]{0:T(128)S(1)}, s32[16]{0:T(128)}, u32[]{:S(2)}) %copy-start.3) | copy-done | bytes 88
  10.5 0.0 copy-start.4
  10.5 0.7 %copy-done.4 = s32[4]{0:T(128)S(1)} copy-done((s32[4]{0:T(128)S(1)}, s32[4]{0:T(128)}, u32[]{:S(2)}) %copy-start.4) | copy-done | bytes 40
  11.1 8.0 %integrals.1.refs_4_ = f32[2,2352,128]{2,1,0:T(8,128)S(1)} custom-call(s32[2]{0:T(128)S(1)} %pad_add_fusion.where.me, s32[16]{0:T(128)S(1)} %copy-done.2, s32[16]{0:T(128)S(1)} %copy-done.3, s32[4]{0:T(128)S(1)} %copy-done.4, f32[4,2,8,64,128]{4,3,2,1,0:T(8,128)S(1)} %copy-done.1), custom_call_target="tpu_custom_call" | custom-call | flops 10000000000 | bytes 3000000 | tf_op jit(solution)/shard_map/integrals/pallas_call | solution.py:133
  19.1 0.0 copy-start
  19.1 0.0 collective-permute-done.refs_1_
  19.1 0.0 collective-permute-done.1.refs_2_
  19.2 0.0 collective-permute-done.2.refs_3_
  19.2 14.3 %pick.1.own = f32[1408,128]{1,0:T(8,128)S(1)} custom-call(s32[2]{0:T(128)S(1)} %pad_add_fusion.where.me, s32[42,4]{1,0:T(8,128)S(1)} %copy.11.refs_0_, s32[42,4]{1,0:T(8,128)S(1)} %collective-permute-done.refs_1_, s32[42,4]{1,0:T(8,128)S(1)} %collective-permute-done.1.refs_2_, s32[42,4]{1,0:T(8,128)S(1)} %collective-permute-done.2.refs_3_, ...), custom_call_target="tpu_custom_call" | custom-call | tf_op jit(solution)/shard_map/pick/pallas_call | solution.py:188
  33.5 0.1 collective-permute-start.3
  33.6 2.2 %collective-permute-done.3.other = f32[1408,128]{1,0:T(8,128)S(1)} collective-permute-done((f32[1408,128]{1,0:T(8,128)S(1)}, f32[1408,128]{1,0:T(8,128)S(1)}, u32[]{:S(2)}, u32[]{:S(2)}) %collective-permute-start.3) | collective-permute-done | bytes 720928 | tf_op jit(solution)/shard_map/ppermute | solution.py:339
  35.8 0.0 copy-done
  35.8 2.0 %fit.1 = (f32[32,640]{1,0:T(8,128)S(1)}, f32[176,168]{1,0:T(8,128)S(1)}, f32[48,168]{1,0:T(8,128)S(1)}) custom-call(f32[1408,128]{1,0:T(8,128)S(1)} %pick.1.own, f32[1408,128]{1,0:T(8,128)S(1)} %collective-permute-done.3.other, s32[1,168]{1,0:T(1,128)S(1)} %bitcast.3), custom_call_target="tpu_custom_call" | custom-call | tf_op jit(solution)/shard_map/fit/pallas_call | solution.py:240
  37.8 2.9 %collective-permute-start.4 = (f32[32,640]{1,0:T(8,128)S(1)}, f32[32,640]{1,0:T(8,128)S(1)}, u32[]{:S(2)}, u32[]{:S(2)}) collective-permute-start(f32[32,640]{1,0:T(8,128)S(1)} %get-tuple-element.7), channel_id=1, source_target_pairs={{1,0},{2,1},{3,2},{0,3},{5,4},{6,5},{7,6},{4,7},{9,8},{10,9},{11,1... | collective-permute-start | bytes 245768 | tf_op jit(solution)/shard_map/ppermute | solution.py:348
  40.6 1.1 %collective-permute-start.5 = (f32[32,640]{1,0:T(8,128)S(1)}, f32[32,640]{1,0:T(8,128)S(1)}, u32[]{:S(2)}, u32[]{:S(2)}) collective-permute-start(f32[32,640]{1,0:T(8,128)S(1)} %get-tuple-element.7), channel_id=1, source_target_pairs={{2,0},{3,1},{0,2},{1,3},{6,4},{7,5},{4,6},{5,7},{10,8},{11,9},{8,1... | collective-permute-start | bytes 245768 | tf_op jit(solution)/shard_map/ppermute | solution.py:348
  41.7 0.0 collective-permute-start.6
  41.8 1.7 %collective-permute-done.4 = f32[32,640]{1,0:T(8,128)S(1)} collective-permute-done((f32[32,640]{1,0:T(8,128)S(1)}, f32[32,640]{1,0:T(8,128)S(1)}, u32[]{:S(2)}, u32[]{:S(2)}) %collective-permute-start.4) | collective-permute-done | bytes 81952 | tf_op jit(solution)/shard_map/ppermute | solution.py:348
  43.5 6.0 %collective-permute-done.5 = f32[32,640]{1,0:T(8,128)S(1)} collective-permute-done((f32[32,640]{1,0:T(8,128)S(1)}, f32[32,640]{1,0:T(8,128)S(1)}, u32[]{:S(2)}, u32[]{:S(2)}) %collective-permute-start.5) | collective-permute-done | bytes 81952 | tf_op jit(solution)/shard_map/ppermute | solution.py:348
  49.5 0.0 collective-permute-done.6
  49.5 0.1 add_select_fusion.refs_0_
  49.5 2.5 %collective-permute-start.7 = (f32[32,640]{1,0:T(8,128)S(1)}, f32[32,640]{1,0:T(8,128)S(1)}, u32[]{:S(2)}, u32[]{:S(2)}) collective-permute-start(f32[32,640]{1,0:T(8,128)S(1)} %add_select_fusion.refs_0_), channel_id=1, source_target_pairs={{8,0},{16,8},{24,16},{0,24},{9,1},{17,9},{25,17},{1,25},{10,2},{18... | collective-permute-start | bytes 245768 | tf_op jit(solution)/shard_map/ppermute | solution.py:354
  52.0 0.5 collective-permute-start.8
  52.5 0.6 %collective-permute-start.9 = (f32[32,640]{1,0:T(8,128)S(1)}, f32[32,640]{1,0:T(8,128)S(1)}, u32[]{:S(2)}, u32[]{:S(2)}) collective-permute-start(f32[32,640]{1,0:T(8,128)S(1)} %add_select_fusion.refs_0_), channel_id=1, source_target_pairs={{24,0},{0,8},{8,16},{16,24},{25,1},{1,9},{9,17},{17,25},{26,2},{2,... | collective-permute-start | bytes 245768 | tf_op jit(solution)/shard_map/ppermute | solution.py:354
  53.1 1.2 %collective-permute-done.7.refs_1_ = f32[32,640]{1,0:T(8,128)S(1)} collective-permute-done((f32[32,640]{1,0:T(8,128)S(1)}, f32[32,640]{1,0:T(8,128)S(1)}, u32[]{:S(2)}, u32[]{:S(2)}) %collective-permute-start.7) | collective-permute-done | bytes 81952 | tf_op jit(solution)/shard_map/ppermute | solution.py:354
  54.3 2.5 %collective-permute-done.8.refs_2_ = f32[32,640]{1,0:T(8,128)S(1)} collective-permute-done((f32[32,640]{1,0:T(8,128)S(1)}, f32[32,640]{1,0:T(8,128)S(1)}, u32[]{:S(2)}, u32[]{:S(2)}) %collective-permute-start.8) | collective-permute-done | bytes 81952 | tf_op jit(solution)/shard_map/ppermute | solution.py:354
  56.8 1.1 %collective-permute-done.9.refs_3_ = f32[32,640]{1,0:T(8,128)S(1)} collective-permute-done((f32[32,640]{1,0:T(8,128)S(1)}, f32[32,640]{1,0:T(8,128)S(1)}, u32[]{:S(2)}, u32[]{:S(2)}) %collective-permute-start.9) | collective-permute-done | bytes 81952 | tf_op jit(solution)/shard_map/ppermute | solution.py:354
  57.8 1.2 %finish.1 = (f32[1,2,168]{2,1,0:T(2,128)}, f32[1,2,168]{2,1,0:T(2,128)}) custom-call(s32[1,168]{1,0:T(1,128)S(1)} %bitcast.4, f32[176,168]{1,0:T(8,128)S(1)} %get-tuple-element.5.normal, f32[48,168]{1,0:T(8,128)S(1)} %get-tuple-element.6.dmat, f32[32,640]{1,0:T(8,128)S(1)} %add_select_fusion.refs_0_, f32[32,640]{1,0:T(8,128)S(1)} %collective-permute-done.7.refs_1_, ...), custom_call_target="tpu_custom_call" | custom-call | tf_op jit(solution)/shard_map/finish/pallas_call | solution.py:314
  (1 shorter events, 0.0 us)
Async XLA Ops:
  1.4 17.7 %collective-permute-start = (s32[42,4]{1,0:T(8,128)S(1)}, s32[42,4]{1,0:T(8,128)S(1)}, u32[]{:S(2)}, u32[]{:S(2)}) collective-permute-start(s32[42,4]{1,0:T(8,128)S(1)} %copy.11.refs_0_), channel_id=1, source_target_pairs={{1,0},{2,1},{3,2},{0,3},{5,4},{6,5},{7,6},{4,7},{9,8},{10,9},{11,1... | collective-permute-start | bytes 2024 | tf_op jit(solution)/shard_map/ppermute | solution.py:333
  6.5 12.7 %collective-permute-start.1 = (s32[42,4]{1,0:T(8,128)S(1)}, s32[42,4]{1,0:T(8,128)S(1)}, u32[]{:S(2)}, u32[]{:S(2)}) collective-permute-start(s32[42,4]{1,0:T(8,128)S(1)} %copy.11.refs_0_), channel_id=1, source_target_pairs={{2,0},{3,1},{0,2},{1,3},{6,4},{7,5},{4,6},{5,7},{10,8},{11,9},{8,1... | collective-permute-start | bytes 2024 | tf_op jit(solution)/shard_map/ppermute | solution.py:333
  6.5 12.7 %collective-permute-start.2 = (s32[42,4]{1,0:T(8,128)S(1)}, s32[42,4]{1,0:T(8,128)S(1)}, u32[]{:S(2)}, u32[]{:S(2)}) collective-permute-start(s32[42,4]{1,0:T(8,128)S(1)} %copy.11.refs_0_), channel_id=1, source_target_pairs={{3,0},{0,1},{1,2},{2,3},{7,4},{4,5},{5,6},{6,7},{11,8},{8,9},{9,10... | collective-permute-start | bytes 2024 | tf_op jit(solution)/shard_map/ppermute | solution.py:333
  7.6 1.6 %copy-start.1 = (f32[4,2,8,64,128]{4,3,2,1,0:T(8,128)S(1)}, f32[4,2,8,64,128]{4,3,2,1,0:T(8,128)}, u32[]{:S(2)}) copy-start(f32[4,2,8,64,128]{4,3,2,1,0:T(8,128)} %fields.1) | copy-start | bytes 6291460
  9.2 0.7 %copy-start.2 = (s32[16]{0:T(128)S(1)}, s32[16]{0:T(128)}, u32[]{:S(2)}) copy-start(s32[16]{0:T(128)} %cx.1) | copy-start | bytes 196
  9.8 0.7 %copy-start.3 = (s32[16]{0:T(128)S(1)}, s32[16]{0:T(128)}, u32[]{:S(2)}) copy-start(s32[16]{0:T(128)} %cy.1) | copy-start | bytes 196
  10.5 0.7 %copy-start.4 = (s32[4]{0:T(128)S(1)}, s32[4]{0:T(128)}, u32[]{:S(2)}) copy-start(s32[4]{0:T(128)} %ct.1) | copy-start | bytes 52
  19.1 16.6 %copy-start = (s32[168]{0:T(256)S(1)}, s32[168]{0:T(256)}, u32[]{:S(2)}) copy-start(s32[168]{0:T(256)} %param.11) | copy-start | bytes 2020
  33.5 2.3 %collective-permute-start.3 = (f32[1408,128]{1,0:T(8,128)S(1)}, f32[1408,128]{1,0:T(8,128)S(1)}, u32[]{:S(2)}, u32[]{:S(2)}) collective-permute-start(f32[1408,128]{1,0:T(8,128)S(1)} %pick.1.own), channel_id=1, source_target_pairs={{4,0},{0,4},{5,1},{1,5},{6,2},{2,6},{7,3},{3,7},{12,8},{8,12},{13,... | collective-permute-start | bytes 2162696 | tf_op jit(solution)/shard_map/ppermute | solution.py:339
  37.8 5.7 %collective-permute-start.4 = (f32[32,640]{1,0:T(8,128)S(1)}, f32[32,640]{1,0:T(8,128)S(1)}, u32[]{:S(2)}, u32[]{:S(2)}) collective-permute-start(f32[32,640]{1,0:T(8,128)S(1)} %get-tuple-element.7), channel_id=1, source_target_pairs={{1,0},{2,1},{3,2},{0,3},{5,4},{6,5},{7,6},{4,7},{9,8},{10,9},{11,1... | collective-permute-start | bytes 245768 | tf_op jit(solution)/shard_map/ppermute | solution.py:348
  40.6 8.8 %collective-permute-start.5 = (f32[32,640]{1,0:T(8,128)S(1)}, f32[32,640]{1,0:T(8,128)S(1)}, u32[]{:S(2)}, u32[]{:S(2)}) collective-permute-start(f32[32,640]{1,0:T(8,128)S(1)} %get-tuple-element.7), channel_id=1, source_target_pairs={{2,0},{3,1},{0,2},{1,3},{6,4},{7,5},{4,6},{5,7},{10,8},{11,9},{8,1... | collective-permute-start | bytes 245768 | tf_op jit(solution)/shard_map/ppermute | solution.py:348
  41.7 7.7 %collective-permute-start.6 = (f32[32,640]{1,0:T(8,128)S(1)}, f32[32,640]{1,0:T(8,128)S(1)}, u32[]{:S(2)}, u32[]{:S(2)}) collective-permute-start(f32[32,640]{1,0:T(8,128)S(1)} %get-tuple-element.7), channel_id=1, source_target_pairs={{3,0},{0,1},{1,2},{2,3},{7,4},{4,5},{5,6},{6,7},{11,8},{8,9},{9,10... | collective-permute-start | bytes 245768 | tf_op jit(solution)/shard_map/ppermute | solution.py:348
  49.5 4.8 %collective-permute-start.7 = (f32[32,640]{1,0:T(8,128)S(1)}, f32[32,640]{1,0:T(8,128)S(1)}, u32[]{:S(2)}, u32[]{:S(2)}) collective-permute-start(f32[32,640]{1,0:T(8,128)S(1)} %add_select_fusion.refs_0_), channel_id=1, source_target_pairs={{8,0},{16,8},{24,16},{0,24},{9,1},{17,9},{25,17},{1,25},{10,2},{18... | collective-permute-start | bytes 245768 | tf_op jit(solution)/shard_map/ppermute | solution.py:354
  52.0 4.8 %collective-permute-start.8 = (f32[32,640]{1,0:T(8,128)S(1)}, f32[32,640]{1,0:T(8,128)S(1)}, u32[]{:S(2)}, u32[]{:S(2)}) collective-permute-start(f32[32,640]{1,0:T(8,128)S(1)} %add_select_fusion.refs_0_), channel_id=1, source_target_pairs={{16,0},{24,8},{0,16},{8,24},{17,1},{25,9},{1,17},{9,25},{18,2},{26... | collective-permute-start | bytes 245768 | tf_op jit(solution)/shard_map/ppermute | solution.py:354
  52.5 5.3 %collective-permute-start.9 = (f32[32,640]{1,0:T(8,128)S(1)}, f32[32,640]{1,0:T(8,128)S(1)}, u32[]{:S(2)}, u32[]{:S(2)}) collective-permute-start(f32[32,640]{1,0:T(8,128)S(1)} %add_select_fusion.refs_0_), channel_id=1, source_target_pairs={{24,0},{0,8},{8,16},{16,24},{25,1},{1,9},{9,17},{17,25},{26,2},{2,... | collective-permute-start | bytes 245768 | tf_op jit(solution)/shard_map/ppermute | solution.py:354

commit v2 on v1

--- a/solution.py
+++ b/solution.py
@@ -21,6 +21,8 @@
 GROUPS = 24
 ROWS = 3 * KY
 LANES = 4 * KT * KX
+HALF = GROUPS // 2 + 1
+WIDTH = 384
 VMEM_LIMIT = 40 * 2**20
 
 f32, bf16 = jnp.float32, jnp.bfloat16
@@ -57,11 +59,21 @@
 
 
 def integrals_kernel(
-    rows, where, cx, cy, ct, fields, out, pair, power_u, powers_v, y_split, tx_split, high, low, sem
+    rows, centers_x, centers_y, centers_t, fields, out,
+    cx, cy, ct, pair, power_u, powers_v, y_split, tx_split, high, low, sem,
 ):
     cells = NT * rows
-    copy = pltpu.make_async_copy(fields.at[where[0]], pair, sem)
+    first_row = lax.axis_index("space") * rows
+    copy = pltpu.make_async_copy(fields.at[lax.axis_index("term")], pair, sem.at[0])
+    small = [
+        pltpu.make_async_copy(source, target, sem.at[1 + i])
+        for i, (source, target) in enumerate(((centers_x, cx), (centers_y, cy), (centers_t, ct)))
+    ]
+    for one in small:
+        one.start()
     copy.start()
+    for one in small:
+        one.wait()
     row = lax.broadcasted_iota(jnp.int32, (KY, NY), 0)
     lane = lax.broadcasted_iota(jnp.int32, (KY, NY), 1)
     center = jnp.zeros((KY, NY), jnp.int32)
@@ -78,7 +90,7 @@
         center_x = jnp.where(kx == k, cx[k], center_x)
     for k in range(KT):
         center_t = jnp.where(kt == k, ct[k], center_t)
-    row = lax.broadcasted_iota(jnp.int32, (rows, LANES), 0) + where[1]
+    row = lax.broadcasted_iota(jnp.int32, (rows, LANES), 0) + first_row
     offset = ((row - center_x + NX // 2) & (NX - 1)) - NX // 2
     value, first, second = space_rows(offset)
     x_table = jnp.where(slot == 1, first, jnp.where(slot == 2, second, value))
@@ -126,16 +138,19 @@
     lax.fori_loop(0, POWERS, one_power, 0)
 
 
-def integrals(where, cx, cy, ct, fields):
+def integrals(cx, cy, ct, fields):
     rows = fields.shape[3]
     cells = NT * rows
-    smem = pl.BlockSpec(memory_space=pltpu.SMEM)
+    operands = [pltpu.with_memory_space_constraint(x, pltpu.HBM) for x in (cx, cy, ct, fields)]
     return pl.pallas_call(
         functools.partial(integrals_kernel, rows),
         out_shape=jax.ShapeDtypeStruct((2, POWERS * POWERS * ROWS, 128), f32),
-        in_specs=[smem] * 4 + [pl.BlockSpec(memory_space=pl.ANY)],
+        in_specs=[pl.BlockSpec(memory_space=pltpu.HBM)] * 4,
         out_specs=pl.BlockSpec(memory_space=pltpu.VMEM),
         scratch_shapes=[
+            pltpu.SMEM((KX,), jnp.int32),
+            pltpu.SMEM((KY,), jnp.int32),
+            pltpu.SMEM((KT,), jnp.int32),
             pltpu.VMEM((2, NT, rows, NY), f32),
             pltpu.VMEM((cells, NY), f32),
             pltpu.VMEM((POWERS - 1, cells, NY), f32),
@@ -143,56 +158,61 @@
             pltpu.VMEM((2, cells, LANES), bf16),
             pltpu.VMEM((POWERS * ROWS, cells), bf16),
             pltpu.VMEM((POWERS * ROWS, cells), bf16),
-            pltpu.SemaphoreType.DMA,
+            pltpu.SemaphoreType.DMA((4,)),
         ],
         compiler_params=pltpu.CompilerParams(vmem_limit_bytes=VMEM_LIMIT),
         cost_estimate=pl.CostEstimate(flops=10**10, bytes_accessed=3 * 10**6, transcendentals=0),
         name="integrals",
-    )(where, cx, cy, ct, fields)
-
-
-def pick_kernel(local, shares, me, *refs):
+    )(*operands)
+
+
+def pick_kernel(local, shares, *refs):
     libs = refs[:shares]
     flat, out = refs[shares:]
-    lane = lax.broadcasted_iota(jnp.int32, (8, 128), 1)
-    left = lane < 64
-
-    def place(j, a, b, dx, dy):
+    left = lax.broadcasted_iota(jnp.int32, (8, 128), 1) < 64
+    me = lax.axis_index("term")
+
+    def load(a, b, dx, dy):
         row = pl.multiple_of((a * POWERS + b) * ROWS + dy * KY, 8)
         chunk = dx >> 1
-        odd = (dx & 1) == 1
-        top = flat[chunk, pl.ds(row, 8), :]
-        low = flat[chunk, pl.ds(row + 8, 8), :]
+        return (dx & 1) == 1, flat[chunk, pl.ds(row, 8), :], flat[chunk, pl.ds(row + 8, 8), :]
+
+    def store(j, odd, top, low):
         even_value = jnp.where(left, top, pltpu.roll(low, 64, 1))
         odd_value = jnp.where(left, pltpu.roll(top, 64, 1), low)
         out[pl.ds(pl.multiple_of(j * 8, 8), 8), :] = jnp.where(odd, odd_value, even_value)
 
+    batch = max(n for n in range(1, 22) if local % n == 0)
     for k in range(shares):
-        owner = lax.rem(me[0] + k, shares)
+        first = lax.rem(me + k, shares) * local
         lib = libs[k]
 
-        def term(i, _):
-            place(owner * local + i, lib[i, 0], lib[i, 1], lib[i, 2], lib[i, 3])
+        def some(i, _):
+            loaded = [
+                load(*(lib[part, i * batch + n] for part in range(4))) for n in range(batch)
+            ]
+            for n in range(batch):
+                store(first + i * batch + n, *loaded[n])
             return 0
 
-        lax.fori_loop(0, local, term, 0)
-    place(TERMS, 1, 0, 3, 0)
-    place(TERMS + 1, 0, 1, 3, 0)
+        lax.fori_loop(0, local // batch, some, 0)
+    store(TERMS, *load(1, 0, 3, 0))
+    store(TERMS + 1, *load(0, 1, 3, 0))
     out[pl.ds((TERMS + 2) * 8, 48), :] = jnp.zeros((48, 128), f32)
 
 
-def pick(where, libs, flat):
+def pick(libs, flat):
     shares = len(libs)
     smem = pl.BlockSpec(memory_space=pltpu.SMEM)
     vmem = pl.BlockSpec(memory_space=pltpu.VMEM)
     return pl.pallas_call(
-        functools.partial(pick_kernel, libs[0].shape[0], shares),
+        functools.partial(pick_kernel, libs[0].shape[1], shares),
         out_shape=jax.ShapeDtypeStruct(((TERMS + 8) * 8, 128), f32),
-        in_specs=[smem] * (1 + shares) + [vmem],
+        in_specs=[smem] * shares + [vmem],
         out_specs=vmem,
         compiler_params=pltpu.CompilerParams(vmem_limit_bytes=VMEM_LIMIT),
         name="pick",
-    )(where, *libs, flat)
+    )(*libs, flat)
 
 
 def fit_kernel(own, other, grp, payload, normal, dmat):
@@ -219,20 +239,25 @@
     normal[...] = norm[:, :TERMS]
     gi = lax.broadcasted_iota(jnp.int32, (GROUPS, TERMS), 0)
     onehot = gi == grp[...]
-    quad = jnp.zeros((32, GROUPS * GROUPS + GROUPS), f32)
+    products = [0.0] * (HALF + 2)
     for s in range(2):
         right = norm[TERMS + s : TERMS + s + 1, :TERMS]
-        spread = jnp.where(onehot, right, 0.0)
-        d = dot3(spread, corr, NN_DIMS)
+        d = dot3(jnp.where(onehot, right, 0.0), corr, NN_DIMS)
         dmat[pl.ds(s * GROUPS, GROUPS), :] = d
-        masked = [jnp.where(grp[...] == h, d, 0.0) for h in range(GROUPS)]
-        masked = jnp.concatenate(masked + [spread], axis=0)
-        left = jnp.concatenate([d, right, jnp.zeros((7, TERMS), f32)], axis=0)
-        quad = quad + dot3(left, masked, NT_DIMS)
-    width = payload.shape[1]
-    payload[...] = jnp.zeros((32, width), f32)
-    payload[:, : quad.shape[1]] = quad
-    payload[pl.ds(31, 1), :] = jnp.broadcast_to(squares, (1, width))
+        products[0] = products[0] + d * d
+        for shift in range(1, HALF):
+            products[shift] = products[shift] + d * jnp.concatenate([d[shift:], d[:shift]], axis=0)
+        products[HALF] = products[HALF] + d * right
+        products[HALF + 1] = products[HALF + 1] + right * right
+    used = HALF * GROUPS + GROUPS + 1
+    products[HALF + 1] = jnp.concatenate(
+        [products[HALF + 1], jnp.zeros((WIDTH - used, TERMS), f32)], axis=0
+    )
+    high, low = split(jnp.concatenate(products, axis=0))
+    members = onehot.astype(f32).astype(bf16)
+    sums = dot(members, high, NT_DIMS) + dot(members, low, NT_DIMS)
+    col = lax.broadcasted_iota(jnp.int32, (GROUPS, WIDTH), 1)
+    payload[...] = jnp.where(col == WIDTH - 1, squares, sums)
 
 
 def fit(own, other, grp):
@@ -240,7 +265,7 @@
     return pl.pallas_call(
         fit_kernel,
         out_shape=(
-            jax.ShapeDtypeStruct((32, 640), f32),
+            jax.ShapeDtypeStruct((GROUPS, WIDTH), f32),
             jax.ShapeDtypeStruct((TERMS + 8, TERMS), f32),
             jax.ShapeDtypeStruct((2 * GROUPS, TERMS), f32),
         ),
@@ -251,50 +276,45 @@
     )(own, other, grp)
 
 
-def column(row, n):
-    ri = lax.broadcasted_iota(jnp.int32, (n, n), 0)
-    ci = lax.broadcasted_iota(jnp.int32, (n, n), 1)
-    return jnp.sum(jnp.where(ri == ci, row, 0.0), axis=1, keepdims=True)
-
-
 def end_kernel(shares, grp, normal, dmat, *refs):
     pieces = refs[:shares]
     coef, misfit = refs[shares:]
     total = pieces[0][...]
-    largest = total[31:32, :1]
+    largest = total[:1, WIDTH - 1 :]
     for piece in pieces[1:]:
         value = piece[...]
         total = total + value
-        largest = jnp.maximum(largest, value[31:32, :1])
+        largest = jnp.maximum(largest, value[:1, WIDTH - 1 :])
     step = 1.0 / jnp.sqrt(largest)
-    wide = GROUPS * GROUPS
-    quad = total[:GROUPS, :wide]
-    cross = total[GROUPS : GROUPS + 1, :wide]
-    rr = total[GROUPS : GROUPS + 1, wide : wide + GROUPS]
+    first = HALF * GROUPS
 
     def factor(totals):
-        threshold = 0.7 * jnp.sqrt(jnp.sum(totals, axis=1, keepdims=True) * (1.0 / GROUPS))
+        threshold = 0.7 * jnp.sqrt(jnp.sum(totals, axis=0, keepdims=True) * (1.0 / GROUPS))
         return jnp.maximum(0.0, 1.0 - threshold / jnp.sqrt(totals + 1e-12))
 
-    f_row = factor(step * step * rr)
-    f_col = column(f_row, GROUPS)
-    ci = lax.broadcasted_iota(jnp.int32, (GROUPS, wide), 1)
-    gi = lax.broadcasted_iota(jnp.int32, (GROUPS, wide), 0)
-    block = (ci >= gi * GROUPS) & (ci < gi * GROUPS + GROUPS)
-    first_col = jnp.sum(jnp.where(block, gi * GROUPS, 0), axis=0, keepdims=True)
-    tiled = jnp.sum(jnp.where(ci - first_col == gi, f_col, 0.0), axis=0, keepdims=True)
-    dd = jnp.sum(quad * f_col, axis=0, keepdims=True) * tiled
-    rd = cross * tiled
-    dd_col = jnp.sum(jnp.where(block, dd, 0.0), axis=1, keepdims=True)
-    rd_col = jnp.sum(jnp.where(block, rd, 0.0), axis=1, keepdims=True)
+    squares = total[:, first + GROUPS : first + GROUPS + 1]
+    f_col = factor(step * step * squares)
+    col = lax.broadcasted_iota(jnp.int32, (GROUPS, WIDTH), 1)
+    group = lax.broadcasted_iota(jnp.int32, (GROUPS, WIDTH), 0)
+    shift = jnp.zeros((GROUPS, WIDTH), jnp.int32)
+    for k in range(1, HALF + 1):
+        shift = jnp.where(col >= k * GROUPS, k, shift)
+    one = col - shift * GROUPS
+    two = one + shift
+    two = jnp.where(two >= GROUPS, two - GROUPS, two)
+    f_one = jnp.sum(jnp.where(group == one, f_col, 0.0), axis=0, keepdims=True)
+    f_two = jnp.sum(jnp.where(group == two, f_col, 0.0), axis=0, keepdims=True)
+    col, shift = col[:1], shift[:1]
+    twice = jnp.where((shift == 0) | (shift == HALF - 1), 1.0, 2.0)
+    pairs = jnp.where(col < first, twice * f_one * f_two, 0.0)
+    singles = jnp.where((col >= first) & (col < first + GROUPS), f_one, 0.0)
+    quad = jnp.sum(total * pairs, axis=1, keepdims=True)
+    cross = jnp.sum(total * singles, axis=1, keepdims=True)
     grow = 1.0 + f_col
-    rr_col = column(rr, GROUPS)
-    two_col = (step * step) * (grow * grow * rr_col - 2.0 * step * grow * rd_col + step * step * dd_col)
-    two_col = jnp.maximum(two_col, 0.0)
-    threshold = 0.7 * jnp.sqrt(jnp.sum(two_col, axis=0, keepdims=True) * (1.0 / GROUPS))
-    f2_col = jnp.maximum(0.0, 1.0 - threshold / jnp.sqrt(two_col + 1e-12))
-    g2 = lax.broadcasted_iota(jnp.int32, (GROUPS, TERMS), 0)
-    onehot = g2 == grp[...]
+    totals = grow * grow * squares - 2.0 * step * grow * cross + step * step * quad
+    f2_col = factor(jnp.maximum(step * step * totals, 0.0))
+    term_group = lax.broadcasted_iota(jnp.int32, (GROUPS, TERMS), 0)
+    onehot = term_group == grp[...]
     f_term = jnp.sum(jnp.where(onehot, f_col, 0.0), axis=0, keepdims=True)
     f2_term = jnp.sum(jnp.where(onehot, f2_col, 0.0), axis=0, keepdims=True)
     seconds = []
@@ -322,18 +342,17 @@
 
 
 def body(fields, library, centers_x, centers_y, centers_t, groups):
-    pgroup, rows = fields.shape[0], fields.shape[3]
+    pgroup = fields.shape[0]
     shares = lax.axis_size("term")
     local = library.shape[0]
+    library = library.T
     if pgroup != shares or local * shares != TERMS:
         raise ValueError("unexpected split")
-    me = lax.axis_index("term")
     libs = [library]
     for k in range(1, shares):
         libs.append(lax.ppermute(library, "term", [((i + k) % shares, i) for i in range(shares)]))
-    where = jnp.stack([me, lax.axis_index("space") * rows]).astype(jnp.int32)
-    flat = integrals(where, centers_x, centers_y, centers_t, fields)
-    own = pick(where, libs, flat)
+    flat = integrals(centers_x, centers_y, centers_t, fields)
+    own = pick(libs, flat)
     spaces = lax.axis_size("space")
     others = [
         lax.ppermute(own, "space", [((i + k) % spaces, i) for i in range(spaces)])
@@ -341,14 +360,14 @@
     ]
     grp = groups.reshape(1, TERMS)
     payload, normal, dmat = fit(own, sum(others[1:], others[0]), grp)
-    row = lax.broadcasted_iota(jnp.int32, payload.shape, 0)
+    col = lax.broadcasted_iota(jnp.int32, payload.shape, 1)
     params = lax.axis_size("param")
     pieces = [payload]
     for k in range(1, shares):
         pieces.append(lax.ppermute(payload, "term", [((i + k) % shares, i) for i in range(shares)]))
     total = sum(pieces[1:], pieces[0])
     largest = functools.reduce(jnp.maximum, pieces)
-    payload = jnp.where(row == 31, largest, total)
+    payload = jnp.where(col == WIDTH - 1, largest, total)
     pieces = [payload]
     for k in range(1, params):
         pieces.append(lax.ppermute(payload, "param", [((i + k) % params, i) for i in range(params)]))

time: 59.2 us -> 39.7 us (0.67)
  Pallas kernels: 25.5 us -> 12.9 us
  local copies, waits for them, and re-layouts: 4.34 us -> 0.01 us
  waiting for transfers between devices: 14.6 us -> 12.2 us
    pallas_call x2, Pallas kernels: 16.3 us -> 3.52 us  [the longest x1 2.24 us: pick(): pl.pallas_call(functools.partial(pick_kernel, libs[0].shape[1], shares),...]
    unnamed x11 -> x4, local copies, waits for them, and re-layouts: 4.34 us -> 0.01 us
    ppermute x3, waiting for transfers between devices: 7.71 us -> 5.75 us  [body(): lax.ppermute(payload, 'term', [((i + k) % shares, i) for i in range(share...]
  transfers between devices with their start and end apart: 10 -> 10, of which waited for: 6 -> 7; matrix products, arithmetic and copies ran while one was open for 0% -> 0% of each run, Pallas kernels for 14% -> 21%
where the time goes in v2:
time: 39.7 us; the launch traced here: 39.5 us
  starting transfers between devices  13.7 us (35%)
  Pallas kernels  12.9 us (32%)
  waiting for transfers between devices  12.2 us (31%)
  between operations  0.71 us (2%)
    pallas_call x1, Pallas kernels, integrals(): pl.pallas_call(functools.partial(integrals_kernel, rows), out_shape=jax.S...  8.25 us
    ppermute x3, starting transfers between devices, body(): lax.ppermute(library, 'term', [((i + k) % shares, i) for i in range(share...  6.11 us
    ppermute x3, waiting for transfers between devices, body(): lax.ppermute(payload, 'term', [((i + k) % shares, i) for i in range(share...  5.75 us
    ppermute x3, waiting for transfers between devices, body(): lax.ppermute(payload, 'param', [((i + k) % params, i) for i in range(para...  4.26 us
    ppermute x3, starting transfers between devices, body(): lax.ppermute(payload, 'term', [((i + k) % shares, i) for i in range(share...  4 us
    ppermute x3, starting transfers between devices, body(): lax.ppermute(payload, 'param', [((i + k) % params, i) for i in range(para...  3.6 us
    pallas_call x1, Pallas kernels, pick(): pl.pallas_call(functools.partial(pick_kernel, libs[0].shape[1], shares),...  2.24 us
    ppermute x1, waiting for transfers between devices, body(): lax.ppermute(own, 'space', [((i + k) % spaces, i) for i in range(spaces)])  2.18 us
  transfers between devices with their start and end apart: 10, of which 7 were waited for; matrix products, arithmetic and copies ran while one was open for 0% of the time, Pallas kernels for 21%

profile of v2, /device:TPU:0, one launch (start us, length us, event | category | flops | bytes accessed | tf_op | source)
XLA Modules:
  0.0 39.5 jit_solution(16858027902808642631)
XLA Ops:
  0.6 0.0 copy-start.1
  0.6 5.1 %collective-permute-start = (s32[4,42]{1,0:T(4,128)}, s32[4,42]{1,0:T(4,128)S(1)}, u32[]{:S(2)}, u32[]{:S(2)}) collective-permute-start(s32[4,42]{1,0:T(4,128)} %bitcast.4), channel_id=1, source_target_pairs={{1,0},{2,1},{3,2},{0,3},{5,4},{6,5},{7,6},{4,7},{9,8},{10,9},{11,1... | collective-permute-start | bytes 2024 | tf_op jit(solution)/shard_map/ppermute | solution.py:353
  5.7 0.0 collective-permute-start.1
  5.7 1.0 %collective-permute-start.2 = (s32[4,42]{1,0:T(4,128)}, s32[4,42]{1,0:T(4,128)S(1)}, u32[]{:S(2)}, u32[]{:S(2)}) collective-permute-start(s32[4,42]{1,0:T(4,128)} %bitcast.6), channel_id=1, source_target_pairs={{3,0},{0,1},{1,2},{2,3},{7,4},{4,5},{5,6},{6,7},{11,8},{8,9},{9,10... | collective-permute-start | bytes 2024 | tf_op jit(solution)/shard_map/ppermute | solution.py:353
  6.8 8.2 %integrals.1.refs_4_ = f32[2,2352,128]{2,1,0:T(8,128)S(1)} custom-call(s32[16]{0:T(128)} %centers_x.1, s32[16]{0:T(128)} %centers_y.1, s32[4]{0:T(128)} %centers_t.1, f32[4,2,8,64,128]{4,3,2,1,0:T(8,128)} %fields.1), custom_call_target="tpu_custom_call" | custom-call | flops 10000000000 | bytes 3000000 | tf_op jit(solution)/shard_map/integrals/pallas_call | solution.py:145
  15.0 0.0 copy-start
  15.0 0.0 collective-permute-done.refs_1_
  15.0 0.0 collective-permute-done.1.refs_2_
  15.0 0.0 collective-permute-done.2.refs_3_
  15.1 0.0 copy-done.1
  15.1 2.2 %pick.1.own = f32[1408,128]{1,0:T(8,128)S(1)} custom-call(s32[4,42]{1,0:T(4,128)S(1)} %bitcast.7, s32[4,42]{1,0:T(4,128)S(1)} %collective-permute-done.refs_1_, s32[4,42]{1,0:T(4,128)S(1)} %collective-permute-done.1.refs_2_, s32[4,42]{1,0:T(4,128)S(1)} %collective-permute-done.2.refs_3_, f32[2,2352,128]{2,1,0:T(8,128)S(1)} %integrals.1.refs_4_), custom_call_target="tpu_custom_call" | custom-call | tf_op jit(solution)/shard_map/pick/pallas_call | solution.py:208
  17.3 0.0 collective-permute-start.3
  17.3 2.2 %collective-permute-done.3.other = f32[1408,128]{1,0:T(8,128)S(1)} collective-permute-done((f32[1408,128]{1,0:T(8,128)S(1)}, f32[1408,128]{1,0:T(8,128)S(1)}, u32[]{:S(2)}, u32[]{:S(2)}) %collective-permute-start.3) | collective-permute-done | bytes 720928 | tf_op jit(solution)/shard_map/ppermute | solution.py:358
  19.5 0.0 copy-done
  19.5 1.3 %fit.1 = (f32[24,384]{1,0:T(8,128)S(1)}, f32[176,168]{1,0:T(8,128)S(1)}, f32[48,168]{1,0:T(8,128)S(1)}) custom-call(f32[1408,128]{1,0:T(8,128)S(1)} %pick.1.own, f32[1408,128]{1,0:T(8,128)S(1)} %collective-permute-done.3.other, s32[1,168]{1,0:T(1,128)S(1)} %bitcast.2), custom_call_target="tpu_custom_call" | custom-call | tf_op jit(solution)/shard_map/fit/pallas_call | solution.py:265
  20.8 2.9 %collective-permute-start.4 = (f32[24,384]{1,0:T(8,128)S(1)}, f32[24,384]{1,0:T(8,128)S(1)}, u32[]{:S(2)}, u32[]{:S(2)}) collective-permute-start(f32[24,384]{1,0:T(8,128)S(1)} %get-tuple-element.7), channel_id=1, source_target_pairs={{1,0},{2,1},{3,2},{0,3},{5,4},{6,5},{7,6},{4,7},{9,8},{10,9},{11,1... | collective-permute-start | bytes 110600 | tf_op jit(solution)/shard_map/ppermute | solution.py:367
  23.7 1.1 %collective-permute-start.5 = (f32[24,384]{1,0:T(8,128)S(1)}, f32[24,384]{1,0:T(8,128)S(1)}, u32[]{:S(2)}, u32[]{:S(2)}) collective-permute-start(f32[24,384]{1,0:T(8,128)S(1)} %get-tuple-element.7), channel_id=1, source_target_pairs={{2,0},{3,1},{0,2},{1,3},{6,4},{7,5},{4,6},{5,7},{10,8},{11,9},{8,1... | collective-permute-start | bytes 110600 | tf_op jit(solution)/shard_map/ppermute | solution.py:367
  24.8 0.0 collective-permute-start.6
  24.8 0.7 %collective-permute-done.4 = f32[24,384]{1,0:T(8,128)S(1)} collective-permute-done((f32[24,384]{1,0:T(8,128)S(1)}, f32[24,384]{1,0:T(8,128)S(1)}, u32[]{:S(2)}, u32[]{:S(2)}) %collective-permute-start.4) | collective-permute-done | bytes 36896 | tf_op jit(solution)/shard_map/ppermute | solution.py:367
  25.5 3.0 %collective-permute-done.5 = f32[24,384]{1,0:T(8,128)S(1)} collective-permute-done((f32[24,384]{1,0:T(8,128)S(1)}, f32[24,384]{1,0:T(8,128)S(1)}, u32[]{:S(2)}, u32[]{:S(2)}) %collective-permute-start.5) | collective-permute-done | bytes 36896 | tf_op jit(solution)/shard_map/ppermute | solution.py:367
  28.5 2.0 %collective-permute-done.6 = f32[24,384]{1,0:T(8,128)S(1)} collective-permute-done((f32[24,384]{1,0:T(8,128)S(1)}, f32[24,384]{1,0:T(8,128)S(1)}, u32[]{:S(2)}, u32[]{:S(2)}) %collective-permute-start.6) | collective-permute-done | bytes 36896 | tf_op jit(solution)/shard_map/ppermute | solution.py:367
  30.6 2.5 %collective-permute-start.7 = (f32[24,384]{1,0:T(8,128)S(1)}, f32[24,384]{1,0:T(8,128)S(1)}, u32[]{:S(2)}, u32[]{:S(2)}) collective-permute-start(f32[24,384]{1,0:T(8,128)S(1)} %add_select_fusion.refs_0_), channel_id=1, source_target_pairs={{8,0},{16,8},{24,16},{0,24},{9,1},{17,9},{25,17},{1,25},{10,2},{18... | collective-permute-start | bytes 110600 | tf_op jit(solution)/shard_map/ppermute | solution.py:373
  33.1 0.5 %collective-permute-start.8 = (f32[24,384]{1,0:T(8,128)S(1)}, f32[24,384]{1,0:T(8,128)S(1)}, u32[]{:S(2)}, u32[]{:S(2)}) collective-permute-start(f32[24,384]{1,0:T(8,128)S(1)} %add_select_fusion.refs_0_), channel_id=1, source_target_pairs={{16,0},{24,8},{0,16},{8,24},{17,1},{25,9},{1,17},{9,25},{18,2},{26... | collective-permute-start | bytes 110600 | tf_op jit(solution)/shard_map/ppermute | solution.py:373
  33.6 0.6 %collective-permute-start.9 = (f32[24,384]{1,0:T(8,128)S(1)}, f32[24,384]{1,0:T(8,128)S(1)}, u32[]{:S(2)}, u32[]{:S(2)}) collective-permute-start(f32[24,384]{1,0:T(8,128)S(1)} %add_select_fusion.refs_0_), channel_id=1, source_target_pairs={{24,0},{0,8},{8,16},{16,24},{25,1},{1,9},{9,17},{17,25},{26,2},{2,... | collective-permute-start | bytes 110600 | tf_op jit(solution)/shard_map/ppermute | solution.py:373
  34.2 0.5 %collective-permute-done.7.refs_1_ = f32[24,384]{1,0:T(8,128)S(1)} collective-permute-done((f32[24,384]{1,0:T(8,128)S(1)}, f32[24,384]{1,0:T(8,128)S(1)}, u32[]{:S(2)}, u32[]{:S(2)}) %collective-permute-start.7) | collective-permute-done | bytes 36896 | tf_op jit(solution)/shard_map/ppermute | solution.py:373
  34.7 2.3 %collective-permute-done.8.refs_2_ = f32[24,384]{1,0:T(8,128)S(1)} collective-permute-done((f32[24,384]{1,0:T(8,128)S(1)}, f32[24,384]{1,0:T(8,128)S(1)}, u32[]{:S(2)}, u32[]{:S(2)}) %collective-permute-start.8) | collective-permute-done | bytes 36896 | tf_op jit(solution)/shard_map/ppermute | solution.py:373
  37.0 1.4 %collective-permute-done.9.refs_3_ = f32[24,384]{1,0:T(8,128)S(1)} collective-permute-done((f32[24,384]{1,0:T(8,128)S(1)}, f32[24,384]{1,0:T(8,128)S(1)}, u32[]{:S(2)}, u32[]{:S(2)}) %collective-permute-start.9) | collective-permute-done | bytes 36896 | tf_op jit(solution)/shard_map/ppermute | solution.py:373
  38.4 1.1 %finish.1 = (f32[1,2,168]{2,1,0:T(2,128)}, f32[1,2,168]{2,1,0:T(2,128)}) custom-call(s32[1,168]{1,0:T(1,128)S(1)} %bitcast.3, f32[176,168]{1,0:T(8,128)S(1)} %get-tuple-element.5.normal, f32[48,168]{1,0:T(8,128)S(1)} %get-tuple-element.6.dmat, f32[24,384]{1,0:T(8,128)S(1)} %add_select_fusion.refs_0_, f32[24,384]{1,0:T(8,128)S(1)} %collective-permute-done.7.refs_1_, ...), custom_call_target="tpu_custom_call" | custom-call | tf_op jit(solution)/shard_map/finish/pallas_call | solution.py:334
  (2 shorter events, 0.0 us)
Async XLA Ops:
  0.6 14.4 %copy-start.1 = (s32[42,4]{0,1:T(4,128)S(1)}, s32[42,4]{0,1:T(4,128)}, u32[]{:S(2)}) copy-start(s32[42,4]{0,1:T(4,128)} %param.7) | copy-start | bytes 2020
  0.6 14.4 %collective-permute-start = (s32[4,42]{1,0:T(4,128)}, s32[4,42]{1,0:T(4,128)S(1)}, u32[]{:S(2)}, u32[]{:S(2)}) collective-permute-start(s32[4,42]{1,0:T(4,128)} %bitcast.4), channel_id=1, source_target_pairs={{1,0},{2,1},{3,2},{0,3},{5,4},{6,5},{7,6},{4,7},{9,8},{10,9},{11,1... | collective-permute-start | bytes 2024 | tf_op jit(solution)/shard_map/ppermute | solution.py:353
  5.7 9.3 %collective-permute-start.1 = (s32[4,42]{1,0:T(4,128)}, s32[4,42]{1,0:T(4,128)S(1)}, u32[]{:S(2)}, u32[]{:S(2)}) collective-permute-start(s32[4,42]{1,0:T(4,128)} %bitcast.5), channel_id=1, source_target_pairs={{2,0},{3,1},{0,2},{1,3},{6,4},{7,5},{4,6},{5,7},{10,8},{11,9},{8,1... | collective-permute-start | bytes 2024 | tf_op jit(solution)/shard_map/ppermute | solution.py:353
  5.7 9.3 %collective-permute-start.2 = (s32[4,42]{1,0:T(4,128)}, s32[4,42]{1,0:T(4,128)S(1)}, u32[]{:S(2)}, u32[]{:S(2)}) collective-permute-start(s32[4,42]{1,0:T(4,128)} %bitcast.6), channel_id=1, source_target_pairs={{3,0},{0,1},{1,2},{2,3},{7,4},{4,5},{5,6},{6,7},{11,8},{8,9},{9,10... | collective-permute-start | bytes 2024 | tf_op jit(solution)/shard_map/ppermute | solution.py:353
  15.0 4.5 %copy-start = (s32[168]{0:T(256)S(1)}, s32[168]{0:T(256)}, u32[]{:S(2)}) copy-start(s32[168]{0:T(256)} %param.11) | copy-start | bytes 2020
  17.3 2.2 %collective-permute-start.3 = (f32[1408,128]{1,0:T(8,128)S(1)}, f32[1408,128]{1,0:T(8,128)S(1)}, u32[]{:S(2)}, u32[]{:S(2)}) collective-permute-start(f32[1408,128]{1,0:T(8,128)S(1)} %pick.1.own), channel_id=1, source_target_pairs={{4,0},{0,4},{5,1},{1,5},{6,2},{2,6},{7,3},{3,7},{12,8},{8,12},{13,... | collective-permute-start | bytes 2162696 | tf_op jit(solution)/shard_map/ppermute | solution.py:358
  20.8 4.7 %collective-permute-start.4 = (f32[24,384]{1,0:T(8,128)S(1)}, f32[24,384]{1,0:T(8,128)S(1)}, u32[]{:S(2)}, u32[]{:S(2)}) collective-permute-start(f32[24,384]{1,0:T(8,128)S(1)} %get-tuple-element.7), channel_id=1, source_target_pairs={{1,0},{2,1},{3,2},{0,3},{5,4},{6,5},{7,6},{4,7},{9,8},{10,9},{11,1... | collective-permute-start | bytes 110600 | tf_op jit(solution)/shard_map/ppermute | solution.py:367
  23.7 4.9 %collective-permute-start.5 = (f32[24,384]{1,0:T(8,128)S(1)}, f32[24,384]{1,0:T(8,128)S(1)}, u32[]{:S(2)}, u32[]{:S(2)}) collective-permute-start(f32[24,384]{1,0:T(8,128)S(1)} %get-tuple-element.7), channel_id=1, source_target_pairs={{2,0},{3,1},{0,2},{1,3},{6,4},{7,5},{4,6},{5,7},{10,8},{11,9},{8,1... | collective-permute-start | bytes 110600 | tf_op jit(solution)/shard_map/ppermute | solution.py:367
  24.8 5.8 %collective-permute-start.6 = (f32[24,384]{1,0:T(8,128)S(1)}, f32[24,384]{1,0:T(8,128)S(1)}, u32[]{:S(2)}, u32[]{:S(2)}) collective-permute-start(f32[24,384]{1,0:T(8,128)S(1)} %get-tuple-element.7), channel_id=1, source_target_pairs={{3,0},{0,1},{1,2},{2,3},{7,4},{4,5},{5,6},{6,7},{11,8},{8,9},{9,10... | collective-permute-start | bytes 110600 | tf_op jit(solution)/shard_map/ppermute | solution.py:367
  30.6 4.1 %collective-permute-start.7 = (f32[24,384]{1,0:T(8,128)S(1)}, f32[24,384]{1,0:T(8,128)S(1)}, u32[]{:S(2)}, u32[]{:S(2)}) collective-permute-start(f32[24,384]{1,0:T(8,128)S(1)} %add_select_fusion.refs_0_), channel_id=1, source_target_pairs={{8,0},{16,8},{24,16},{0,24},{9,1},{17,9},{25,17},{1,25},{10,2},{18... | collective-permute-start | bytes 110600 | tf_op jit(solution)/shard_map/ppermute | solution.py:373
  33.1 4.0 %collective-permute-start.8 = (f32[24,384]{1,0:T(8,128)S(1)}, f32[24,384]{1,0:T(8,128)S(1)}, u32[]{:S(2)}, u32[]{:S(2)}) collective-permute-start(f32[24,384]{1,0:T(8,128)S(1)} %add_select_fusion.refs_0_), channel_id=1, source_target_pairs={{16,0},{24,8},{0,16},{8,24},{17,1},{25,9},{1,17},{9,25},{18,2},{26... | collective-permute-start | bytes 110600 | tf_op jit(solution)/shard_map/ppermute | solution.py:373
  33.6 4.9 %collective-permute-start.9 = (f32[24,384]{1,0:T(8,128)S(1)}, f32[24,384]{1,0:T(8,128)S(1)}, u32[]{:S(2)}, u32[]{:S(2)}) collective-permute-start(f32[24,384]{1,0:T(8,128)S(1)} %add_select_fusion.refs_0_), channel_id=1, source_target_pairs={{24,0},{0,8},{8,16},{16,24},{25,1},{1,9},{9,17},{17,25},{26,2},{2,... | collective-permute-start | bytes 110600 | tf_op jit(solution)/shard_map/ppermute | solution.py:373

commit v3 on v2

--- a/solution.py
+++ b/solution.py
@@ -60,7 +60,7 @@
 
 def integrals_kernel(
     rows, centers_x, centers_y, centers_t, fields, out,
-    cx, cy, ct, pair, power_u, powers_v, y_split, tx_split, high, low, sem,
+    cx, cy, ct, pair, u_cells, power_u, powers_v, y_split, tx_split, high, low, sem,
 ):
     cells = NT * rows
     first_row = lax.axis_index("space") * rows
@@ -102,8 +102,9 @@
         for i, part in enumerate(split(x_table * weight)):
             tx_split[i, pl.ds(t * rows, rows), :] = part
     copy.wait()
-    power_u[...] = jnp.ones((cells, NY), f32)
-    v = pair[1].reshape(cells, NY)
+    power_u[...] = jnp.ones((NY, cells), f32)
+    u_cells[...] = pair[0].reshape(cells, NY).T
+    v = pair[1].reshape(cells, NY).T
     power = v
     powers_v[0] = v
     for b in range(1, POWERS - 1):
@@ -115,11 +116,11 @@
         for b in range(POWERS):
             for h in range(cells // tile):
                 part = pl.ds(h * tile, tile)
-                monomial = power_u[part, :]
+                monomial = power_u[:, part]
                 if b:
-                    monomial = monomial * powers_v[b - 1, part, :]
-                both = jnp.concatenate(split(monomial), axis=1)
-                across = dot(y_split[...], both, NT_DIMS)
+                    monomial = monomial * powers_v[b - 1, :, part]
+                both = jnp.concatenate(split(monomial), axis=0)
+                across = dot(y_split[...], both, NN_DIMS)
                 across_high, across_low = split(across[:ROWS] + across[ROWS:])
                 high[pl.ds(b * ROWS, ROWS), part] = across_high
                 low[pl.ds(b * ROWS, ROWS), part] = across_low
@@ -132,7 +133,7 @@
         place = pl.ds(pl.multiple_of(a * span, 8), span)
         out[0, place, :] = result[:, :128]
         out[1, place, :] = result[:, 128:]
-        power_u[...] = power_u[...] * pair[0].reshape(cells, NY)
+        power_u[...] = power_u[...] * u_cells[...]
         return 0
 
     lax.fori_loop(0, POWERS, one_power, 0)
@@ -152,8 +153,9 @@
             pltpu.SMEM((KY,), jnp.int32),
             pltpu.SMEM((KT,), jnp.int32),
             pltpu.VMEM((2, NT, rows, NY), f32),
-            pltpu.VMEM((cells, NY), f32),
-            pltpu.VMEM((POWERS - 1, cells, NY), f32),
+            pltpu.VMEM((NY, cells), f32),
+            pltpu.VMEM((NY, cells), f32),
+            pltpu.VMEM((POWERS - 1, NY, cells), f32),
             pltpu.VMEM((2 * ROWS, 2 * NY), bf16),
             pltpu.VMEM((2, cells, LANES), bf16),
             pltpu.VMEM((POWERS * ROWS, cells), bf16),
@@ -166,9 +168,8 @@
     )(*operands)
 
 
-def pick_kernel(local, shares, *refs):
-    libs = refs[:shares]
-    flat, out = refs[shares:]
+def pick_kernel(local, *refs):
+    *libs, flat, out = refs
     left = lax.broadcasted_iota(jnp.int32, (8, 128), 1) < 64
     me = lax.axis_index("term")
 
@@ -182,33 +183,26 @@
         odd_value = jnp.where(left, pltpu.roll(top, 64, 1), low)
         out[pl.ds(pl.multiple_of(j * 8, 8), 8), :] = jnp.where(odd, odd_value, even_value)
 
-    batch = max(n for n in range(1, 22) if local % n == 0)
-    for k in range(shares):
-        first = lax.rem(me + k, shares) * local
-        lib = libs[k]
-
-        def some(i, _):
-            loaded = [
-                load(*(lib[part, i * batch + n] for part in range(4))) for n in range(batch)
-            ]
-            for n in range(batch):
-                store(first + i * batch + n, *loaded[n])
-            return 0
-
-        lax.fori_loop(0, local // batch, some, 0)
+    done = 0
+    for lib in libs:
+        for k in range(lib.shape[0] // 4):
+            first = (me ^ done) * local
+            loaded = [load(*(lib[4 * k + part, n] for part in range(4))) for n in range(local)]
+            for n in range(local):
+                store(first + n, *loaded[n])
+            done += 1
     store(TERMS, *load(1, 0, 3, 0))
     store(TERMS + 1, *load(0, 1, 3, 0))
     out[pl.ds((TERMS + 2) * 8, 48), :] = jnp.zeros((48, 128), f32)
 
 
 def pick(libs, flat):
-    shares = len(libs)
     smem = pl.BlockSpec(memory_space=pltpu.SMEM)
     vmem = pl.BlockSpec(memory_space=pltpu.VMEM)
     return pl.pallas_call(
-        functools.partial(pick_kernel, libs[0].shape[1], shares),
+        functools.partial(pick_kernel, libs[0].shape[1]),
         out_shape=jax.ShapeDtypeStruct(((TERMS + 8) * 8, 128), f32),
-        in_specs=[smem] * shares + [vmem],
+        in_specs=[smem] * len(libs) + [vmem],
         out_specs=vmem,
         compiler_params=pltpu.CompilerParams(vmem_limit_bytes=VMEM_LIMIT),
         name="pick",
@@ -341,36 +335,44 @@
     )(grp, normal, dmat, *pieces)
 
 
+def partner(index, k, size):
+    return index ^ k if size & (size - 1) == 0 else (index + k) % size
+
+
+def neighbour_last(size):
+    return (*range(2, size), 1) if size > 1 else ()
+
+
+def exchange(value, axis, k):
+    size = lax.axis_size(axis)
+    return lax.ppermute(value, axis, [(partner(i, k, size), i) for i in range(size)])
+
+
 def body(fields, library, centers_x, centers_y, centers_t, groups):
     pgroup = fields.shape[0]
     shares = lax.axis_size("term")
     local = library.shape[0]
     library = library.T
-    if pgroup != shares or local * shares != TERMS:
+    if pgroup != shares or local * shares != TERMS or shares & (shares - 1):
         raise ValueError("unexpected split")
-    libs = [library]
-    for k in range(1, shares):
-        libs.append(lax.ppermute(library, "term", [((i + k) % shares, i) for i in range(shares)]))
+    libs = [library] + [exchange(library, "term", k) for k in range(1, shares)]
     flat = integrals(centers_x, centers_y, centers_t, fields)
     own = pick(libs, flat)
     spaces = lax.axis_size("space")
-    others = [
-        lax.ppermute(own, "space", [((i + k) % spaces, i) for i in range(spaces)])
-        for k in range(1, spaces)
-    ]
+    others = [exchange(own, "space", k) for k in range(1, spaces)]
     grp = groups.reshape(1, TERMS)
     payload, normal, dmat = fit(own, sum(others[1:], others[0]), grp)
     col = lax.broadcasted_iota(jnp.int32, payload.shape, 1)
     params = lax.axis_size("param")
     pieces = [payload]
-    for k in range(1, shares):
-        pieces.append(lax.ppermute(payload, "term", [((i + k) % shares, i) for i in range(shares)]))
+    for k in neighbour_last(shares):
+        pieces.append(exchange(payload, "term", k))
     total = sum(pieces[1:], pieces[0])
     largest = functools.reduce(jnp.maximum, pieces)
     payload = jnp.where(col == WIDTH - 1, largest, total)
     pieces = [payload]
-    for k in range(1, params):
-        pieces.append(lax.ppermute(payload, "param", [((i + k) % params, i) for i in range(params)]))
+    for k in neighbour_last(params):
+        pieces.append(exchange(payload, "param", k))
     return end(grp, normal, dmat, pieces)
 
 

time: 39.7 us -> 35.1 us (0.88)
  waiting for transfers between devices: 12.2 us -> 9.27 us
  Pallas kernels: 12.9 us -> 11.2 us
    ppermute x10, waiting for transfers between devices: 12.2 us -> 9.27 us  [exchange(): lax.ppermute(value, axis, [(partner(i, k, size), i) for i in range(size)])]
    pallas_call x1, Pallas kernels: 8.25 us -> 7.3 us  [integrals(): pl.pallas_call(functools.partial(integrals_kernel, rows), out_shape=jax.S...]
    pallas_call x1, Pallas kernels: 2.24 us -> 1.49 us  [pick(): pl.pallas_call(functools.partial(pick_kernel, libs[0].shape[1]), out_shap...]
where the time goes in v3:
time: 35.1 us; the launch traced here: 34.9 us
  starting transfers between devices  13.8 us (39%)
  Pallas kernels  11.2 us (32%)
  waiting for transfers between devices  9.27 us (26%)
  between operations  0.71 us (2%)
    ppermute x10, starting transfers between devices, exchange(): lax.ppermute(value, axis, [(partner(i, k, size), i) for i in range(size)])  13.8 us
    ppermute x10, waiting for transfers between devices, exchange(): lax.ppermute(value, axis, [(partner(i, k, size), i) for i in range(size)])  9.27 us
    pallas_call x1, Pallas kernels, integrals(): pl.pallas_call(functools.partial(integrals_kernel, rows), out_shape=jax.S...  7.3 us
    pallas_call x1, Pallas kernels, pick(): pl.pallas_call(functools.partial(pick_kernel, libs[0].shape[1]), out_shap...  1.49 us
    pallas_call x1, Pallas kernels, fit(): pl.pallas_call(fit_kernel, out_shape=(jax.ShapeDtypeStruct((GROUPS, WIDTH...  1.28 us
    pallas_call x1, Pallas kernels, end(): pl.pallas_call(functools.partial(end_kernel, len(pieces)), out_shape=(sha...  1.1 us
  transfers between devices with their start and end apart: 10, of which 7 were waited for; matrix products, arithmetic and copies ran while one was open for 0% of the time, Pallas kernels for 21%

profile of v3, /device:TPU:0, one launch (start us, length us, event | category | flops | bytes accessed | tf_op | source)
XLA Modules:
  0.0 34.9 jit_solution(10079913392438093694)
XLA Ops:
  0.6 0.0 copy-start.1
  0.6 3.1 %collective-permute-start = (s32[4,42]{1,0:T(4,128)}, s32[4,42]{1,0:T(4,128)S(1)}, u32[]{:S(2)}, u32[]{:S(2)}) collective-permute-start(s32[4,42]{1,0:T(4,128)} %bitcast.4), channel_id=1, source_target_pairs={{1,0},{0,1},{3,2},{2,3},{5,4},{4,5},{7,6},{6,7},{9,8},{8,9},{11,10... | collective-permute-start | bytes 2024 | tf_op jit(solution)/shard_map/ppermute | solution.py:348
  3.7 2.6 %collective-permute-start.1 = (s32[4,42]{1,0:T(4,128)}, s32[4,42]{1,0:T(4,128)S(1)}, u32[]{:S(2)}, u32[]{:S(2)}) collective-permute-start(s32[4,42]{1,0:T(4,128)} %bitcast.5), channel_id=1, source_target_pairs={{2,0},{3,1},{0,2},{1,3},{6,4},{7,5},{4,6},{5,7},{10,8},{11,9},{8,1... | collective-permute-start | bytes 2024 | tf_op jit(solution)/shard_map/ppermute | solution.py:348
  6.3 0.0 collective-permute-start.2
  6.3 7.3 %integrals.1.refs_4_ = f32[2,2352,128]{2,1,0:T(8,128)S(1)} custom-call(s32[16]{0:T(128)} %centers_x.1, s32[16]{0:T(128)} %centers_y.1, s32[4]{0:T(128)} %centers_t.1, f32[4,2,8,64,128]{4,3,2,1,0:T(8,128)} %fields.1), custom_call_target="tpu_custom_call" | custom-call | flops 10000000000 | bytes 3000000 | tf_op jit(solution)/shard_map/integrals/pallas_call | solution.py:146
  13.6 0.0 copy-start
  13.6 0.0 collective-permute-done.refs_1_
  13.7 0.0 collective-permute-done.1.refs_2_
  13.7 0.0 collective-permute-done.2.refs_3_
  13.7 0.0 copy-done.1
  13.7 1.5 %pick.1.own = f32[1408,128]{1,0:T(8,128)S(1)} custom-call(s32[4,42]{1,0:T(4,128)S(1)} %bitcast.7, s32[4,42]{1,0:T(4,128)S(1)} %collective-permute-done.refs_1_, s32[4,42]{1,0:T(4,128)S(1)} %collective-permute-done.1.refs_2_, s32[4,42]{1,0:T(4,128)S(1)} %collective-permute-done.2.refs_3_, f32[2,2352,128]{2,1,0:T(8,128)S(1)} %integrals.1.refs_4_), custom_call_target="tpu_custom_call" | custom-call | tf_op jit(solution)/shard_map/pick/pallas_call | solution.py:202
  15.2 0.1 collective-permute-start.3
  15.2 2.2 %collective-permute-done.3.other = f32[1408,128]{1,0:T(8,128)S(1)} collective-permute-done((f32[1408,128]{1,0:T(8,128)S(1)}, f32[1408,128]{1,0:T(8,128)S(1)}, u32[]{:S(2)}, u32[]{:S(2)}) %collective-permute-start.3) | collective-permute-done | bytes 720928 | tf_op jit(solution)/shard_map/ppermute | solution.py:348
  17.4 0.0 copy-done
  17.4 1.3 %fit.1 = (f32[24,384]{1,0:T(8,128)S(1)}, f32[176,168]{1,0:T(8,128)S(1)}, f32[48,168]{1,0:T(8,128)S(1)}) custom-call(f32[1408,128]{1,0:T(8,128)S(1)} %pick.1.own, f32[1408,128]{1,0:T(8,128)S(1)} %collective-permute-done.3.other, s32[1,168]{1,0:T(1,128)S(1)} %bitcast.2), custom_call_target="tpu_custom_call" | custom-call | tf_op jit(solution)/shard_map/fit/pallas_call | solution.py:259
  18.7 2.0 %collective-permute-start.4 = (f32[24,384]{1,0:T(8,128)S(1)}, f32[24,384]{1,0:T(8,128)S(1)}, u32[]{:S(2)}, u32[]{:S(2)}) collective-permute-start(f32[24,384]{1,0:T(8,128)S(1)} %get-tuple-element.7), channel_id=1, source_target_pairs={{2,0},{3,1},{0,2},{1,3},{6,4},{7,5},{4,6},{5,7},{10,8},{11,9},{8,1... | collective-permute-start | bytes 110600 | tf_op jit(solution)/shard_map/ppermute | solution.py:348
  20.7 2.0 %collective-permute-start.5 = (f32[24,384]{1,0:T(8,128)S(1)}, f32[24,384]{1,0:T(8,128)S(1)}, u32[]{:S(2)}, u32[]{:S(2)}) collective-permute-start(f32[24,384]{1,0:T(8,128)S(1)} %get-tuple-element.7), channel_id=1, source_target_pairs={{3,0},{2,1},{1,2},{0,3},{7,4},{6,5},{5,6},{4,7},{11,8},{10,9},{9,1... | collective-permute-start | bytes 110600 | tf_op jit(solution)/shard_map/ppermute | solution.py:348
  22.7 0.5 %collective-permute-start.6 = (f32[24,384]{1,0:T(8,128)S(1)}, f32[24,384]{1,0:T(8,128)S(1)}, u32[]{:S(2)}, u32[]{:S(2)}) collective-permute-start(f32[24,384]{1,0:T(8,128)S(1)} %get-tuple-element.7), channel_id=1, source_target_pairs={{1,0},{0,1},{3,2},{2,3},{5,4},{4,5},{7,6},{6,7},{9,8},{8,9},{11,10... | collective-permute-start | bytes 110600 | tf_op jit(solution)/shard_map/ppermute | solution.py:348
  23.2 0.5 %collective-permute-done.4 = f32[24,384]{1,0:T(8,128)S(1)} collective-permute-done((f32[24,384]{1,0:T(8,128)S(1)}, f32[24,384]{1,0:T(8,128)S(1)}, u32[]{:S(2)}, u32[]{:S(2)}) %collective-permute-start.4) | collective-permute-done | bytes 36896 | tf_op jit(solution)/shard_map/ppermute | solution.py:348
  23.7 3.0 %collective-permute-done.5 = f32[24,384]{1,0:T(8,128)S(1)} collective-permute-done((f32[24,384]{1,0:T(8,128)S(1)}, f32[24,384]{1,0:T(8,128)S(1)}, u32[]{:S(2)}, u32[]{:S(2)}) %collective-permute-start.5) | collective-permute-done | bytes 36896 | tf_op jit(solution)/shard_map/ppermute | solution.py:348
  26.7 0.2 collective-permute-done.6
  26.9 1.6 %collective-permute-start.7 = (f32[24,384]{1,0:T(8,128)S(1)}, f32[24,384]{1,0:T(8,128)S(1)}, u32[]{:S(2)}, u32[]{:S(2)}) collective-permute-start(f32[24,384]{1,0:T(8,128)S(1)} %add_select_fusion.refs_0_), channel_id=1, source_target_pairs={{16,0},{24,8},{0,16},{8,24},{17,1},{25,9},{1,17},{9,25},{18,2},{26... | collective-permute-start | bytes 110600 | tf_op jit(solution)/shard_map/ppermute | solution.py:348
  28.5 1.4 %collective-permute-start.8 = (f32[24,384]{1,0:T(8,128)S(1)}, f32[24,384]{1,0:T(8,128)S(1)}, u32[]{:S(2)}, u32[]{:S(2)}) collective-permute-start(f32[24,384]{1,0:T(8,128)S(1)} %add_select_fusion.refs_0_), channel_id=1, source_target_pairs={{24,0},{16,8},{8,16},{0,24},{25,1},{17,9},{9,17},{1,25},{26,2},{18... | collective-permute-start | bytes 110600 | tf_op jit(solution)/shard_map/ppermute | solution.py:348
  29.9 0.5 %collective-permute-start.9 = (f32[24,384]{1,0:T(8,128)S(1)}, f32[24,384]{1,0:T(8,128)S(1)}, u32[]{:S(2)}, u32[]{:S(2)}) collective-permute-start(f32[24,384]{1,0:T(8,128)S(1)} %add_select_fusion.refs_0_), channel_id=1, source_target_pairs={{8,0},{0,8},{24,16},{16,24},{9,1},{1,9},{25,17},{17,25},{10,2},{2,... | collective-permute-start | bytes 110600 | tf_op jit(solution)/shard_map/ppermute | solution.py:348
  30.4 0.7 %collective-permute-done.7.refs_1_ = f32[24,384]{1,0:T(8,128)S(1)} collective-permute-done((f32[24,384]{1,0:T(8,128)S(1)}, f32[24,384]{1,0:T(8,128)S(1)}, u32[]{:S(2)}, u32[]{:S(2)}) %collective-permute-start.7) | collective-permute-done | bytes 36896 | tf_op jit(solution)/shard_map/ppermute | solution.py:348
  31.2 2.1 %collective-permute-done.8.refs_2_ = f32[24,384]{1,0:T(8,128)S(1)} collective-permute-done((f32[24,384]{1,0:T(8,128)S(1)}, f32[24,384]{1,0:T(8,128)S(1)}, u32[]{:S(2)}, u32[]{:S(2)}) %collective-permute-start.8) | collective-permute-done | bytes 36896 | tf_op jit(solution)/shard_map/ppermute | solution.py:348
  33.3 0.5 %collective-permute-done.9.refs_3_ = f32[24,384]{1,0:T(8,128)S(1)} collective-permute-done((f32[24,384]{1,0:T(8,128)S(1)}, f32[24,384]{1,0:T(8,128)S(1)}, u32[]{:S(2)}, u32[]{:S(2)}) %collective-permute-start.9) | collective-permute-done | bytes 36896 | tf_op jit(solution)/shard_map/ppermute | solution.py:348
  33.8 1.1 %finish.1 = (f32[1,2,168]{2,1,0:T(2,128)}, f32[1,2,168]{2,1,0:T(2,128)}) custom-call(s32[1,168]{1,0:T(1,128)S(1)} %bitcast.3, f32[176,168]{1,0:T(8,128)S(1)} %get-tuple-element.5.normal, f32[48,168]{1,0:T(8,128)S(1)} %get-tuple-element.6.dmat, f32[24,384]{1,0:T(8,128)S(1)} %add_select_fusion.refs_0_, f32[24,384]{1,0:T(8,128)S(1)} %collective-permute-done.7.refs_1_, ...), custom_call_target="tpu_custom_call" | custom-call | tf_op jit(solution)/shard_map/finish/pallas_call | solution.py:328
  (2 shorter events, 0.0 us)
Async XLA Ops:
  0.6 13.0 %copy-start.1 = (s32[42,4]{0,1:T(4,128)S(1)}, s32[42,4]{0,1:T(4,128)}, u32[]{:S(2)}) copy-start(s32[42,4]{0,1:T(4,128)} %param.7) | copy-start | bytes 2020
  0.6 13.0 %collective-permute-start = (s32[4,42]{1,0:T(4,128)}, s32[4,42]{1,0:T(4,128)S(1)}, u32[]{:S(2)}, u32[]{:S(2)}) collective-permute-start(s32[4,42]{1,0:T(4,128)} %bitcast.4), channel_id=1, source_target_pairs={{1,0},{0,1},{3,2},{2,3},{5,4},{4,5},{7,6},{6,7},{9,8},{8,9},{11,10... | collective-permute-start | bytes 2024 | tf_op jit(solution)/shard_map/ppermute | solution.py:348
  3.7 9.9 %collective-permute-start.1 = (s32[4,42]{1,0:T(4,128)}, s32[4,42]{1,0:T(4,128)S(1)}, u32[]{:S(2)}, u32[]{:S(2)}) collective-permute-start(s32[4,42]{1,0:T(4,128)} %bitcast.5), channel_id=1, source_target_pairs={{2,0},{3,1},{0,2},{1,3},{6,4},{7,5},{4,6},{5,7},{10,8},{11,9},{8,1... | collective-permute-start | bytes 2024 | tf_op jit(solution)/shard_map/ppermute | solution.py:348
  6.3 7.3 %collective-permute-start.2 = (s32[4,42]{1,0:T(4,128)}, s32[4,42]{1,0:T(4,128)S(1)}, u32[]{:S(2)}, u32[]{:S(2)}) collective-permute-start(s32[4,42]{1,0:T(4,128)} %bitcast.6), channel_id=1, source_target_pairs={{3,0},{2,1},{1,2},{0,3},{7,4},{6,5},{5,6},{4,7},{11,8},{10,9},{9,1... | collective-permute-start | bytes 2024 | tf_op jit(solution)/shard_map/ppermute | solution.py:348
  13.6 3.8 %copy-start = (s32[168]{0:T(256)S(1)}, s32[168]{0:T(256)}, u32[]{:S(2)}) copy-start(s32[168]{0:T(256)} %param.11) | copy-start | bytes 2020
  15.2 2.3 %collective-permute-start.3 = (f32[1408,128]{1,0:T(8,128)S(1)}, f32[1408,128]{1,0:T(8,128)S(1)}, u32[]{:S(2)}, u32[]{:S(2)}) collective-permute-start(f32[1408,128]{1,0:T(8,128)S(1)} %pick.1.own), channel_id=1, source_target_pairs={{4,0},{0,4},{5,1},{1,5},{6,2},{2,6},{7,3},{3,7},{12,8},{8,12},{13,... | collective-permute-start | bytes 2162696 | tf_op jit(solution)/shard_map/ppermute | solution.py:348
  18.7 4.9 %collective-permute-start.4 = (f32[24,384]{1,0:T(8,128)S(1)}, f32[24,384]{1,0:T(8,128)S(1)}, u32[]{:S(2)}, u32[]{:S(2)}) collective-permute-start(f32[24,384]{1,0:T(8,128)S(1)} %get-tuple-element.7), channel_id=1, source_target_pairs={{2,0},{3,1},{0,2},{1,3},{6,4},{7,5},{4,6},{5,7},{10,8},{11,9},{8,1... | collective-permute-start | bytes 110600 | tf_op jit(solution)/shard_map/ppermute | solution.py:348
  20.7 6.0 %collective-permute-start.5 = (f32[24,384]{1,0:T(8,128)S(1)}, f32[24,384]{1,0:T(8,128)S(1)}, u32[]{:S(2)}, u32[]{:S(2)}) collective-permute-start(f32[24,384]{1,0:T(8,128)S(1)} %get-tuple-element.7), channel_id=1, source_target_pairs={{3,0},{2,1},{1,2},{0,3},{7,4},{6,5},{5,6},{4,7},{11,8},{10,9},{9,1... | collective-permute-start | bytes 110600 | tf_op jit(solution)/shard_map/ppermute | solution.py:348
  22.7 4.2 %collective-permute-start.6 = (f32[24,384]{1,0:T(8,128)S(1)}, f32[24,384]{1,0:T(8,128)S(1)}, u32[]{:S(2)}, u32[]{:S(2)}) collective-permute-start(f32[24,384]{1,0:T(8,128)S(1)} %get-tuple-element.7), channel_id=1, source_target_pairs={{1,0},{0,1},{3,2},{2,3},{5,4},{4,5},{7,6},{6,7},{9,8},{8,9},{11,10... | collective-permute-start | bytes 110600 | tf_op jit(solution)/shard_map/ppermute | solution.py:348
  26.9 4.3 %collective-permute-start.7 = (f32[24,384]{1,0:T(8,128)S(1)}, f32[24,384]{1,0:T(8,128)S(1)}, u32[]{:S(2)}, u32[]{:S(2)}) collective-permute-start(f32[24,384]{1,0:T(8,128)S(1)} %add_select_fusion.refs_0_), channel_id=1, source_target_pairs={{16,0},{24,8},{0,16},{8,24},{17,1},{25,9},{1,17},{9,25},{18,2},{26... | collective-permute-start | bytes 110600 | tf_op jit(solution)/shard_map/ppermute | solution.py:348
  28.5 4.9 %collective-permute-start.8 = (f32[24,384]{1,0:T(8,128)S(1)}, f32[24,384]{1,0:T(8,128)S(1)}, u32[]{:S(2)}, u32[]{:S(2)}) collective-permute-start(f32[24,384]{1,0:T(8,128)S(1)} %add_select_fusion.refs_0_), channel_id=1, source_target_pairs={{24,0},{16,8},{8,16},{0,24},{25,1},{17,9},{9,17},{1,25},{26,2},{18... | collective-permute-start | bytes 110600 | tf_op jit(solution)/shard_map/ppermute | solution.py:348
  29.9 4.0 %collective-permute-start.9 = (f32[24,384]{1,0:T(8,128)S(1)}, f32[24,384]{1,0:T(8,128)S(1)}, u32[]{:S(2)}, u32[]{:S(2)}) collective-permute-start(f32[24,384]{1,0:T(8,128)S(1)} %add_select_fusion.refs_0_), channel_id=1, source_target_pairs={{8,0},{0,8},{24,16},{16,24},{9,1},{1,9},{25,17},{17,25},{10,2},{2,... | collective-permute-start | bytes 110600 | tf_op jit(solution)/shard_map/ppermute | solution.py:348

commit v4 on v3

--- a/solution.py
+++ b/solution.py
@@ -102,41 +102,44 @@
         for i, part in enumerate(split(x_table * weight)):
             tx_split[i, pl.ds(t * rows, rows), :] = part
     copy.wait()
-    power_u[...] = jnp.ones((NY, cells), f32)
-    u_cells[...] = pair[0].reshape(cells, NY).T
+    u = pair[0].reshape(cells, NY).T
     v = pair[1].reshape(cells, NY).T
+    power_u[...] = u
+    u_cells[...] = u
     power = v
     powers_v[0] = v
     for b in range(1, POWERS - 1):
         power = power * v
         powers_v[b] = power
     tile = 256
-
-    def one_power(a, _):
+    span = POWERS * ROWS
+
+    def contract(a):
+        result = (
+            dot(high[a & 1], tx_split[0], NN_DIMS)
+            + dot(low[a & 1], tx_split[0], NN_DIMS)
+            + dot(high[a & 1], tx_split[1], NN_DIMS)
+        )
+        out[0, pl.ds(a * span, span), :] = result[:, :128]
+        out[1, pl.ds(a * span, span), :] = result[:, 128:]
+
+    for a in range(POWERS):
+        if a > 1:
+            power_u[...] = power_u[...] * u_cells[...]
         for b in range(POWERS):
             for h in range(cells // tile):
                 part = pl.ds(h * tile, tile)
-                monomial = power_u[:, part]
-                if b:
-                    monomial = monomial * powers_v[b - 1, :, part]
+                factors = ([power_u[:, part]] if a else []) + ([powers_v[b - 1, :, part]] if b else [])
+                monomial = factors[0] if factors else jnp.ones((NY, tile), f32)
+                if len(factors) > 1:
+                    monomial = monomial * factors[1]
                 both = jnp.concatenate(split(monomial), axis=0)
                 across = dot(y_split[...], both, NN_DIMS)
                 across_high, across_low = split(across[:ROWS] + across[ROWS:])
-                high[pl.ds(b * ROWS, ROWS), part] = across_high
-                low[pl.ds(b * ROWS, ROWS), part] = across_low
-        result = (
-            dot(high[...], tx_split[0], NN_DIMS)
-            + dot(low[...], tx_split[0], NN_DIMS)
-            + dot(high[...], tx_split[1], NN_DIMS)
-        )
-        span = POWERS * ROWS
-        place = pl.ds(pl.multiple_of(a * span, 8), span)
-        out[0, place, :] = result[:, :128]
-        out[1, place, :] = result[:, 128:]
-        power_u[...] = power_u[...] * u_cells[...]
-        return 0
-
-    lax.fori_loop(0, POWERS, one_power, 0)
+                high[a & 1, pl.ds( b * ROWS, ROWS), part] = across_high
+                low[a & 1, pl.ds( b * ROWS, ROWS), part] = across_low
+        if a: contract(a - 1)
+    contract(POWERS - 1)
 
 
 def integrals(cx, cy, ct, fields):
@@ -158,8 +161,8 @@
             pltpu.VMEM((POWERS - 1, NY, cells), f32),
             pltpu.VMEM((2 * ROWS, 2 * NY), bf16),
             pltpu.VMEM((2, cells, LANES), bf16),
-            pltpu.VMEM((POWERS * ROWS, cells), bf16),
-            pltpu.VMEM((POWERS * ROWS, cells), bf16),
+            pltpu.VMEM((2, POWERS * ROWS, cells), bf16),
+            pltpu.VMEM((2, POWERS * ROWS, cells), bf16),
             pltpu.SemaphoreType.DMA((4,)),
         ],
         compiler_params=pltpu.CompilerParams(vmem_limit_bytes=VMEM_LIMIT),

time: 35.1 us -> 33.2 us (0.946)
  Pallas kernels: 11.2 us -> 9.26 us
    pallas_call x1, Pallas kernels: 7.3 us -> 5.39 us  [integrals(): pl.pallas_call(functools.partial(integrals_kernel, rows), out_shape=jax.S...]
  transfers between devices with their start and end apart: 10 -> 10, of which waited for: 7 -> 8; matrix products, arithmetic and copies ran while one was open for 0% -> 0% of each run, Pallas kernels for 21% -> 16%
where the time goes in v4:
time: 33.2 us; the launch traced here: 33 us
  starting transfers between devices  13.6 us (41%)
  waiting for transfers between devices  9.43 us (28%)
  Pallas kernels  9.26 us (28%)
  between operations  0.7 us (2%)
    ppermute x10, starting transfers between devices, exchange(): lax.ppermute(value, axis, [(partner(i, k, size), i) for i in range(size)])  13.6 us
    ppermute x10, waiting for transfers between devices, exchange(): lax.ppermute(value, axis, [(partner(i, k, size), i) for i in range(size)])  9.43 us
    pallas_call x1, Pallas kernels, integrals(): pl.pallas_call(functools.partial(integrals_kernel, rows), out_shape=jax.S...  5.39 us
    pallas_call x1, Pallas kernels, pick(): pl.pallas_call(functools.partial(pick_kernel, libs[0].shape[1]), out_shap...  1.49 us
    pallas_call x1, Pallas kernels, fit(): pl.pallas_call(fit_kernel, out_shape=(jax.ShapeDtypeStruct((GROUPS, WIDTH...  1.28 us
    pallas_call x1, Pallas kernels, end(): pl.pallas_call(functools.partial(end_kernel, len(pieces)), out_shape=(sha...  1.1 us
  transfers between devices with their start and end apart: 10, of which 8 were waited for; matrix products, arithmetic and copies ran while one was open for 0% of the time, Pallas kernels for 16%

profile of v4, /device:TPU:0, one launch (start us, length us, event | category | flops | bytes accessed | tf_op | source)
XLA Modules:
  0.0 33.0 jit_solution(12247361463825713433)
XLA Ops:
  0.6 0.0 copy-start.1
  0.6 3.1 %collective-permute-start = (s32[4,42]{1,0:T(4,128)}, s32[4,42]{1,0:T(4,128)S(1)}, u32[]{:S(2)}, u32[]{:S(2)}) collective-permute-start(s32[4,42]{1,0:T(4,128)} %bitcast.4), channel_id=1, source_target_pairs={{1,0},{0,1},{3,2},{2,3},{5,4},{4,5},{7,6},{6,7},{9,8},{8,9},{11,10... | collective-permute-start | bytes 2024 | tf_op jit(solution)/shard_map/ppermute | solution.py:351
  3.7 2.6 %collective-permute-start.1 = (s32[4,42]{1,0:T(4,128)}, s32[4,42]{1,0:T(4,128)S(1)}, u32[]{:S(2)}, u32[]{:S(2)}) collective-permute-start(s32[4,42]{1,0:T(4,128)} %bitcast.5), channel_id=1, source_target_pairs={{2,0},{3,1},{0,2},{1,3},{6,4},{7,5},{4,6},{5,7},{10,8},{11,9},{8,1... | collective-permute-start | bytes 2024 | tf_op jit(solution)/shard_map/ppermute | solution.py:351
  6.3 0.0 collective-permute-start.2
  6.3 5.4 %integrals.1.refs_4_ = f32[2,2352,128]{2,1,0:T(8,128)S(1)} custom-call(s32[16]{0:T(128)} %centers_x.1, s32[16]{0:T(128)} %centers_y.1, s32[4]{0:T(128)} %centers_t.1, f32[4,2,8,64,128]{4,3,2,1,0:T(8,128)} %fields.1), custom_call_target="tpu_custom_call" | custom-call | flops 10000000000 | bytes 3000000 | tf_op jit(solution)/shard_map/integrals/pallas_call | solution.py:149
  11.7 0.0 copy-start
  11.7 0.0 collective-permute-done.refs_1_
  11.7 0.0 collective-permute-done.1.refs_2_
  11.8 0.2 collective-permute-done.2.refs_3_
  11.9 0.0 copy-done.1
  11.9 1.5 %pick.1.own = f32[1408,128]{1,0:T(8,128)S(1)} custom-call(s32[4,42]{1,0:T(4,128)S(1)} %bitcast.7, s32[4,42]{1,0:T(4,128)S(1)} %collective-permute-done.refs_1_, s32[4,42]{1,0:T(4,128)S(1)} %collective-permute-done.1.refs_2_, s32[4,42]{1,0:T(4,128)S(1)} %collective-permute-done.2.refs_3_, f32[2,2352,128]{2,1,0:T(8,128)S(1)} %integrals.1.refs_4_), custom_call_target="tpu_custom_call" | custom-call | tf_op jit(solution)/shard_map/pick/pallas_call | solution.py:205
  13.4 0.1 collective-permute-start.3
  13.5 2.2 %collective-permute-done.3.other = f32[1408,128]{1,0:T(8,128)S(1)} collective-permute-done((f32[1408,128]{1,0:T(8,128)S(1)}, f32[1408,128]{1,0:T(8,128)S(1)}, u32[]{:S(2)}, u32[]{:S(2)}) %collective-permute-start.3) | collective-permute-done | bytes 720928 | tf_op jit(solution)/shard_map/ppermute | solution.py:351
  15.7 0.0 copy-done
  15.7 1.3 %fit.1 = (f32[24,384]{1,0:T(8,128)S(1)}, f32[176,168]{1,0:T(8,128)S(1)}, f32[48,168]{1,0:T(8,128)S(1)}) custom-call(f32[1408,128]{1,0:T(8,128)S(1)} %pick.1.own, f32[1408,128]{1,0:T(8,128)S(1)} %collective-permute-done.3.other, s32[1,168]{1,0:T(1,128)S(1)} %bitcast.2), custom_call_target="tpu_custom_call" | custom-call | tf_op jit(solution)/shard_map/fit/pallas_call | solution.py:262
  17.0 1.8 %collective-permute-start.4 = (f32[24,384]{1,0:T(8,128)S(1)}, f32[24,384]{1,0:T(8,128)S(1)}, u32[]{:S(2)}, u32[]{:S(2)}) collective-permute-start(f32[24,384]{1,0:T(8,128)S(1)} %get-tuple-element.7), channel_id=1, source_target_pairs={{2,0},{3,1},{0,2},{1,3},{6,4},{7,5},{4,6},{5,7},{10,8},{11,9},{8,1... | collective-permute-start | bytes 110600 | tf_op jit(solution)/shard_map/ppermute | solution.py:351
  18.8 2.0 %collective-permute-start.5 = (f32[24,384]{1,0:T(8,128)S(1)}, f32[24,384]{1,0:T(8,128)S(1)}, u32[]{:S(2)}, u32[]{:S(2)}) collective-permute-start(f32[24,384]{1,0:T(8,128)S(1)} %get-tuple-element.7), channel_id=1, source_target_pairs={{3,0},{2,1},{1,2},{0,3},{7,4},{6,5},{5,6},{4,7},{11,8},{10,9},{9,1... | collective-permute-start | bytes 110600 | tf_op jit(solution)/shard_map/ppermute | solution.py:351
  20.8 0.5 %collective-permute-start.6 = (f32[24,384]{1,0:T(8,128)S(1)}, f32[24,384]{1,0:T(8,128)S(1)}, u32[]{:S(2)}, u32[]{:S(2)}) collective-permute-start(f32[24,384]{1,0:T(8,128)S(1)} %get-tuple-element.7), channel_id=1, source_target_pairs={{1,0},{0,1},{3,2},{2,3},{5,4},{4,5},{7,6},{6,7},{9,8},{8,9},{11,10... | collective-permute-start | bytes 110600 | tf_op jit(solution)/shard_map/ppermute | solution.py:351
  21.3 1.4 %collective-permute-done.4 = f32[24,384]{1,0:T(8,128)S(1)} collective-permute-done((f32[24,384]{1,0:T(8,128)S(1)}, f32[24,384]{1,0:T(8,128)S(1)}, u32[]{:S(2)}, u32[]{:S(2)}) %collective-permute-start.4) | collective-permute-done | bytes 36896 | tf_op jit(solution)/shard_map/ppermute | solution.py:351
  22.7 2.1 %collective-permute-done.5 = f32[24,384]{1,0:T(8,128)S(1)} collective-permute-done((f32[24,384]{1,0:T(8,128)S(1)}, f32[24,384]{1,0:T(8,128)S(1)}, u32[]{:S(2)}, u32[]{:S(2)}) %collective-permute-start.5) | collective-permute-done | bytes 36896 | tf_op jit(solution)/shard_map/ppermute | solution.py:351
  24.8 0.2 collective-permute-done.6
  25.0 1.6 %collective-permute-start.7 = (f32[24,384]{1,0:T(8,128)S(1)}, f32[24,384]{1,0:T(8,128)S(1)}, u32[]{:S(2)}, u32[]{:S(2)}) collective-permute-start(f32[24,384]{1,0:T(8,128)S(1)} %add_select_fusion.refs_0_), channel_id=1, source_target_pairs={{16,0},{24,8},{0,16},{8,24},{17,1},{25,9},{1,17},{9,25},{18,2},{26... | collective-permute-start | bytes 110600 | tf_op jit(solution)/shard_map/ppermute | solution.py:351
  26.6 1.4 %collective-permute-start.8 = (f32[24,384]{1,0:T(8,128)S(1)}, f32[24,384]{1,0:T(8,128)S(1)}, u32[]{:S(2)}, u32[]{:S(2)}) collective-permute-start(f32[24,384]{1,0:T(8,128)S(1)} %add_select_fusion.refs_0_), channel_id=1, source_target_pairs={{24,0},{16,8},{8,16},{0,24},{25,1},{17,9},{9,17},{1,25},{26,2},{18... | collective-permute-start | bytes 110600 | tf_op jit(solution)/shard_map/ppermute | solution.py:351
  28.0 0.5 %collective-permute-start.9 = (f32[24,384]{1,0:T(8,128)S(1)}, f32[24,384]{1,0:T(8,128)S(1)}, u32[]{:S(2)}, u32[]{:S(2)}) collective-permute-start(f32[24,384]{1,0:T(8,128)S(1)} %add_select_fusion.refs_0_), channel_id=1, source_target_pairs={{8,0},{0,8},{24,16},{16,24},{9,1},{1,9},{25,17},{17,25},{10,2},{2,... | collective-permute-start | bytes 110600 | tf_op jit(solution)/shard_map/ppermute | solution.py:351
  28.5 0.7 %collective-permute-done.7.refs_1_ = f32[24,384]{1,0:T(8,128)S(1)} collective-permute-done((f32[24,384]{1,0:T(8,128)S(1)}, f32[24,384]{1,0:T(8,128)S(1)}, u32[]{:S(2)}, u32[]{:S(2)}) %collective-permute-start.7) | collective-permute-done | bytes 36896 | tf_op jit(solution)/shard_map/ppermute | solution.py:351
  29.3 2.1 %collective-permute-done.8.refs_2_ = f32[24,384]{1,0:T(8,128)S(1)} collective-permute-done((f32[24,384]{1,0:T(8,128)S(1)}, f32[24,384]{1,0:T(8,128)S(1)}, u32[]{:S(2)}, u32[]{:S(2)}) %collective-permute-start.8) | collective-permute-done | bytes 36896 | tf_op jit(solution)/shard_map/ppermute | solution.py:351
  31.4 0.5 %collective-permute-done.9.refs_3_ = f32[24,384]{1,0:T(8,128)S(1)} collective-permute-done((f32[24,384]{1,0:T(8,128)S(1)}, f32[24,384]{1,0:T(8,128)S(1)}, u32[]{:S(2)}, u32[]{:S(2)}) %collective-permute-start.9) | collective-permute-done | bytes 36896 | tf_op jit(solution)/shard_map/ppermute | solution.py:351
  31.9 1.1 %finish.1 = (f32[1,2,168]{2,1,0:T(2,128)}, f32[1,2,168]{2,1,0:T(2,128)}) custom-call(s32[1,168]{1,0:T(1,128)S(1)} %bitcast.3, f32[176,168]{1,0:T(8,128)S(1)} %get-tuple-element.5.normal, f32[48,168]{1,0:T(8,128)S(1)} %get-tuple-element.6.dmat, f32[24,384]{1,0:T(8,128)S(1)} %add_select_fusion.refs_0_, f32[24,384]{1,0:T(8,128)S(1)} %collective-permute-done.7.refs_1_, ...), custom_call_target="tpu_custom_call" | custom-call | tf_op jit(solution)/shard_map/finish/pallas_call | solution.py:331
  (2 shorter events, 0.0 us)
Async XLA Ops:
  0.6 11.3 %copy-start.1 = (s32[42,4]{0,1:T(4,128)S(1)}, s32[42,4]{0,1:T(4,128)}, u32[]{:S(2)}) copy-start(s32[42,4]{0,1:T(4,128)} %param.7) | copy-start | bytes 2020
  0.6 11.1 %collective-permute-start = (s32[4,42]{1,0:T(4,128)}, s32[4,42]{1,0:T(4,128)S(1)}, u32[]{:S(2)}, u32[]{:S(2)}) collective-permute-start(s32[4,42]{1,0:T(4,128)} %bitcast.4), channel_id=1, source_target_pairs={{1,0},{0,1},{3,2},{2,3},{5,4},{4,5},{7,6},{6,7},{9,8},{8,9},{11,10... | collective-permute-start | bytes 2024 | tf_op jit(solution)/shard_map/ppermute | solution.py:351
  3.7 8.0 %collective-permute-start.1 = (s32[4,42]{1,0:T(4,128)}, s32[4,42]{1,0:T(4,128)S(1)}, u32[]{:S(2)}, u32[]{:S(2)}) collective-permute-start(s32[4,42]{1,0:T(4,128)} %bitcast.5), channel_id=1, source_target_pairs={{2,0},{3,1},{0,2},{1,3},{6,4},{7,5},{4,6},{5,7},{10,8},{11,9},{8,1... | collective-permute-start | bytes 2024 | tf_op jit(solution)/shard_map/ppermute | solution.py:351
  6.3 5.6 %collective-permute-start.2 = (s32[4,42]{1,0:T(4,128)}, s32[4,42]{1,0:T(4,128)S(1)}, u32[]{:S(2)}, u32[]{:S(2)}) collective-permute-start(s32[4,42]{1,0:T(4,128)} %bitcast.6), channel_id=1, source_target_pairs={{3,0},{2,1},{1,2},{0,3},{7,4},{6,5},{5,6},{4,7},{11,8},{10,9},{9,1... | collective-permute-start | bytes 2024 | tf_op jit(solution)/shard_map/ppermute | solution.py:351
  11.7 3.9 %copy-start = (s32[168]{0:T(256)S(1)}, s32[168]{0:T(256)}, u32[]{:S(2)}) copy-start(s32[168]{0:T(256)} %param.11) | copy-start | bytes 2020
  13.4 2.3 %collective-permute-start.3 = (f32[1408,128]{1,0:T(8,128)S(1)}, f32[1408,128]{1,0:T(8,128)S(1)}, u32[]{:S(2)}, u32[]{:S(2)}) collective-permute-start(f32[1408,128]{1,0:T(8,128)S(1)} %pick.1.own), channel_id=1, source_target_pairs={{4,0},{0,4},{5,1},{1,5},{6,2},{2,6},{7,3},{3,7},{12,8},{8,12},{13,... | collective-permute-start | bytes 2162696 | tf_op jit(solution)/shard_map/ppermute | solution.py:351
  17.0 5.7 %collective-permute-start.4 = (f32[24,384]{1,0:T(8,128)S(1)}, f32[24,384]{1,0:T(8,128)S(1)}, u32[]{:S(2)}, u32[]{:S(2)}) collective-permute-start(f32[24,384]{1,0:T(8,128)S(1)} %get-tuple-element.7), channel_id=1, source_target_pairs={{2,0},{3,1},{0,2},{1,3},{6,4},{7,5},{4,6},{5,7},{10,8},{11,9},{8,1... | collective-permute-start | bytes 110600 | tf_op jit(solution)/shard_map/ppermute | solution.py:351
  18.8 6.0 %collective-permute-start.5 = (f32[24,384]{1,0:T(8,128)S(1)}, f32[24,384]{1,0:T(8,128)S(1)}, u32[]{:S(2)}, u32[]{:S(2)}) collective-permute-start(f32[24,384]{1,0:T(8,128)S(1)} %get-tuple-element.7), channel_id=1, source_target_pairs={{3,0},{2,1},{1,2},{0,3},{7,4},{6,5},{5,6},{4,7},{11,8},{10,9},{9,1... | collective-permute-start | bytes 110600 | tf_op jit(solution)/shard_map/ppermute | solution.py:351
  20.8 4.2 %collective-permute-start.6 = (f32[24,384]{1,0:T(8,128)S(1)}, f32[24,384]{1,0:T(8,128)S(1)}, u32[]{:S(2)}, u32[]{:S(2)}) collective-permute-start(f32[24,384]{1,0:T(8,128)S(1)} %get-tuple-element.7), channel_id=1, source_target_pairs={{1,0},{0,1},{3,2},{2,3},{5,4},{4,5},{7,6},{6,7},{9,8},{8,9},{11,10... | collective-permute-start | bytes 110600 | tf_op jit(solution)/shard_map/ppermute | solution.py:351
  25.0 4.3 %collective-permute-start.7 = (f32[24,384]{1,0:T(8,128)S(1)}, f32[24,384]{1,0:T(8,128)S(1)}, u32[]{:S(2)}, u32[]{:S(2)}) collective-permute-start(f32[24,384]{1,0:T(8,128)S(1)} %add_select_fusion.refs_0_), channel_id=1, source_target_pairs={{16,0},{24,8},{0,16},{8,24},{17,1},{25,9},{1,17},{9,25},{18,2},{26... | collective-permute-start | bytes 110600 | tf_op jit(solution)/shard_map/ppermute | solution.py:351
  26.6 4.9 %collective-permute-start.8 = (f32[24,384]{1,0:T(8,128)S(1)}, f32[24,384]{1,0:T(8,128)S(1)}, u32[]{:S(2)}, u32[]{:S(2)}) collective-permute-start(f32[24,384]{1,0:T(8,128)S(1)} %add_select_fusion.refs_0_), channel_id=1, source_target_pairs={{24,0},{16,8},{8,16},{0,24},{25,1},{17,9},{9,17},{1,25},{26,2},{18... | collective-permute-start | bytes 110600 | tf_op jit(solution)/shard_map/ppermute | solution.py:351
  28.0 4.0 %collective-permute-start.9 = (f32[24,384]{1,0:T(8,128)S(1)}, f32[24,384]{1,0:T(8,128)S(1)}, u32[]{:S(2)}, u32[]{:S(2)}) collective-permute-start(f32[24,384]{1,0:T(8,128)S(1)} %add_select_fusion.refs_0_), channel_id=1, source_target_pairs={{8,0},{0,8},{24,16},{16,24},{9,1},{1,9},{25,17},{17,25},{10,2},{2,... | collective-permute-start | bytes 110600 | tf_op jit(solution)/shard_map/ppermute | solution.py:351

commit v5 on v4

--- a/solution.py
+++ b/solution.py
@@ -351,32 +351,45 @@
     return lax.ppermute(value, axis, [(partner(i, k, size), i) for i in range(size)])
 
 
+def shared_exchange(value, axis):
+    size = lax.axis_size(axis)
+    rounds = []
+    for first in range(0, size, 2):
+        steps = [(core, first + 2 - core) for core in range(2) if first + 2 - core < size]
+        pairs = [
+            (core * size + partner(i, k, size), core * size + i)
+            for core, k in steps
+            for i in range(size)
+        ]
+        rounds.append(lax.ppermute(value, ("space", axis), pairs))
+    return rounds
+
+
+def merge(values, own_core=None):
+    col = lax.broadcasted_iota(jnp.int32, values[0].shape, 1)
+    largest = functools.reduce(jnp.maximum, values)
+    if own_core is not None:
+        values = [jnp.where(lax.axis_index("space") == own_core, values[0], 0.0)] + values[1:]
+    return jnp.where(col == WIDTH - 1, largest, sum(values[1:], values[0]))
+
+
 def body(fields, library, centers_x, centers_y, centers_t, groups):
     pgroup = fields.shape[0]
     shares = lax.axis_size("term")
     local = library.shape[0]
     library = library.T
-    if pgroup != shares or local * shares != TERMS or shares & (shares - 1):
+    spaces = lax.axis_size("space")
+    if spaces != 2 or pgroup != shares or local * shares != TERMS or shares & (shares - 1):
         raise ValueError("unexpected split")
     libs = [library] + [exchange(library, "term", k) for k in range(1, shares)]
     flat = integrals(centers_x, centers_y, centers_t, fields)
     own = pick(libs, flat)
-    spaces = lax.axis_size("space")
-    others = [exchange(own, "space", k) for k in range(1, spaces)]
     grp = groups.reshape(1, TERMS)
-    payload, normal, dmat = fit(own, sum(others[1:], others[0]), grp)
-    col = lax.broadcasted_iota(jnp.int32, payload.shape, 1)
+    payload, normal, dmat = fit(own, exchange(own, "space", 1), grp)
     params = lax.axis_size("param")
-    pieces = [payload]
-    for k in neighbour_last(shares):
-        pieces.append(exchange(payload, "term", k))
-    total = sum(pieces[1:], pieces[0])
-    largest = functools.reduce(jnp.maximum, pieces)
-    payload = jnp.where(col == WIDTH - 1, largest, total)
-    pieces = [payload]
-    for k in neighbour_last(params):
-        pieces.append(exchange(payload, "param", k))
-    return end(grp, normal, dmat, pieces)
+    payload = merge([payload] + shared_exchange(payload, "term"), 0)
+    payload = merge([payload] + [exchange(payload, "param", k) for k in neighbour_last(params)])
+    return end(grp, normal, dmat, [payload, exchange(payload, "space", 1)])
 
 
 def solution(mesh):

time: 33.2 us -> 31.7 us (0.955)
  starting transfers between devices: 13.6 us -> 12.4 us
    ppermute x10 -> x8, starting transfers between devices: 13.6 us -> 9.92 us  [exchange(): lax.ppermute(value, axis, [(partner(i, k, size), i) for i in range(size)])]
    ppermute x10 -> x8, waiting for transfers between devices: 9.43 us -> 6.71 us  [exchange(): lax.ppermute(value, axis, [(partner(i, k, size), i) for i in range(size)])]
    ppermute x0 -> x2, starting transfers between devices: none -> 2.49 us  [shared_exchange(): rounds.append(lax.ppermute(value, ('space', axis), pairs))]
    ppermute x0 -> x2, waiting for transfers between devices: none -> 2.41 us  [shared_exchange(): rounds.append(lax.ppermute(value, ('space', axis), pairs))]
  transfers between devices with their start and end apart: 10 -> 10, of which waited for: 8 -> 7; matrix products, arithmetic and copies ran while one was open for 0% -> 0% of each run, Pallas kernels for 16% -> 17%
where the time goes in v5:
time: 31.7 us; the launch traced here: 31.6 us
  starting transfers between devices  12.4 us (39%)
  Pallas kernels  9.26 us (29%)
  waiting for transfers between devices  9.12 us (29%)
  between operations  0.72 us (2%)
    ppermute x8, starting transfers between devices, exchange(): lax.ppermute(value, axis, [(partner(i, k, size), i) for i in range(size)])  9.92 us
    ppermute x8, waiting for transfers between devices, exchange(): lax.ppermute(value, axis, [(partner(i, k, size), i) for i in range(size)])  6.71 us
    pallas_call x1, Pallas kernels, integrals(): pl.pallas_call(functools.partial(integrals_kernel, rows), out_shape=jax.S...  5.39 us
    ppermute x2, starting transfers between devices, shared_exchange(): rounds.append(lax.ppermute(value, ('space', axis), pairs))  2.49 us
    ppermute x2, waiting for transfers between devices, shared_exchange(): rounds.append(lax.ppermute(value, ('space', axis), pairs))  2.41 us
    pallas_call x1, Pallas kernels, pick(): pl.pallas_call(functools.partial(pick_kernel, libs[0].shape[1]), out_shap...  1.49 us
    pallas_call x1, Pallas kernels, fit(): pl.pallas_call(fit_kernel, out_shape=(jax.ShapeDtypeStruct((GROUPS, WIDTH...  1.28 us
    pallas_call x1, Pallas kernels, end(): pl.pallas_call(functools.partial(end_kernel, len(pieces)), out_shape=(sha...  1.09 us
  transfers between devices with their start and end apart: 10, of which 7 were waited for; matrix products, arithmetic and copies ran while one was open for 0% of the time, Pallas kernels for 17%

profile of v5, /device:TPU:0, one launch (start us, length us, event | category | flops | bytes accessed | tf_op | source)
XLA Modules:
  0.0 31.6 jit_solution(18340401287107555089)
XLA Ops:
  0.6 0.0 copy-start.1
  0.6 3.1 %collective-permute-start = (s32[4,42]{1,0:T(4,128)}, s32[4,42]{1,0:T(4,128)S(1)}, u32[]{:S(2)}, u32[]{:S(2)}) collective-permute-start(s32[4,42]{1,0:T(4,128)} %bitcast.4), channel_id=1, source_target_pairs={{1,0},{0,1},{3,2},{2,3},{5,4},{4,5},{7,6},{6,7},{9,8},{8,9},{11,10... | collective-permute-start | bytes 2024 | tf_op jit(solution)/shard_map/ppermute | solution.py:351
  3.7 2.6 %collective-permute-start.1 = (s32[4,42]{1,0:T(4,128)}, s32[4,42]{1,0:T(4,128)S(1)}, u32[]{:S(2)}, u32[]{:S(2)}) collective-permute-start(s32[4,42]{1,0:T(4,128)} %bitcast.5), channel_id=1, source_target_pairs={{2,0},{3,1},{0,2},{1,3},{6,4},{7,5},{4,6},{5,7},{10,8},{11,9},{8,1... | collective-permute-start | bytes 2024 | tf_op jit(solution)/shard_map/ppermute | solution.py:351
  6.3 0.0 collective-permute-start.2
  6.3 5.4 %integrals.1.refs_4_ = f32[2,2352,128]{2,1,0:T(8,128)S(1)} custom-call(s32[16]{0:T(128)} %centers_x.1, s32[16]{0:T(128)} %centers_y.1, s32[4]{0:T(128)} %centers_t.1, f32[4,2,8,64,128]{4,3,2,1,0:T(8,128)} %fields.1), custom_call_target="tpu_custom_call" | custom-call | flops 10000000000 | bytes 3000000 | tf_op jit(solution)/shard_map/integrals/pallas_call | solution.py:149
  11.7 0.0 copy-start
  11.7 0.0 collective-permute-done.refs_1_
  11.7 0.0 collective-permute-done.1.refs_2_
  11.8 0.2 collective-permute-done.2.refs_3_
  11.9 0.0 copy-done.1
  11.9 1.5 %pick.1.own = f32[1408,128]{1,0:T(8,128)S(1)} custom-call(s32[4,42]{1,0:T(4,128)S(1)} %bitcast.7, s32[4,42]{1,0:T(4,128)S(1)} %collective-permute-done.refs_1_, s32[4,42]{1,0:T(4,128)S(1)} %collective-permute-done.1.refs_2_, s32[4,42]{1,0:T(4,128)S(1)} %collective-permute-done.2.refs_3_, f32[2,2352,128]{2,1,0:T(8,128)S(1)} %integrals.1.refs_4_), custom_call_target="tpu_custom_call" | custom-call | tf_op jit(solution)/shard_map/pick/pallas_call | solution.py:205
  13.4 0.1 collective-permute-start.3
  13.5 2.2 %collective-permute-done.3.other = f32[1408,128]{1,0:T(8,128)S(1)} collective-permute-done((f32[1408,128]{1,0:T(8,128)S(1)}, f32[1408,128]{1,0:T(8,128)S(1)}, u32[]{:S(2)}, u32[]{:S(2)}) %collective-permute-start.3) | collective-permute-done | bytes 720928 | tf_op jit(solution)/shard_map/ppermute | solution.py:351
  15.7 0.0 copy-done
  15.7 1.3 %fit.1 = (f32[24,384]{1,0:T(8,128)S(1)}, f32[176,168]{1,0:T(8,128)S(1)}, f32[48,168]{1,0:T(8,128)S(1)}) custom-call(f32[1408,128]{1,0:T(8,128)S(1)} %pick.1.own, f32[1408,128]{1,0:T(8,128)S(1)} %collective-permute-done.3.other, s32[1,168]{1,0:T(1,128)S(1)} %bitcast.2), custom_call_target="tpu_custom_call" | custom-call | tf_op jit(solution)/shard_map/fit/pallas_call | solution.py:262
  17.0 1.8 %collective-permute-start.4 = (f32[24,384]{1,0:T(8,128)S(1)}, f32[24,384]{1,0:T(8,128)S(1)}, u32[]{:S(2)}, u32[]{:S(2)}) collective-permute-start(f32[24,384]{1,0:T(8,128)S(1)} %get-tuple-element.7), channel_id=1, source_target_pairs={{2,0},{3,1},{0,2},{1,3},{5,4},{4,5},{7,6},{6,7},{10,8},{11,9},{8,1... | collective-permute-start | bytes 110600 | tf_op jit(solution)/shard_map/ppermute | solution.py:364
  18.8 0.7 %collective-permute-start.5 = (f32[24,384]{1,0:T(8,128)S(1)}, f32[24,384]{1,0:T(8,128)S(1)}, u32[]{:S(2)}, u32[]{:S(2)}) collective-permute-start(f32[24,384]{1,0:T(8,128)S(1)} %get-tuple-element.7), channel_id=1, source_target_pairs={{7,4},{6,5},{5,6},{4,7},{15,12},{14,13},{13,14},{12,15},{23,20},{2... | collective-permute-start | bytes 110600 | tf_op jit(solution)/shard_map/ppermute | solution.py:364
  19.5 2.4 %collective-permute-done.4 = f32[24,384]{1,0:T(8,128)S(1)} collective-permute-done((f32[24,384]{1,0:T(8,128)S(1)}, f32[24,384]{1,0:T(8,128)S(1)}, u32[]{:S(2)}, u32[]{:S(2)}) %collective-permute-start.4) | collective-permute-done | bytes 36896 | tf_op jit(solution)/shard_map/ppermute | solution.py:364
  21.9 0.0 collective-permute-done.5
  21.9 1.7 %collective-permute-start.6 = (f32[24,384]{1,0:T(8,128)S(1)}, f32[24,384]{1,0:T(8,128)S(1)}, u32[]{:S(2)}, u32[]{:S(2)}) collective-permute-start(f32[24,384]{1,0:T(8,128)S(1)} %add_select_fusion.1), channel_id=1, source_target_pairs={{16,0},{24,8},{0,16},{8,24},{17,1},{25,9},{1,17},{9,25},{18,2},{26... | collective-permute-start | bytes 110600 | tf_op jit(solution)/shard_map/ppermute | solution.py:351
  23.6 1.4 %collective-permute-start.7 = (f32[24,384]{1,0:T(8,128)S(1)}, f32[24,384]{1,0:T(8,128)S(1)}, u32[]{:S(2)}, u32[]{:S(2)}) collective-permute-start(f32[24,384]{1,0:T(8,128)S(1)} %add_select_fusion.1), channel_id=1, source_target_pairs={{24,0},{16,8},{8,16},{0,24},{25,1},{17,9},{9,17},{1,25},{26,2},{18... | collective-permute-start | bytes 110600 | tf_op jit(solution)/shard_map/ppermute | solution.py:351
  25.0 0.5 %collective-permute-start.8 = (f32[24,384]{1,0:T(8,128)S(1)}, f32[24,384]{1,0:T(8,128)S(1)}, u32[]{:S(2)}, u32[]{:S(2)}) collective-permute-start(f32[24,384]{1,0:T(8,128)S(1)} %add_select_fusion.1), channel_id=1, source_target_pairs={{8,0},{0,8},{24,16},{16,24},{9,1},{1,9},{25,17},{17,25},{10,2},{2,... | collective-permute-start | bytes 110600 | tf_op jit(solution)/shard_map/ppermute | solution.py:351
  25.5 0.5 %collective-permute-done.6 = f32[24,384]{1,0:T(8,128)S(1)} collective-permute-done((f32[24,384]{1,0:T(8,128)S(1)}, f32[24,384]{1,0:T(8,128)S(1)}, u32[]{:S(2)}, u32[]{:S(2)}) %collective-permute-start.6) | collective-permute-done | bytes 36896 | tf_op jit(solution)/shard_map/ppermute | solution.py:351
  25.9 2.5 %collective-permute-done.7 = f32[24,384]{1,0:T(8,128)S(1)} collective-permute-done((f32[24,384]{1,0:T(8,128)S(1)}, f32[24,384]{1,0:T(8,128)S(1)}, u32[]{:S(2)}, u32[]{:S(2)}) %collective-permute-start.7) | collective-permute-done | bytes 36896 | tf_op jit(solution)/shard_map/ppermute | solution.py:351
  28.4 0.5 %collective-permute-done.8 = f32[24,384]{1,0:T(8,128)S(1)} collective-permute-done((f32[24,384]{1,0:T(8,128)S(1)}, f32[24,384]{1,0:T(8,128)S(1)}, u32[]{:S(2)}, u32[]{:S(2)}) %collective-permute-start.8) | collective-permute-done | bytes 36896 | tf_op jit(solution)/shard_map/ppermute | solution.py:351
  29.0 0.6 %collective-permute-start.9 = (f32[24,384]{1,0:T(8,128)S(1)}, f32[24,384]{1,0:T(8,128)S(1)}, u32[]{:S(2)}, u32[]{:S(2)}) collective-permute-start(f32[24,384]{1,0:T(8,128)S(1)} %add_select_fusion.refs_0_), channel_id=1, source_target_pairs={{4,0},{0,4},{5,1},{1,5},{6,2},{2,6},{7,3},{3,7},{12,8},{8,12},{13,... | collective-permute-start | bytes 110600 | tf_op jit(solution)/shard_map/ppermute | solution.py:351
  29.6 0.9 %collective-permute-done.9.refs_1_ = f32[24,384]{1,0:T(8,128)S(1)} collective-permute-done((f32[24,384]{1,0:T(8,128)S(1)}, f32[24,384]{1,0:T(8,128)S(1)}, u32[]{:S(2)}, u32[]{:S(2)}) %collective-permute-start.9) | collective-permute-done | bytes 36896 | tf_op jit(solution)/shard_map/ppermute | solution.py:351
  30.5 1.1 %finish.1 = (f32[1,2,168]{2,1,0:T(2,128)}, f32[1,2,168]{2,1,0:T(2,128)}) custom-call(s32[1,168]{1,0:T(1,128)S(1)} %bitcast.3, f32[176,168]{1,0:T(8,128)S(1)} %get-tuple-element.5.normal, f32[48,168]{1,0:T(8,128)S(1)} %get-tuple-element.6.dmat, f32[24,384]{1,0:T(8,128)S(1)} %add_select_fusion.refs_0_, f32[24,384]{1,0:T(8,128)S(1)} %collective-permute-done.9.refs_1_), custom_call_target="tpu_custom_call" | custom-call | tf_op jit(solution)/shard_map/finish/pallas_call | solution.py:331
  (3 shorter events, 0.0 us)
Async XLA Ops:
  0.6 11.3 %copy-start.1 = (s32[42,4]{0,1:T(4,128)S(1)}, s32[42,4]{0,1:T(4,128)}, u32[]{:S(2)}) copy-start(s32[42,4]{0,1:T(4,128)} %param.7) | copy-start | bytes 2020
  0.6 11.1 %collective-permute-start = (s32[4,42]{1,0:T(4,128)}, s32[4,42]{1,0:T(4,128)S(1)}, u32[]{:S(2)}, u32[]{:S(2)}) collective-permute-start(s32[4,42]{1,0:T(4,128)} %bitcast.4), channel_id=1, source_target_pairs={{1,0},{0,1},{3,2},{2,3},{5,4},{4,5},{7,6},{6,7},{9,8},{8,9},{11,10... | collective-permute-start | bytes 2024 | tf_op jit(solution)/shard_map/ppermute | solution.py:351
  3.7 8.0 %collective-permute-start.1 = (s32[4,42]{1,0:T(4,128)}, s32[4,42]{1,0:T(4,128)S(1)}, u32[]{:S(2)}, u32[]{:S(2)}) collective-permute-start(s32[4,42]{1,0:T(4,128)} %bitcast.5), channel_id=1, source_target_pairs={{2,0},{3,1},{0,2},{1,3},{6,4},{7,5},{4,6},{5,7},{10,8},{11,9},{8,1... | collective-permute-start | bytes 2024 | tf_op jit(solution)/shard_map/ppermute | solution.py:351
  6.3 5.6 %collective-permute-start.2 = (s32[4,42]{1,0:T(4,128)}, s32[4,42]{1,0:T(4,128)S(1)}, u32[]{:S(2)}, u32[]{:S(2)}) collective-permute-start(s32[4,42]{1,0:T(4,128)} %bitcast.6), channel_id=1, source_target_pairs={{3,0},{2,1},{1,2},{0,3},{7,4},{6,5},{5,6},{4,7},{11,8},{10,9},{9,1... | collective-permute-start | bytes 2024 | tf_op jit(solution)/shard_map/ppermute | solution.py:351
  11.7 3.9 %copy-start = (s32[168]{0:T(256)S(1)}, s32[168]{0:T(256)}, u32[]{:S(2)}) copy-start(s32[168]{0:T(256)} %param.11) | copy-start | bytes 2020
  13.4 2.3 %collective-permute-start.3 = (f32[1408,128]{1,0:T(8,128)S(1)}, f32[1408,128]{1,0:T(8,128)S(1)}, u32[]{:S(2)}, u32[]{:S(2)}) collective-permute-start(f32[1408,128]{1,0:T(8,128)S(1)} %pick.1.own), channel_id=1, source_target_pairs={{4,0},{0,4},{5,1},{1,5},{6,2},{2,6},{7,3},{3,7},{12,8},{8,12},{13,... | collective-permute-start | bytes 2162696 | tf_op jit(solution)/shard_map/ppermute | solution.py:351
  17.0 4.9 %collective-permute-start.4 = (f32[24,384]{1,0:T(8,128)S(1)}, f32[24,384]{1,0:T(8,128)S(1)}, u32[]{:S(2)}, u32[]{:S(2)}) collective-permute-start(f32[24,384]{1,0:T(8,128)S(1)} %get-tuple-element.7), channel_id=1, source_target_pairs={{2,0},{3,1},{0,2},{1,3},{5,4},{4,5},{7,6},{6,7},{10,8},{11,9},{8,1... | collective-permute-start | bytes 110600 | tf_op jit(solution)/shard_map/ppermute | solution.py:364
  18.8 3.1 %collective-permute-start.5 = (f32[24,384]{1,0:T(8,128)S(1)}, f32[24,384]{1,0:T(8,128)S(1)}, u32[]{:S(2)}, u32[]{:S(2)}) collective-permute-start(f32[24,384]{1,0:T(8,128)S(1)} %get-tuple-element.7), channel_id=1, source_target_pairs={{7,4},{6,5},{5,6},{4,7},{15,12},{14,13},{13,14},{12,15},{23,20},{2... | collective-permute-start | bytes 110600 | tf_op jit(solution)/shard_map/ppermute | solution.py:364
  21.9 4.0 %collective-permute-start.6 = (f32[24,384]{1,0:T(8,128)S(1)}, f32[24,384]{1,0:T(8,128)S(1)}, u32[]{:S(2)}, u32[]{:S(2)}) collective-permute-start(f32[24,384]{1,0:T(8,128)S(1)} %add_select_fusion.1), channel_id=1, source_target_pairs={{16,0},{24,8},{0,16},{8,24},{17,1},{25,9},{1,17},{9,25},{18,2},{26... | collective-permute-start | bytes 110600 | tf_op jit(solution)/shard_map/ppermute | solution.py:351
  23.6 4.9 %collective-permute-start.7 = (f32[24,384]{1,0:T(8,128)S(1)}, f32[24,384]{1,0:T(8,128)S(1)}, u32[]{:S(2)}, u32[]{:S(2)}) collective-permute-start(f32[24,384]{1,0:T(8,128)S(1)} %add_select_fusion.1), channel_id=1, source_target_pairs={{24,0},{16,8},{8,16},{0,24},{25,1},{17,9},{9,17},{1,25},{26,2},{18... | collective-permute-start | bytes 110600 | tf_op jit(solution)/shard_map/ppermute | solution.py:351
  25.0 4.0 %collective-permute-start.8 = (f32[24,384]{1,0:T(8,128)S(1)}, f32[24,384]{1,0:T(8,128)S(1)}, u32[]{:S(2)}, u32[]{:S(2)}) collective-permute-start(f32[24,384]{1,0:T(8,128)S(1)} %add_select_fusion.1), channel_id=1, source_target_pairs={{8,0},{0,8},{24,16},{16,24},{9,1},{1,9},{25,17},{17,25},{10,2},{2,... | collective-permute-start | bytes 110600 | tf_op jit(solution)/shard_map/ppermute | solution.py:351
  29.0 1.5 %collective-permute-start.9 = (f32[24,384]{1,0:T(8,128)S(1)}, f32[24,384]{1,0:T(8,128)S(1)}, u32[]{:S(2)}, u32[]{:S(2)}) collective-permute-start(f32[24,384]{1,0:T(8,128)S(1)} %add_select_fusion.refs_0_), channel_id=1, source_target_pairs={{4,0},{0,4},{5,1},{1,5},{6,2},{2,6},{7,3},{3,7},{12,8},{8,12},{13,... | collective-permute-start | bytes 110600 | tf_op jit(solution)/shard_map/ppermute | solution.py:351

commit v6 on v5

--- a/solution.py
+++ b/solution.py
@@ -80,7 +80,10 @@
     for k in range(KY):
         center = jnp.where(row == k, cy[k], center)
     offset = ((lane - center + NY // 2) & (NY - 1)) - NY // 2
-    for i, part in enumerate(split(jnp.concatenate(space_rows(offset), axis=0))):
+    rest = jnp.concatenate(space_rows(offset), axis=0)
+    for i in range(3):
+        part = rest.astype(bf16)
+        rest = rest - part.astype(f32)
         y_split[pl.ds(i * ROWS, ROWS), :] = jnp.concatenate([part, part], axis=1)
     lane = lax.broadcasted_iota(jnp.int32, (1, LANES), 1)
     slot, kt, kx = lane >> 6, (lane >> 4) & 3, lane & 15
@@ -135,7 +138,9 @@
                     monomial = monomial * factors[1]
                 both = jnp.concatenate(split(monomial), axis=0)
                 across = dot(y_split[...], both, NN_DIMS)
-                across_high, across_low = split(across[:ROWS] + across[ROWS:])
+                across_high, across_low = split(
+                    across[:ROWS] + (across[ROWS : 2 * ROWS] + across[2 * ROWS :])
+                )
                 high[a & 1, pl.ds( b * ROWS, ROWS), part] = across_high
                 low[a & 1, pl.ds( b * ROWS, ROWS), part] = across_low
         if a: contract(a - 1)
@@ -159,7 +164,7 @@
             pltpu.VMEM((NY, cells), f32),
             pltpu.VMEM((NY, cells), f32),
             pltpu.VMEM((POWERS - 1, NY, cells), f32),
-            pltpu.VMEM((2 * ROWS, 2 * NY), bf16),
+            pltpu.VMEM((3 * ROWS, 2 * NY), bf16),
             pltpu.VMEM((2, cells, LANES), bf16),
             pltpu.VMEM((2, POWERS * ROWS, cells), bf16),
             pltpu.VMEM((2, POWERS * ROWS, cells), bf16),

time: 31.7 us -> 31.6 us (level)
  no operation moved by 1% of the time
where the time goes in v6:
time: 31.6 us; the launch traced here: 31.4 us
  starting transfers between devices  12.2 us (39%)
  waiting for transfers between devices  9.34 us (30%)
  Pallas kernels  9.11 us (29%)
  between operations  0.72 us (2%)
    ppermute x8, starting transfers between devices, exchange(): lax.ppermute(value, axis, [(partner(i, k, size), i) for i in range(size)])  9.86 us
    ppermute x8, waiting for transfers between devices, exchange(): lax.ppermute(value, axis, [(partner(i, k, size), i) for i in range(size)])  6.78 us
    pallas_call x1, Pallas kernels, integrals(): pl.pallas_call(functools.partial(integrals_kernel, rows), out_shape=jax.S...  5.24 us
    ppermute x2, waiting for transfers between devices, shared_exchange(): rounds.append(lax.ppermute(value, ('space', axis), pairs))  2.56 us
    ppermute x2, starting transfers between devices, shared_exchange(): rounds.append(lax.ppermute(value, ('space', axis), pairs))  2.34 us
    pallas_call x1, Pallas kernels, pick(): pl.pallas_call(functools.partial(pick_kernel, libs[0].shape[1]), out_shap...  1.49 us
    pallas_call x1, Pallas kernels, fit(): pl.pallas_call(fit_kernel, out_shape=(jax.ShapeDtypeStruct((GROUPS, WIDTH...  1.28 us
    pallas_call x1, Pallas kernels, end(): pl.pallas_call(functools.partial(end_kernel, len(pieces)), out_shape=(sha...  1.09 us
  transfers between devices with their start and end apart: 10, of which 7 were waited for; matrix products, arithmetic and copies ran while one was open for 0% of the time, Pallas kernels for 17%

profile of v6, /device:TPU:0, one launch (start us, length us, event | category | flops | bytes accessed | tf_op | source)
XLA Modules:
  0.0 31.4 jit_solution(13761525463137768235)
XLA Ops:
  0.6 0.0 copy-start.1
  0.6 3.1 %collective-permute-start = (s32[4,42]{1,0:T(4,128)}, s32[4,42]{1,0:T(4,128)S(1)}, u32[]{:S(2)}, u32[]{:S(2)}) collective-permute-start(s32[4,42]{1,0:T(4,128)} %bitcast.4), channel_id=1, source_target_pairs={{1,0},{0,1},{3,2},{2,3},{5,4},{4,5},{7,6},{6,7},{9,8},{8,9},{11,10... | collective-permute-start | bytes 2024 | tf_op jit(solution)/shard_map/ppermute | solution.py:356
  3.7 2.6 %collective-permute-start.1 = (s32[4,42]{1,0:T(4,128)}, s32[4,42]{1,0:T(4,128)S(1)}, u32[]{:S(2)}, u32[]{:S(2)}) collective-permute-start(s32[4,42]{1,0:T(4,128)} %bitcast.5), channel_id=1, source_target_pairs={{2,0},{3,1},{0,2},{1,3},{6,4},{7,5},{4,6},{5,7},{10,8},{11,9},{8,1... | collective-permute-start | bytes 2024 | tf_op jit(solution)/shard_map/ppermute | solution.py:356
  6.3 0.0 collective-permute-start.2
  6.3 5.2 %integrals.1.refs_4_ = f32[2,2352,128]{2,1,0:T(8,128)S(1)} custom-call(s32[16]{0:T(128)} %centers_x.1, s32[16]{0:T(128)} %centers_y.1, s32[4]{0:T(128)} %centers_t.1, f32[4,2,8,64,128]{4,3,2,1,0:T(8,128)} %fields.1), custom_call_target="tpu_custom_call" | custom-call | flops 10000000000 | bytes 3000000 | tf_op jit(solution)/shard_map/integrals/pallas_call | solution.py:154
  11.6 0.0 copy-start
  11.6 0.0 collective-permute-done.refs_1_
  11.6 0.0 collective-permute-done.1.refs_2_
  11.6 0.3 collective-permute-done.2.refs_3_
  11.9 0.0 copy-done.1
  11.9 1.5 %pick.1.own = f32[1408,128]{1,0:T(8,128)S(1)} custom-call(s32[4,42]{1,0:T(4,128)S(1)} %bitcast.7, s32[4,42]{1,0:T(4,128)S(1)} %collective-permute-done.refs_1_, s32[4,42]{1,0:T(4,128)S(1)} %collective-permute-done.1.refs_2_, s32[4,42]{1,0:T(4,128)S(1)} %collective-permute-done.2.refs_3_, f32[2,2352,128]{2,1,0:T(8,128)S(1)} %integrals.1.refs_4_), custom_call_target="tpu_custom_call" | custom-call | tf_op jit(solution)/shard_map/pick/pallas_call | solution.py:210
  13.4 0.1 collective-permute-start.3
  13.5 2.2 %collective-permute-done.3.other = f32[1408,128]{1,0:T(8,128)S(1)} collective-permute-done((f32[1408,128]{1,0:T(8,128)S(1)}, f32[1408,128]{1,0:T(8,128)S(1)}, u32[]{:S(2)}, u32[]{:S(2)}) %collective-permute-start.3) | collective-permute-done | bytes 720928 | tf_op jit(solution)/shard_map/ppermute | solution.py:356
  15.7 0.0 copy-done
  15.7 1.3 %fit.1 = (f32[24,384]{1,0:T(8,128)S(1)}, f32[176,168]{1,0:T(8,128)S(1)}, f32[48,168]{1,0:T(8,128)S(1)}) custom-call(f32[1408,128]{1,0:T(8,128)S(1)} %pick.1.own, f32[1408,128]{1,0:T(8,128)S(1)} %collective-permute-done.3.other, s32[1,168]{1,0:T(1,128)S(1)} %bitcast.2), custom_call_target="tpu_custom_call" | custom-call | tf_op jit(solution)/shard_map/fit/pallas_call | solution.py:267
  17.0 1.7 %collective-permute-start.4 = (f32[24,384]{1,0:T(8,128)S(1)}, f32[24,384]{1,0:T(8,128)S(1)}, u32[]{:S(2)}, u32[]{:S(2)}) collective-permute-start(f32[24,384]{1,0:T(8,128)S(1)} %get-tuple-element.7), channel_id=1, source_target_pairs={{2,0},{3,1},{0,2},{1,3},{5,4},{4,5},{7,6},{6,7},{10,8},{11,9},{8,1... | collective-permute-start | bytes 110600 | tf_op jit(solution)/shard_map/ppermute | solution.py:369
  18.6 0.7 %collective-permute-start.5 = (f32[24,384]{1,0:T(8,128)S(1)}, f32[24,384]{1,0:T(8,128)S(1)}, u32[]{:S(2)}, u32[]{:S(2)}) collective-permute-start(f32[24,384]{1,0:T(8,128)S(1)} %get-tuple-element.7), channel_id=1, source_target_pairs={{7,4},{6,5},{5,6},{4,7},{15,12},{14,13},{13,14},{12,15},{23,20},{2... | collective-permute-start | bytes 110600 | tf_op jit(solution)/shard_map/ppermute | solution.py:369
  19.3 2.6 %collective-permute-done.4 = f32[24,384]{1,0:T(8,128)S(1)} collective-permute-done((f32[24,384]{1,0:T(8,128)S(1)}, f32[24,384]{1,0:T(8,128)S(1)}, u32[]{:S(2)}, u32[]{:S(2)}) %collective-permute-start.4) | collective-permute-done | bytes 36896 | tf_op jit(solution)/shard_map/ppermute | solution.py:369
  21.9 0.0 collective-permute-done.5
  21.9 1.6 %collective-permute-start.6 = (f32[24,384]{1,0:T(8,128)S(1)}, f32[24,384]{1,0:T(8,128)S(1)}, u32[]{:S(2)}, u32[]{:S(2)}) collective-permute-start(f32[24,384]{1,0:T(8,128)S(1)} %add_select_fusion.1), channel_id=1, source_target_pairs={{16,0},{24,8},{0,16},{8,24},{17,1},{25,9},{1,17},{9,25},{18,2},{26... | collective-permute-start | bytes 110600 | tf_op jit(solution)/shard_map/ppermute | solution.py:356
  23.5 1.4 %collective-permute-start.7 = (f32[24,384]{1,0:T(8,128)S(1)}, f32[24,384]{1,0:T(8,128)S(1)}, u32[]{:S(2)}, u32[]{:S(2)}) collective-permute-start(f32[24,384]{1,0:T(8,128)S(1)} %add_select_fusion.1), channel_id=1, source_target_pairs={{24,0},{16,8},{8,16},{0,24},{25,1},{17,9},{9,17},{1,25},{26,2},{18... | collective-permute-start | bytes 110600 | tf_op jit(solution)/shard_map/ppermute | solution.py:356
  24.9 0.5 %collective-permute-start.8 = (f32[24,384]{1,0:T(8,128)S(1)}, f32[24,384]{1,0:T(8,128)S(1)}, u32[]{:S(2)}, u32[]{:S(2)}) collective-permute-start(f32[24,384]{1,0:T(8,128)S(1)} %add_select_fusion.1), channel_id=1, source_target_pairs={{8,0},{0,8},{24,16},{16,24},{9,1},{1,9},{25,17},{17,25},{10,2},{2,... | collective-permute-start | bytes 110600 | tf_op jit(solution)/shard_map/ppermute | solution.py:356
  25.5 0.5 %collective-permute-done.6 = f32[24,384]{1,0:T(8,128)S(1)} collective-permute-done((f32[24,384]{1,0:T(8,128)S(1)}, f32[24,384]{1,0:T(8,128)S(1)}, u32[]{:S(2)}, u32[]{:S(2)}) %collective-permute-start.6) | collective-permute-done | bytes 36896 | tf_op jit(solution)/shard_map/ppermute | solution.py:356
  25.9 2.4 %collective-permute-done.7 = f32[24,384]{1,0:T(8,128)S(1)} collective-permute-done((f32[24,384]{1,0:T(8,128)S(1)}, f32[24,384]{1,0:T(8,128)S(1)}, u32[]{:S(2)}, u32[]{:S(2)}) %collective-permute-start.7) | collective-permute-done | bytes 36896 | tf_op jit(solution)/shard_map/ppermute | solution.py:356
  28.3 0.5 %collective-permute-done.8 = f32[24,384]{1,0:T(8,128)S(1)} collective-permute-done((f32[24,384]{1,0:T(8,128)S(1)}, f32[24,384]{1,0:T(8,128)S(1)}, u32[]{:S(2)}, u32[]{:S(2)}) %collective-permute-start.8) | collective-permute-done | bytes 36896 | tf_op jit(solution)/shard_map/ppermute | solution.py:356
  28.9 0.6 %collective-permute-start.9 = (f32[24,384]{1,0:T(8,128)S(1)}, f32[24,384]{1,0:T(8,128)S(1)}, u32[]{:S(2)}, u32[]{:S(2)}) collective-permute-start(f32[24,384]{1,0:T(8,128)S(1)} %add_select_fusion.refs_0_), channel_id=1, source_target_pairs={{4,0},{0,4},{5,1},{1,5},{6,2},{2,6},{7,3},{3,7},{12,8},{8,12},{13,... | collective-permute-start | bytes 110600 | tf_op jit(solution)/shard_map/ppermute | solution.py:356
  29.5 0.9 %collective-permute-done.9.refs_1_ = f32[24,384]{1,0:T(8,128)S(1)} collective-permute-done((f32[24,384]{1,0:T(8,128)S(1)}, f32[24,384]{1,0:T(8,128)S(1)}, u32[]{:S(2)}, u32[]{:S(2)}) %collective-permute-start.9) | collective-permute-done | bytes 36896 | tf_op jit(solution)/shard_map/ppermute | solution.py:356
  30.3 1.1 %finish.1 = (f32[1,2,168]{2,1,0:T(2,128)}, f32[1,2,168]{2,1,0:T(2,128)}) custom-call(s32[1,168]{1,0:T(1,128)S(1)} %bitcast.3, f32[176,168]{1,0:T(8,128)S(1)} %get-tuple-element.5.normal, f32[48,168]{1,0:T(8,128)S(1)} %get-tuple-element.6.dmat, f32[24,384]{1,0:T(8,128)S(1)} %add_select_fusion.refs_0_, f32[24,384]{1,0:T(8,128)S(1)} %collective-permute-done.9.refs_1_), custom_call_target="tpu_custom_call" | custom-call | tf_op jit(solution)/shard_map/finish/pallas_call | solution.py:336
  (3 shorter events, 0.0 us)
Async XLA Ops:
  0.6 11.3 %copy-start.1 = (s32[42,4]{0,1:T(4,128)S(1)}, s32[42,4]{0,1:T(4,128)}, u32[]{:S(2)}) copy-start(s32[42,4]{0,1:T(4,128)} %param.7) | copy-start | bytes 2020
  0.6 10.9 %collective-permute-start = (s32[4,42]{1,0:T(4,128)}, s32[4,42]{1,0:T(4,128)S(1)}, u32[]{:S(2)}, u32[]{:S(2)}) collective-permute-start(s32[4,42]{1,0:T(4,128)} %bitcast.4), channel_id=1, source_target_pairs={{1,0},{0,1},{3,2},{2,3},{5,4},{4,5},{7,6},{6,7},{9,8},{8,9},{11,10... | collective-permute-start | bytes 2024 | tf_op jit(solution)/shard_map/ppermute | solution.py:356
  3.7 7.9 %collective-permute-start.1 = (s32[4,42]{1,0:T(4,128)}, s32[4,42]{1,0:T(4,128)S(1)}, u32[]{:S(2)}, u32[]{:S(2)}) collective-permute-start(s32[4,42]{1,0:T(4,128)} %bitcast.5), channel_id=1, source_target_pairs={{2,0},{3,1},{0,2},{1,3},{6,4},{7,5},{4,6},{5,7},{10,8},{11,9},{8,1... | collective-permute-start | bytes 2024 | tf_op jit(solution)/shard_map/ppermute | solution.py:356
  6.3 5.6 %collective-permute-start.2 = (s32[4,42]{1,0:T(4,128)}, s32[4,42]{1,0:T(4,128)S(1)}, u32[]{:S(2)}, u32[]{:S(2)}) collective-permute-start(s32[4,42]{1,0:T(4,128)} %bitcast.6), channel_id=1, source_target_pairs={{3,0},{2,1},{1,2},{0,3},{7,4},{6,5},{5,6},{4,7},{11,8},{10,9},{9,1... | collective-permute-start | bytes 2024 | tf_op jit(solution)/shard_map/ppermute | solution.py:356
  11.6 4.1 %copy-start = (s32[168]{0:T(256)S(1)}, s32[168]{0:T(256)}, u32[]{:S(2)}) copy-start(s32[168]{0:T(256)} %param.11) | copy-start | bytes 2020
  13.4 2.3 %collective-permute-start.3 = (f32[1408,128]{1,0:T(8,128)S(1)}, f32[1408,128]{1,0:T(8,128)S(1)}, u32[]{:S(2)}, u32[]{:S(2)}) collective-permute-start(f32[1408,128]{1,0:T(8,128)S(1)} %pick.1.own), channel_id=1, source_target_pairs={{4,0},{0,4},{5,1},{1,5},{6,2},{2,6},{7,3},{3,7},{12,8},{8,12},{13,... | collective-permute-start | bytes 2162696 | tf_op jit(solution)/shard_map/ppermute | solution.py:356
  17.0 4.9 %collective-permute-start.4 = (f32[24,384]{1,0:T(8,128)S(1)}, f32[24,384]{1,0:T(8,128)S(1)}, u32[]{:S(2)}, u32[]{:S(2)}) collective-permute-start(f32[24,384]{1,0:T(8,128)S(1)} %get-tuple-element.7), channel_id=1, source_target_pairs={{2,0},{3,1},{0,2},{1,3},{5,4},{4,5},{7,6},{6,7},{10,8},{11,9},{8,1... | collective-permute-start | bytes 110600 | tf_op jit(solution)/shard_map/ppermute | solution.py:369
  18.6 3.2 %collective-permute-start.5 = (f32[24,384]{1,0:T(8,128)S(1)}, f32[24,384]{1,0:T(8,128)S(1)}, u32[]{:S(2)}, u32[]{:S(2)}) collective-permute-start(f32[24,384]{1,0:T(8,128)S(1)} %get-tuple-element.7), channel_id=1, source_target_pairs={{7,4},{6,5},{5,6},{4,7},{15,12},{14,13},{13,14},{12,15},{23,20},{2... | collective-permute-start | bytes 110600 | tf_op jit(solution)/shard_map/ppermute | solution.py:369
  21.9 4.0 %collective-permute-start.6 = (f32[24,384]{1,0:T(8,128)S(1)}, f32[24,384]{1,0:T(8,128)S(1)}, u32[]{:S(2)}, u32[]{:S(2)}) collective-permute-start(f32[24,384]{1,0:T(8,128)S(1)} %add_select_fusion.1), channel_id=1, source_target_pairs={{16,0},{24,8},{0,16},{8,24},{17,1},{25,9},{1,17},{9,25},{18,2},{26... | collective-permute-start | bytes 110600 | tf_op jit(solution)/shard_map/ppermute | solution.py:356
  23.5 4.9 %collective-permute-start.7 = (f32[24,384]{1,0:T(8,128)S(1)}, f32[24,384]{1,0:T(8,128)S(1)}, u32[]{:S(2)}, u32[]{:S(2)}) collective-permute-start(f32[24,384]{1,0:T(8,128)S(1)} %add_select_fusion.1), channel_id=1, source_target_pairs={{24,0},{16,8},{8,16},{0,24},{25,1},{17,9},{9,17},{1,25},{26,2},{18... | collective-permute-start | bytes 110600 | tf_op jit(solution)/shard_map/ppermute | solution.py:356
  24.9 4.0 %collective-permute-start.8 = (f32[24,384]{1,0:T(8,128)S(1)}, f32[24,384]{1,0:T(8,128)S(1)}, u32[]{:S(2)}, u32[]{:S(2)}) collective-permute-start(f32[24,384]{1,0:T(8,128)S(1)} %add_select_fusion.1), channel_id=1, source_target_pairs={{8,0},{0,8},{24,16},{16,24},{9,1},{1,9},{25,17},{17,25},{10,2},{2,... | collective-permute-start | bytes 110600 | tf_op jit(solution)/shard_map/ppermute | solution.py:356
  28.9 1.4 %collective-permute-start.9 = (f32[24,384]{1,0:T(8,128)S(1)}, f32[24,384]{1,0:T(8,128)S(1)}, u32[]{:S(2)}, u32[]{:S(2)}) collective-permute-start(f32[24,384]{1,0:T(8,128)S(1)} %add_select_fusion.refs_0_), channel_id=1, source_target_pairs={{4,0},{0,4},{5,1},{1,5},{6,2},{2,6},{7,3},{3,7},{12,8},{8,12},{13,... | collective-permute-start | bytes 110600 | tf_op jit(solution)/shard_map/ppermute | solution.py:356

commit v7 on v6

--- a/solution.py
+++ b/solution.py
@@ -220,13 +220,16 @@
 def fit_kernel(own, other, grp, payload, normal, dmat):
     pad = TERMS + 8
     gram = jnp.zeros((pad, pad), f32)
+    cross = jnp.zeros((pad, pad), f32)
     for q in range(4):
         parts = []
         for s in (2 * q, 2 * q + 1):
             rows = pl.ds(s, pad, stride=8)
             parts.append(own[rows, :] + other[rows, :])
-        x = jnp.concatenate(parts, axis=1)
-        gram = gram + dot3(x, x, NT_DIMS)
+        high, low = split(jnp.concatenate(parts, axis=1))
+        gram = gram + dot(high, high, NT_DIMS)
+        cross = cross + dot(high, low, NT_DIMS)
+    gram = gram + (cross + cross.T)
     ri = lax.broadcasted_iota(jnp.int32, (pad, pad), 0)
     ci = lax.broadcasted_iota(jnp.int32, (pad, pad), 1)
     diagonal = jnp.where(ri == ci, gram, 0.0)

time: 31.6 us -> 31.5 us (level)
  no operation moved by 1% of the time
where the time goes in v7:
time: 31.5 us; the launch traced here: 31.3 us
  starting transfers between devices  12.2 us (39%)
  waiting for transfers between devices  9.34 us (30%)
  Pallas kernels  9.04 us (29%)
  between operations  0.72 us (2%)
    ppermute x8, starting transfers between devices, exchange(): lax.ppermute(value, axis, [(partner(i, k, size), i) for i in range(size)])  9.86 us
    ppermute x8, waiting for transfers between devices, exchange(): lax.ppermute(value, axis, [(partner(i, k, size), i) for i in range(size)])  6.78 us
    pallas_call x1, Pallas kernels, integrals(): pl.pallas_call(functools.partial(integrals_kernel, rows), out_shape=jax.S...  5.24 us
    ppermute x2, waiting for transfers between devices, shared_exchange(): rounds.append(lax.ppermute(value, ('space', axis), pairs))  2.56 us
    ppermute x2, starting transfers between devices, shared_exchange(): rounds.append(lax.ppermute(value, ('space', axis), pairs))  2.31 us
    pallas_call x1, Pallas kernels, pick(): pl.pallas_call(functools.partial(pick_kernel, libs[0].shape[1]), out_shap...  1.49 us
    pallas_call x1, Pallas kernels, fit(): pl.pallas_call(fit_kernel, out_shape=(jax.ShapeDtypeStruct((GROUPS, WIDTH...  1.22 us
    pallas_call x1, Pallas kernels, end(): pl.pallas_call(functools.partial(end_kernel, len(pieces)), out_shape=(sha...  1.09 us
  transfers between devices with their start and end apart: 10, of which 7 were waited for; matrix products, arithmetic and copies ran while one was open for 0% of the time, Pallas kernels for 17%

profile of v7, /device:TPU:0, one launch (start us, length us, event | category | flops | bytes accessed | tf_op | source)
XLA Modules:
  0.0 31.3 jit_solution(14441456320169847473)
XLA Ops:
  0.6 0.0 copy-start.1
  0.6 3.1 %collective-permute-start = (s32[4,42]{1,0:T(4,128)}, s32[4,42]{1,0:T(4,128)S(1)}, u32[]{:S(2)}, u32[]{:S(2)}) collective-permute-start(s32[4,42]{1,0:T(4,128)} %bitcast.4), channel_id=1, source_target_pairs={{1,0},{0,1},{3,2},{2,3},{5,4},{4,5},{7,6},{6,7},{9,8},{8,9},{11,10... | collective-permute-start | bytes 2024 | tf_op jit(solution)/shard_map/ppermute | solution.py:359
  3.7 2.6 %collective-permute-start.1 = (s32[4,42]{1,0:T(4,128)}, s32[4,42]{1,0:T(4,128)S(1)}, u32[]{:S(2)}, u32[]{:S(2)}) collective-permute-start(s32[4,42]{1,0:T(4,128)} %bitcast.5), channel_id=1, source_target_pairs={{2,0},{3,1},{0,2},{1,3},{6,4},{7,5},{4,6},{5,7},{10,8},{11,9},{8,1... | collective-permute-start | bytes 2024 | tf_op jit(solution)/shard_map/ppermute | solution.py:359
  6.3 0.0 collective-permute-start.2
  6.3 5.2 %integrals.1.refs_4_ = f32[2,2352,128]{2,1,0:T(8,128)S(1)} custom-call(s32[16]{0:T(128)} %centers_x.1, s32[16]{0:T(128)} %centers_y.1, s32[4]{0:T(128)} %centers_t.1, f32[4,2,8,64,128]{4,3,2,1,0:T(8,128)} %fields.1), custom_call_target="tpu_custom_call" | custom-call | flops 10000000000 | bytes 3000000 | tf_op jit(solution)/shard_map/integrals/pallas_call | solution.py:154
  11.6 0.0 copy-start
  11.6 0.0 collective-permute-done.refs_1_
  11.6 0.0 collective-permute-done.1.refs_2_
  11.6 0.3 collective-permute-done.2.refs_3_
  11.9 0.0 copy-done.1
  11.9 1.5 %pick.1.own = f32[1408,128]{1,0:T(8,128)S(1)} custom-call(s32[4,42]{1,0:T(4,128)S(1)} %bitcast.7, s32[4,42]{1,0:T(4,128)S(1)} %collective-permute-done.refs_1_, s32[4,42]{1,0:T(4,128)S(1)} %collective-permute-done.1.refs_2_, s32[4,42]{1,0:T(4,128)S(1)} %collective-permute-done.2.refs_3_, f32[2,2352,128]{2,1,0:T(8,128)S(1)} %integrals.1.refs_4_), custom_call_target="tpu_custom_call" | custom-call | tf_op jit(solution)/shard_map/pick/pallas_call | solution.py:210
  13.4 0.1 collective-permute-start.3
  13.5 2.2 %collective-permute-done.3.other = f32[1408,128]{1,0:T(8,128)S(1)} collective-permute-done((f32[1408,128]{1,0:T(8,128)S(1)}, f32[1408,128]{1,0:T(8,128)S(1)}, u32[]{:S(2)}, u32[]{:S(2)}) %collective-permute-start.3) | collective-permute-done | bytes 720928 | tf_op jit(solution)/shard_map/ppermute | solution.py:359
  15.7 0.0 copy-done
  15.7 1.2 %fit.1 = (f32[24,384]{1,0:T(8,128)S(1)}, f32[176,168]{1,0:T(8,128)S(1)}, f32[48,168]{1,0:T(8,128)S(1)}) custom-call(f32[1408,128]{1,0:T(8,128)S(1)} %pick.1.own, f32[1408,128]{1,0:T(8,128)S(1)} %collective-permute-done.3.other, s32[1,168]{1,0:T(1,128)S(1)} %bitcast.2), custom_call_target="tpu_custom_call" | custom-call | tf_op jit(solution)/shard_map/fit/pallas_call | solution.py:270
  16.9 1.7 %collective-permute-start.4 = (f32[24,384]{1,0:T(8,128)S(1)}, f32[24,384]{1,0:T(8,128)S(1)}, u32[]{:S(2)}, u32[]{:S(2)}) collective-permute-start(f32[24,384]{1,0:T(8,128)S(1)} %get-tuple-element.7), channel_id=1, source_target_pairs={{2,0},{3,1},{0,2},{1,3},{5,4},{4,5},{7,6},{6,7},{10,8},{11,9},{8,1... | collective-permute-start | bytes 110600 | tf_op jit(solution)/shard_map/ppermute | solution.py:372
  18.5 0.7 %collective-permute-start.5 = (f32[24,384]{1,0:T(8,128)S(1)}, f32[24,384]{1,0:T(8,128)S(1)}, u32[]{:S(2)}, u32[]{:S(2)}) collective-permute-start(f32[24,384]{1,0:T(8,128)S(1)} %get-tuple-element.7), channel_id=1, source_target_pairs={{7,4},{6,5},{5,6},{4,7},{15,12},{14,13},{13,14},{12,15},{23,20},{2... | collective-permute-start | bytes 110600 | tf_op jit(solution)/shard_map/ppermute | solution.py:372
  19.2 2.6 %collective-permute-done.4 = f32[24,384]{1,0:T(8,128)S(1)} collective-permute-done((f32[24,384]{1,0:T(8,128)S(1)}, f32[24,384]{1,0:T(8,128)S(1)}, u32[]{:S(2)}, u32[]{:S(2)}) %collective-permute-start.4) | collective-permute-done | bytes 36896 | tf_op jit(solution)/shard_map/ppermute | solution.py:372
  21.8 0.0 collective-permute-done.5
  21.8 1.6 %collective-permute-start.6 = (f32[24,384]{1,0:T(8,128)S(1)}, f32[24,384]{1,0:T(8,128)S(1)}, u32[]{:S(2)}, u32[]{:S(2)}) collective-permute-start(f32[24,384]{1,0:T(8,128)S(1)} %add_select_fusion.1), channel_id=1, source_target_pairs={{16,0},{24,8},{0,16},{8,24},{17,1},{25,9},{1,17},{9,25},{18,2},{26... | collective-permute-start | bytes 110600 | tf_op jit(solution)/shard_map/ppermute | solution.py:359
  23.4 1.4 %collective-permute-start.7 = (f32[24,384]{1,0:T(8,128)S(1)}, f32[24,384]{1,0:T(8,128)S(1)}, u32[]{:S(2)}, u32[]{:S(2)}) collective-permute-start(f32[24,384]{1,0:T(8,128)S(1)} %add_select_fusion.1), channel_id=1, source_target_pairs={{24,0},{16,8},{8,16},{0,24},{25,1},{17,9},{9,17},{1,25},{26,2},{18... | collective-permute-start | bytes 110600 | tf_op jit(solution)/shard_map/ppermute | solution.py:359
  24.8 0.5 %collective-permute-start.8 = (f32[24,384]{1,0:T(8,128)S(1)}, f32[24,384]{1,0:T(8,128)S(1)}, u32[]{:S(2)}, u32[]{:S(2)}) collective-permute-start(f32[24,384]{1,0:T(8,128)S(1)} %add_select_fusion.1), channel_id=1, source_target_pairs={{8,0},{0,8},{24,16},{16,24},{9,1},{1,9},{25,17},{17,25},{10,2},{2,... | collective-permute-start | bytes 110600 | tf_op jit(solution)/shard_map/ppermute | solution.py:359
  25.4 0.5 %collective-permute-done.6 = f32[24,384]{1,0:T(8,128)S(1)} collective-permute-done((f32[24,384]{1,0:T(8,128)S(1)}, f32[24,384]{1,0:T(8,128)S(1)}, u32[]{:S(2)}, u32[]{:S(2)}) %collective-permute-start.6) | collective-permute-done | bytes 36896 | tf_op jit(solution)/shard_map/ppermute | solution.py:359
  25.8 2.4 %collective-permute-done.7 = f32[24,384]{1,0:T(8,128)S(1)} collective-permute-done((f32[24,384]{1,0:T(8,128)S(1)}, f32[24,384]{1,0:T(8,128)S(1)}, u32[]{:S(2)}, u32[]{:S(2)}) %collective-permute-start.7) | collective-permute-done | bytes 36896 | tf_op jit(solution)/shard_map/ppermute | solution.py:359
  28.2 0.5 %collective-permute-done.8 = f32[24,384]{1,0:T(8,128)S(1)} collective-permute-done((f32[24,384]{1,0:T(8,128)S(1)}, f32[24,384]{1,0:T(8,128)S(1)}, u32[]{:S(2)}, u32[]{:S(2)}) %collective-permute-start.8) | collective-permute-done | bytes 36896 | tf_op jit(solution)/shard_map/ppermute | solution.py:359
  28.8 0.6 %collective-permute-start.9 = (f32[24,384]{1,0:T(8,128)S(1)}, f32[24,384]{1,0:T(8,128)S(1)}, u32[]{:S(2)}, u32[]{:S(2)}) collective-permute-start(f32[24,384]{1,0:T(8,128)S(1)} %add_select_fusion.refs_0_), channel_id=1, source_target_pairs={{4,0},{0,4},{5,1},{1,5},{6,2},{2,6},{7,3},{3,7},{12,8},{8,12},{13,... | collective-permute-start | bytes 110600 | tf_op jit(solution)/shard_map/ppermute | solution.py:359
  29.3 0.9 %collective-permute-done.9.refs_1_ = f32[24,384]{1,0:T(8,128)S(1)} collective-permute-done((f32[24,384]{1,0:T(8,128)S(1)}, f32[24,384]{1,0:T(8,128)S(1)}, u32[]{:S(2)}, u32[]{:S(2)}) %collective-permute-start.9) | collective-permute-done | bytes 36896 | tf_op jit(solution)/shard_map/ppermute | solution.py:359
  30.2 1.1 %finish.1 = (f32[1,2,168]{2,1,0:T(2,128)}, f32[1,2,168]{2,1,0:T(2,128)}) custom-call(s32[1,168]{1,0:T(1,128)S(1)} %bitcast.3, f32[176,168]{1,0:T(8,128)S(1)} %get-tuple-element.5.normal, f32[48,168]{1,0:T(8,128)S(1)} %get-tuple-element.6.dmat, f32[24,384]{1,0:T(8,128)S(1)} %add_select_fusion.refs_0_, f32[24,384]{1,0:T(8,128)S(1)} %collective-permute-done.9.refs_1_), custom_call_target="tpu_custom_call" | custom-call | tf_op jit(solution)/shard_map/finish/pallas_call | solution.py:339
  (3 shorter events, 0.0 us)
Async XLA Ops:
  0.6 11.3 %copy-start.1 = (s32[42,4]{0,1:T(4,128)S(1)}, s32[42,4]{0,1:T(4,128)}, u32[]{:S(2)}) copy-start(s32[42,4]{0,1:T(4,128)} %param.7) | copy-start | bytes 2020
  0.6 10.9 %collective-permute-start = (s32[4,42]{1,0:T(4,128)}, s32[4,42]{1,0:T(4,128)S(1)}, u32[]{:S(2)}, u32[]{:S(2)}) collective-permute-start(s32[4,42]{1,0:T(4,128)} %bitcast.4), channel_id=1, source_target_pairs={{1,0},{0,1},{3,2},{2,3},{5,4},{4,5},{7,6},{6,7},{9,8},{8,9},{11,10... | collective-permute-start | bytes 2024 | tf_op jit(solution)/shard_map/ppermute | solution.py:359
  3.7 7.9 %collective-permute-start.1 = (s32[4,42]{1,0:T(4,128)}, s32[4,42]{1,0:T(4,128)S(1)}, u32[]{:S(2)}, u32[]{:S(2)}) collective-permute-start(s32[4,42]{1,0:T(4,128)} %bitcast.5), channel_id=1, source_target_pairs={{2,0},{3,1},{0,2},{1,3},{6,4},{7,5},{4,6},{5,7},{10,8},{11,9},{8,1... | collective-permute-start | bytes 2024 | tf_op jit(solution)/shard_map/ppermute | solution.py:359
  6.3 5.6 %collective-permute-start.2 = (s32[4,42]{1,0:T(4,128)}, s32[4,42]{1,0:T(4,128)S(1)}, u32[]{:S(2)}, u32[]{:S(2)}) collective-permute-start(s32[4,42]{1,0:T(4,128)} %bitcast.6), channel_id=1, source_target_pairs={{3,0},{2,1},{1,2},{0,3},{7,4},{6,5},{5,6},{4,7},{11,8},{10,9},{9,1... | collective-permute-start | bytes 2024 | tf_op jit(solution)/shard_map/ppermute | solution.py:359
  11.6 4.1 %copy-start = (s32[168]{0:T(256)S(1)}, s32[168]{0:T(256)}, u32[]{:S(2)}) copy-start(s32[168]{0:T(256)} %param.11) | copy-start | bytes 2020
  13.4 2.3 %collective-permute-start.3 = (f32[1408,128]{1,0:T(8,128)S(1)}, f32[1408,128]{1,0:T(8,128)S(1)}, u32[]{:S(2)}, u32[]{:S(2)}) collective-permute-start(f32[1408,128]{1,0:T(8,128)S(1)} %pick.1.own), channel_id=1, source_target_pairs={{4,0},{0,4},{5,1},{1,5},{6,2},{2,6},{7,3},{3,7},{12,8},{8,12},{13,... | collective-permute-start | bytes 2162696 | tf_op jit(solution)/shard_map/ppermute | solution.py:359
  16.9 4.9 %collective-permute-start.4 = (f32[24,384]{1,0:T(8,128)S(1)}, f32[24,384]{1,0:T(8,128)S(1)}, u32[]{:S(2)}, u32[]{:S(2)}) collective-permute-start(f32[24,384]{1,0:T(8,128)S(1)} %get-tuple-element.7), channel_id=1, source_target_pairs={{2,0},{3,1},{0,2},{1,3},{5,4},{4,5},{7,6},{6,7},{10,8},{11,9},{8,1... | collective-permute-start | bytes 110600 | tf_op jit(solution)/shard_map/ppermute | solution.py:372
  18.5 3.2 %collective-permute-start.5 = (f32[24,384]{1,0:T(8,128)S(1)}, f32[24,384]{1,0:T(8,128)S(1)}, u32[]{:S(2)}, u32[]{:S(2)}) collective-permute-start(f32[24,384]{1,0:T(8,128)S(1)} %get-tuple-element.7), channel_id=1, source_target_pairs={{7,4},{6,5},{5,6},{4,7},{15,12},{14,13},{13,14},{12,15},{23,20},{2... | collective-permute-start | bytes 110600 | tf_op jit(solution)/shard_map/ppermute | solution.py:372
  21.8 4.0 %collective-permute-start.6 = (f32[24,384]{1,0:T(8,128)S(1)}, f32[24,384]{1,0:T(8,128)S(1)}, u32[]{:S(2)}, u32[]{:S(2)}) collective-permute-start(f32[24,384]{1,0:T(8,128)S(1)} %add_select_fusion.1), channel_id=1, source_target_pairs={{16,0},{24,8},{0,16},{8,24},{17,1},{25,9},{1,17},{9,25},{18,2},{26... | collective-permute-start | bytes 110600 | tf_op jit(solution)/shard_map/ppermute | solution.py:359
  23.4 4.9 %collective-permute-start.7 = (f32[24,384]{1,0:T(8,128)S(1)}, f32[24,384]{1,0:T(8,128)S(1)}, u32[]{:S(2)}, u32[]{:S(2)}) collective-permute-start(f32[24,384]{1,0:T(8,128)S(1)} %add_select_fusion.1), channel_id=1, source_target_pairs={{24,0},{16,8},{8,16},{0,24},{25,1},{17,9},{9,17},{1,25},{26,2},{18... | collective-permute-start | bytes 110600 | tf_op jit(solution)/shard_map/ppermute | solution.py:359
  24.8 4.0 %collective-permute-start.8 = (f32[24,384]{1,0:T(8,128)S(1)}, f32[24,384]{1,0:T(8,128)S(1)}, u32[]{:S(2)}, u32[]{:S(2)}) collective-permute-start(f32[24,384]{1,0:T(8,128)S(1)} %add_select_fusion.1), channel_id=1, source_target_pairs={{8,0},{0,8},{24,16},{16,24},{9,1},{1,9},{25,17},{17,25},{10,2},{2,... | collective-permute-start | bytes 110600 | tf_op jit(solution)/shard_map/ppermute | solution.py:359
  28.8 1.4 %collective-permute-start.9 = (f32[24,384]{1,0:T(8,128)S(1)}, f32[24,384]{1,0:T(8,128)S(1)}, u32[]{:S(2)}, u32[]{:S(2)}) collective-permute-start(f32[24,384]{1,0:T(8,128)S(1)} %add_select_fusion.refs_0_), channel_id=1, source_target_pairs={{4,0},{0,4},{5,1},{1,5},{6,2},{2,6},{7,3},{3,7},{12,8},{8,12},{13,... | collective-permute-start | bytes 110600 | tf_op jit(solution)/shard_map/ppermute | solution.py:359

commit v8 on v7

--- a/solution.py
+++ b/solution.py
@@ -244,11 +244,13 @@
     normal[...] = norm[:, :TERMS]
     gi = lax.broadcasted_iota(jnp.int32, (GROUPS, TERMS), 0)
     onehot = gi == grp[...]
+    spread = [jnp.where(onehot, norm[TERMS + s : TERMS + s + 1, :TERMS], 0.0) for s in range(2)]
+    grouped = dot3(jnp.concatenate(spread, axis=0), corr, NN_DIMS)
+    dmat[...] = grouped
     products = [0.0] * (HALF + 2)
     for s in range(2):
         right = norm[TERMS + s : TERMS + s + 1, :TERMS]
-        d = dot3(jnp.where(onehot, right, 0.0), corr, NN_DIMS)
-        dmat[pl.ds(s * GROUPS, GROUPS), :] = d
+        d = grouped[s * GROUPS : (s + 1) * GROUPS]
         products[0] = products[0] + d * d
         for shift in range(1, HALF):
             products[shift] = products[shift] + d * jnp.concatenate([d[shift:], d[:shift]], axis=0)

time: 31.5 us -> 31.4 us (level)
  no operation moved by 1% of the time
where the time goes in v8:
time: 31.4 us; the launch traced here: 31.2 us
  starting transfers between devices  12.2 us (39%)
  waiting for transfers between devices  9.34 us (30%)
  Pallas kernels  8.94 us (28%)
  between operations  0.72 us (2%)
    ppermute x8, starting transfers between devices, exchange(): lax.ppermute(value, axis, [(partner(i, k, size), i) for i in range(size)])  9.86 us
    ppermute x8, waiting for transfers between devices, exchange(): lax.ppermute(value, axis, [(partner(i, k, size), i) for i in range(size)])  6.78 us
    pallas_call x1, Pallas kernels, integrals(): pl.pallas_call(functools.partial(integrals_kernel, rows), out_shape=jax.S...  5.24 us
    ppermute x2, waiting for transfers between devices, shared_exchange(): rounds.append(lax.ppermute(value, ('space', axis), pairs))  2.56 us
    ppermute x2, starting transfers between devices, shared_exchange(): rounds.append(lax.ppermute(value, ('space', axis), pairs))  2.34 us
    pallas_call x1, Pallas kernels, pick(): pl.pallas_call(functools.partial(pick_kernel, libs[0].shape[1]), out_shap...  1.49 us
    pallas_call x1, Pallas kernels, fit(): pl.pallas_call(fit_kernel, out_shape=(jax.ShapeDtypeStruct((GROUPS, WIDTH...  1.11 us
    pallas_call x1, Pallas kernels, end(): pl.pallas_call(functools.partial(end_kernel, len(pieces)), out_shape=(sha...  1.09 us
  transfers between devices with their start and end apart: 10, of which 7 were waited for; matrix products, arithmetic and copies ran while one was open for 0% of the time, Pallas kernels for 17%

profile of v8, /device:TPU:0, one launch (start us, length us, event | category | flops | bytes accessed | tf_op | source)
XLA Modules:
  0.0 31.2 jit_solution(1571921593964351550)
XLA Ops:
  0.6 0.0 copy-start.1
  0.6 3.1 %collective-permute-start = (s32[4,42]{1,0:T(4,128)}, s32[4,42]{1,0:T(4,128)S(1)}, u32[]{:S(2)}, u32[]{:S(2)}) collective-permute-start(s32[4,42]{1,0:T(4,128)} %bitcast.4), channel_id=1, source_target_pairs={{1,0},{0,1},{3,2},{2,3},{5,4},{4,5},{7,6},{6,7},{9,8},{8,9},{11,10... | collective-permute-start | bytes 2024 | tf_op jit(solution)/shard_map/ppermute | solution.py:361
  3.7 2.6 %collective-permute-start.1 = (s32[4,42]{1,0:T(4,128)}, s32[4,42]{1,0:T(4,128)S(1)}, u32[]{:S(2)}, u32[]{:S(2)}) collective-permute-start(s32[4,42]{1,0:T(4,128)} %bitcast.5), channel_id=1, source_target_pairs={{2,0},{3,1},{0,2},{1,3},{6,4},{7,5},{4,6},{5,7},{10,8},{11,9},{8,1... | collective-permute-start | bytes 2024 | tf_op jit(solution)/shard_map/ppermute | solution.py:361
  6.3 0.0 collective-permute-start.2
  6.3 5.2 %integrals.1.refs_4_ = f32[2,2352,128]{2,1,0:T(8,128)S(1)} custom-call(s32[16]{0:T(128)} %centers_x.1, s32[16]{0:T(128)} %centers_y.1, s32[4]{0:T(128)} %centers_t.1, f32[4,2,8,64,128]{4,3,2,1,0:T(8,128)} %fields.1), custom_call_target="tpu_custom_call" | custom-call | flops 10000000000 | bytes 3000000 | tf_op jit(solution)/shard_map/integrals/pallas_call | solution.py:154
  11.6 0.0 copy-start
  11.6 0.0 collective-permute-done.refs_1_
  11.6 0.0 collective-permute-done.1.refs_2_
  11.6 0.3 collective-permute-done.2.refs_3_
  11.9 0.0 copy-done.1
  11.9 1.5 %pick.1.own = f32[1408,128]{1,0:T(8,128)S(1)} custom-call(s32[4,42]{1,0:T(4,128)S(1)} %bitcast.7, s32[4,42]{1,0:T(4,128)S(1)} %collective-permute-done.refs_1_, s32[4,42]{1,0:T(4,128)S(1)} %collective-permute-done.1.refs_2_, s32[4,42]{1,0:T(4,128)S(1)} %collective-permute-done.2.refs_3_, f32[2,2352,128]{2,1,0:T(8,128)S(1)} %integrals.1.refs_4_), custom_call_target="tpu_custom_call" | custom-call | tf_op jit(solution)/shard_map/pick/pallas_call | solution.py:210
  13.4 0.1 collective-permute-start.3
  13.5 2.2 %collective-permute-done.3.other = f32[1408,128]{1,0:T(8,128)S(1)} collective-permute-done((f32[1408,128]{1,0:T(8,128)S(1)}, f32[1408,128]{1,0:T(8,128)S(1)}, u32[]{:S(2)}, u32[]{:S(2)}) %collective-permute-start.3) | collective-permute-done | bytes 720928 | tf_op jit(solution)/shard_map/ppermute | solution.py:361
  15.7 0.0 copy-done
  15.7 1.1 %fit.1 = (f32[24,384]{1,0:T(8,128)S(1)}, f32[176,168]{1,0:T(8,128)S(1)}, f32[48,168]{1,0:T(8,128)S(1)}) custom-call(f32[1408,128]{1,0:T(8,128)S(1)} %pick.1.own, f32[1408,128]{1,0:T(8,128)S(1)} %collective-permute-done.3.other, s32[1,168]{1,0:T(1,128)S(1)} %bitcast.2), custom_call_target="tpu_custom_call" | custom-call | tf_op jit(solution)/shard_map/fit/pallas_call | solution.py:272
  16.8 1.7 %collective-permute-start.4 = (f32[24,384]{1,0:T(8,128)S(1)}, f32[24,384]{1,0:T(8,128)S(1)}, u32[]{:S(2)}, u32[]{:S(2)}) collective-permute-start(f32[24,384]{1,0:T(8,128)S(1)} %get-tuple-element.7), channel_id=1, source_target_pairs={{2,0},{3,1},{0,2},{1,3},{5,4},{4,5},{7,6},{6,7},{10,8},{11,9},{8,1... | collective-permute-start | bytes 110600 | tf_op jit(solution)/shard_map/ppermute | solution.py:374
  18.5 0.7 %collective-permute-start.5 = (f32[24,384]{1,0:T(8,128)S(1)}, f32[24,384]{1,0:T(8,128)S(1)}, u32[]{:S(2)}, u32[]{:S(2)}) collective-permute-start(f32[24,384]{1,0:T(8,128)S(1)} %get-tuple-element.7), channel_id=1, source_target_pairs={{7,4},{6,5},{5,6},{4,7},{15,12},{14,13},{13,14},{12,15},{23,20},{2... | collective-permute-start | bytes 110600 | tf_op jit(solution)/shard_map/ppermute | solution.py:374
  19.1 2.6 %collective-permute-done.4 = f32[24,384]{1,0:T(8,128)S(1)} collective-permute-done((f32[24,384]{1,0:T(8,128)S(1)}, f32[24,384]{1,0:T(8,128)S(1)}, u32[]{:S(2)}, u32[]{:S(2)}) %collective-permute-start.4) | collective-permute-done | bytes 36896 | tf_op jit(solution)/shard_map/ppermute | solution.py:374
  21.7 0.0 collective-permute-done.5
  21.7 1.6 %collective-permute-start.6 = (f32[24,384]{1,0:T(8,128)S(1)}, f32[24,384]{1,0:T(8,128)S(1)}, u32[]{:S(2)}, u32[]{:S(2)}) collective-permute-start(f32[24,384]{1,0:T(8,128)S(1)} %add_select_fusion.1), channel_id=1, source_target_pairs={{16,0},{24,8},{0,16},{8,24},{17,1},{25,9},{1,17},{9,25},{18,2},{26... | collective-permute-start | bytes 110600 | tf_op jit(solution)/shard_map/ppermute | solution.py:361
  23.3 1.4 %collective-permute-start.7 = (f32[24,384]{1,0:T(8,128)S(1)}, f32[24,384]{1,0:T(8,128)S(1)}, u32[]{:S(2)}, u32[]{:S(2)}) collective-permute-start(f32[24,384]{1,0:T(8,128)S(1)} %add_select_fusion.1), channel_id=1, source_target_pairs={{24,0},{16,8},{8,16},{0,24},{25,1},{17,9},{9,17},{1,25},{26,2},{18... | collective-permute-start | bytes 110600 | tf_op jit(solution)/shard_map/ppermute | solution.py:361
  24.7 0.5 %collective-permute-start.8 = (f32[24,384]{1,0:T(8,128)S(1)}, f32[24,384]{1,0:T(8,128)S(1)}, u32[]{:S(2)}, u32[]{:S(2)}) collective-permute-start(f32[24,384]{1,0:T(8,128)S(1)} %add_select_fusion.1), channel_id=1, source_target_pairs={{8,0},{0,8},{24,16},{16,24},{9,1},{1,9},{25,17},{17,25},{10,2},{2,... | collective-permute-start | bytes 110600 | tf_op jit(solution)/shard_map/ppermute | solution.py:361
  25.3 0.5 %collective-permute-done.6 = f32[24,384]{1,0:T(8,128)S(1)} collective-permute-done((f32[24,384]{1,0:T(8,128)S(1)}, f32[24,384]{1,0:T(8,128)S(1)}, u32[]{:S(2)}, u32[]{:S(2)}) %collective-permute-start.6) | collective-permute-done | bytes 36896 | tf_op jit(solution)/shard_map/ppermute | solution.py:361
  25.7 2.4 %collective-permute-done.7 = f32[24,384]{1,0:T(8,128)S(1)} collective-permute-done((f32[24,384]{1,0:T(8,128)S(1)}, f32[24,384]{1,0:T(8,128)S(1)}, u32[]{:S(2)}, u32[]{:S(2)}) %collective-permute-start.7) | collective-permute-done | bytes 36896 | tf_op jit(solution)/shard_map/ppermute | solution.py:361
  28.2 0.5 %collective-permute-done.8 = f32[24,384]{1,0:T(8,128)S(1)} collective-permute-done((f32[24,384]{1,0:T(8,128)S(1)}, f32[24,384]{1,0:T(8,128)S(1)}, u32[]{:S(2)}, u32[]{:S(2)}) %collective-permute-start.8) | collective-permute-done | bytes 36896 | tf_op jit(solution)/shard_map/ppermute | solution.py:361
  28.7 0.6 %collective-permute-start.9 = (f32[24,384]{1,0:T(8,128)S(1)}, f32[24,384]{1,0:T(8,128)S(1)}, u32[]{:S(2)}, u32[]{:S(2)}) collective-permute-start(f32[24,384]{1,0:T(8,128)S(1)} %add_select_fusion.refs_0_), channel_id=1, source_target_pairs={{4,0},{0,4},{5,1},{1,5},{6,2},{2,6},{7,3},{3,7},{12,8},{8,12},{13,... | collective-permute-start | bytes 110600 | tf_op jit(solution)/shard_map/ppermute | solution.py:361
  29.3 0.9 %collective-permute-done.9.refs_1_ = f32[24,384]{1,0:T(8,128)S(1)} collective-permute-done((f32[24,384]{1,0:T(8,128)S(1)}, f32[24,384]{1,0:T(8,128)S(1)}, u32[]{:S(2)}, u32[]{:S(2)}) %collective-permute-start.9) | collective-permute-done | bytes 36896 | tf_op jit(solution)/shard_map/ppermute | solution.py:361
  30.1 1.1 %finish.1 = (f32[1,2,168]{2,1,0:T(2,128)}, f32[1,2,168]{2,1,0:T(2,128)}) custom-call(s32[1,168]{1,0:T(1,128)S(1)} %bitcast.3, f32[176,168]{1,0:T(8,128)S(1)} %get-tuple-element.5.normal, f32[48,168]{1,0:T(8,128)S(1)} %get-tuple-element.6.dmat, f32[24,384]{1,0:T(8,128)S(1)} %add_select_fusion.refs_0_, f32[24,384]{1,0:T(8,128)S(1)} %collective-permute-done.9.refs_1_), custom_call_target="tpu_custom_call" | custom-call | tf_op jit(solution)/shard_map/finish/pallas_call | solution.py:341
  (3 shorter events, 0.0 us)
Async XLA Ops:
  0.6 11.3 %copy-start.1 = (s32[42,4]{0,1:T(4,128)S(1)}, s32[42,4]{0,1:T(4,128)}, u32[]{:S(2)}) copy-start(s32[42,4]{0,1:T(4,128)} %param.7) | copy-start | bytes 2020
  0.6 10.9 %collective-permute-start = (s32[4,42]{1,0:T(4,128)}, s32[4,42]{1,0:T(4,128)S(1)}, u32[]{:S(2)}, u32[]{:S(2)}) collective-permute-start(s32[4,42]{1,0:T(4,128)} %bitcast.4), channel_id=1, source_target_pairs={{1,0},{0,1},{3,2},{2,3},{5,4},{4,5},{7,6},{6,7},{9,8},{8,9},{11,10... | collective-permute-start | bytes 2024 | tf_op jit(solution)/shard_map/ppermute | solution.py:361
  3.7 7.9 %collective-permute-start.1 = (s32[4,42]{1,0:T(4,128)}, s32[4,42]{1,0:T(4,128)S(1)}, u32[]{:S(2)}, u32[]{:S(2)}) collective-permute-start(s32[4,42]{1,0:T(4,128)} %bitcast.5), channel_id=1, source_target_pairs={{2,0},{3,1},{0,2},{1,3},{6,4},{7,5},{4,6},{5,7},{10,8},{11,9},{8,1... | collective-permute-start | bytes 2024 | tf_op jit(solution)/shard_map/ppermute | solution.py:361
  6.3 5.6 %collective-permute-start.2 = (s32[4,42]{1,0:T(4,128)}, s32[4,42]{1,0:T(4,128)S(1)}, u32[]{:S(2)}, u32[]{:S(2)}) collective-permute-start(s32[4,42]{1,0:T(4,128)} %bitcast.6), channel_id=1, source_target_pairs={{3,0},{2,1},{1,2},{0,3},{7,4},{6,5},{5,6},{4,7},{11,8},{10,9},{9,1... | collective-permute-start | bytes 2024 | tf_op jit(solution)/shard_map/ppermute | solution.py:361
  11.6 4.1 %copy-start = (s32[168]{0:T(256)S(1)}, s32[168]{0:T(256)}, u32[]{:S(2)}) copy-start(s32[168]{0:T(256)} %param.11) | copy-start | bytes 2020
  13.4 2.3 %collective-permute-start.3 = (f32[1408,128]{1,0:T(8,128)S(1)}, f32[1408,128]{1,0:T(8,128)S(1)}, u32[]{:S(2)}, u32[]{:S(2)}) collective-permute-start(f32[1408,128]{1,0:T(8,128)S(1)} %pick.1.own), channel_id=1, source_target_pairs={{4,0},{0,4},{5,1},{1,5},{6,2},{2,6},{7,3},{3,7},{12,8},{8,12},{13,... | collective-permute-start | bytes 2162696 | tf_op jit(solution)/shard_map/ppermute | solution.py:361
  16.8 4.9 %collective-permute-start.4 = (f32[24,384]{1,0:T(8,128)S(1)}, f32[24,384]{1,0:T(8,128)S(1)}, u32[]{:S(2)}, u32[]{:S(2)}) collective-permute-start(f32[24,384]{1,0:T(8,128)S(1)} %get-tuple-element.7), channel_id=1, source_target_pairs={{2,0},{3,1},{0,2},{1,3},{5,4},{4,5},{7,6},{6,7},{10,8},{11,9},{8,1... | collective-permute-start | bytes 110600 | tf_op jit(solution)/shard_map/ppermute | solution.py:374
  18.5 3.2 %collective-permute-start.5 = (f32[24,384]{1,0:T(8,128)S(1)}, f32[24,384]{1,0:T(8,128)S(1)}, u32[]{:S(2)}, u32[]{:S(2)}) collective-permute-start(f32[24,384]{1,0:T(8,128)S(1)} %get-tuple-element.7), channel_id=1, source_target_pairs={{7,4},{6,5},{5,6},{4,7},{15,12},{14,13},{13,14},{12,15},{23,20},{2... | collective-permute-start | bytes 110600 | tf_op jit(solution)/shard_map/ppermute | solution.py:374
  21.7 4.0 %collective-permute-start.6 = (f32[24,384]{1,0:T(8,128)S(1)}, f32[24,384]{1,0:T(8,128)S(1)}, u32[]{:S(2)}, u32[]{:S(2)}) collective-permute-start(f32[24,384]{1,0:T(8,128)S(1)} %add_select_fusion.1), channel_id=1, source_target_pairs={{16,0},{24,8},{0,16},{8,24},{17,1},{25,9},{1,17},{9,25},{18,2},{26... | collective-permute-start | bytes 110600 | tf_op jit(solution)/shard_map/ppermute | solution.py:361
  23.3 4.9 %collective-permute-start.7 = (f32[24,384]{1,0:T(8,128)S(1)}, f32[24,384]{1,0:T(8,128)S(1)}, u32[]{:S(2)}, u32[]{:S(2)}) collective-permute-start(f32[24,384]{1,0:T(8,128)S(1)} %add_select_fusion.1), channel_id=1, source_target_pairs={{24,0},{16,8},{8,16},{0,24},{25,1},{17,9},{9,17},{1,25},{26,2},{18... | collective-permute-start | bytes 110600 | tf_op jit(solution)/shard_map/ppermute | solution.py:361
  24.7 4.0 %collective-permute-start.8 = (f32[24,384]{1,0:T(8,128)S(1)}, f32[24,384]{1,0:T(8,128)S(1)}, u32[]{:S(2)}, u32[]{:S(2)}) collective-permute-start(f32[24,384]{1,0:T(8,128)S(1)} %add_select_fusion.1), channel_id=1, source_target_pairs={{8,0},{0,8},{24,16},{16,24},{9,1},{1,9},{25,17},{17,25},{10,2},{2,... | collective-permute-start | bytes 110600 | tf_op jit(solution)/shard_map/ppermute | solution.py:361
  28.7 1.4 %collective-permute-start.9 = (f32[24,384]{1,0:T(8,128)S(1)}, f32[24,384]{1,0:T(8,128)S(1)}, u32[]{:S(2)}, u32[]{:S(2)}) collective-permute-start(f32[24,384]{1,0:T(8,128)S(1)} %add_select_fusion.refs_0_), channel_id=1, source_target_pairs={{4,0},{0,4},{5,1},{1,5},{6,2},{2,6},{7,3},{3,7},{12,8},{8,12},{13,... | collective-permute-start | bytes 110600 | tf_op jit(solution)/shard_map/ppermute | solution.py:361
